TPU v7x, 256 devices: a whole 4x4x8 slice. The times are simulated.
256 devices in a mesh: sta: 32 (over z, y_lo, core), hr: 8 (over x, y_hi).
Axes of the slice: x: 4, y: 4 (y_hi: 2, y_lo: 2; y = y_hi * 2 + y_lo), z: 8, core: 2. Of those that a mesh axis runs over, the one named last changes fastest.
Arguments:
- spectra: bfloat16 [2048, 48, 2, 2048], P('sta', 'hr'), may hold values from -640 to 640, as said below
- pair_list: int32 [32, 2, 128], P('sta'), may hold values from 0 to 191, as said below
- pair_count: int32 [32], P('sta'), may hold values from 16 to 128, as said below
Outputs:
- correlation: float32 [4096, 2432], P(('sta', 'hr'))
Inputs may be any that keep to these rules, and one draw needn't show every extreme that they name: `spectra`: raw spectral values. `pair_list`: entries of used slots: the first lies below 64, the second differs from the first; slots at or past the block's count hold 0. In a block that uses all 128 slots, the second entries name every one of 64 .. 191. `pair_count`: some block uses all 128 slots.
All inputs are finite; a program needn't handle non-finite values.
Results may differ from a plain program's by a relative error of at most 0.0041.
Values may be sent and summed in bfloat16 or wider, within the bound.
No kernel may reach another device: no remote copies, remote signals or barrier semaphores. Data moves between devices by JAX's collectives and lax.ppermute only.
A program may use at most 192 MiB of HBM per device.

v0:
```python
import math

import jax
import jax.numpy as jnp
from jax import lax
from jax.sharding import PartitionSpec as P

F = 2048
BAND = 128
HALF = 1216
SAMPLES = 36000
K0 = 90
LAGS = 2432


def from_behind(value, axis, steps):
    count = lax.axis_size(axis)
    pairs = [(source, (source + steps) % count) for source in range(count)]
    return lax.ppermute(value, axis, pairs)


def whiten(spectra):
    stations, segments, halves, freq_bins = spectra.shape
    grouped = spectra.astype(jnp.float32).reshape(
        stations, segments, halves, freq_bins // BAND, BAND
    )
    band_power = jnp.sum(grouped * grouped, axis=(2, 4), keepdims=True) / BAND
    return (grouped * lax.rsqrt(band_power + 1e-06)).reshape(spectra.shape).astype(jnp.bfloat16)


def lag_table():
    freq_index = K0 + jnp.arange(F, dtype=jnp.int32)
    lag_index = jnp.arange(LAGS, dtype=jnp.int32) - HALF
    phase_turns = jnp.remainder(freq_index[:, None] * lag_index[None, :], SAMPLES)
    angles = phase_turns.astype(jnp.float32) * (2.0 * math.pi / SAMPLES)
    return jnp.concatenate([jnp.cos(angles), -jnp.sin(angles)], axis=0)


def cross_tile(buffer, first_index, second_index, live_rows):
    left_spec = jnp.take(buffer, first_index, axis=0)
    right_spec = jnp.take(buffer, second_index, axis=0)
    left_re = left_spec[:, :, 0].astype(jnp.float32)
    left_im = left_spec[:, :, 1].astype(jnp.float32)
    right_re = right_spec[:, :, 0].astype(jnp.float32)
    right_im = right_spec[:, :, 1].astype(jnp.float32)
    cross_re = jnp.sum(left_re * right_re + left_im * right_im, axis=1)
    cross_im = jnp.sum(left_im * right_re - left_re * right_im, axis=1)
    return jnp.concatenate([cross_re, cross_im], axis=-1) * live_rows[:, None]


def on_device(spectra, pair_list, pair_count):
    whitened = whiten(spectra)
    first_round = from_behind(whitened, "sta", 1)
    second_round = from_behind(whitened, "sta", 2)
    buffer = jnp.concatenate([whitened, first_round, second_round], axis=0)
    live_count = pair_count[0]
    capacity = pair_list.shape[2]
    row_index = jnp.arange(capacity, dtype=jnp.int32)
    live_rows = (row_index < live_count).astype(jnp.float32)
    first_index = pair_list[0, 0]
    second_index = pair_list[0, 1]
    cross = cross_tile(buffer, first_index, second_index, live_rows)
    phase_table = lag_table()
    norm_scale = 1.0 / math.sqrt(spectra.shape[1] * lax.axis_size("hr") * F)
    owned_share = lax.psum_scatter(cross, "hr", scatter_dimension=0, tiled=True)
    return (
        jnp.dot(
            owned_share,
            phase_table,
            precision=lax.Precision.HIGHEST,
            preferred_element_type=jnp.float32,
        )
        * norm_scale
    )


def solution(mesh):
    in_specs = (P("sta", "hr", None, None), P("sta", None, None), P("sta"))
    out_specs = P(("sta", "hr"), None)
    return jax.shard_map(
        on_device, mesh=mesh, in_specs=in_specs, out_specs=out_specs, check_vma=False
    )
```

profile of v0, /device:TPU:2, one launch (start us, length us, event | category | flops | bytes accessed | tf_op | source)
XLA Modules:
  0.0 364.8 jit_solution(18285242706540904176)
XLA Ops:
  6.5 12.2 %fusion.10 = f32[64,6,2048]{2,1,0:T(8,128)} fusion(bf16[64,6,2,2048]{3,2,1,0:T(2,128)(2,1)} %param.5), kind=kLoop, calls=%fused_computation.22 | loop fusion | flops 3932160 | bytes 6291456 | tf_op jit(solution)/shard_map/reduce_sum | solution.py:27
  18.7 3.6 %reshape.62 = f32[64,6,16,128]{3,2,1,0:T(8,128)S(1)} reshape(f32[64,6,2048]{2,1,0:T(8,128)} %fusion.10) | data formatting | bytes 6291456 | tf_op jit(solution)/shard_map/reduce_sum | solution.py:27
  22.4 0.9 reduce_sum.36
  23.3 0.1 copy.15
  23.4 0.1 copy.16
  23.5 2.2 mul.75
  25.7 2.8 mul.76
  28.5 0.0 copy-start
  28.5 1.9 copy.17
  30.5 0.0 copy-start.1
  30.5 3.6 fusion.11
  34.0 1.7 collective-permute-start.1
  35.7 0.0 collective-permute-start
  36.4 73.5 %collective-permute-done.1 = bf16[64,6,2,2048]{3,2,1,0:T(2,128)(2,1)S(1)} collective-permute-done((bf16[64,6,2,2048]{3,2,1,0:T(2,128)(2,1)S(1)}, bf16[64,6,2,2048]{3,2,1,0:T(2,128)(2,1)S(1)}, u32[]{:S(2)}, u32[]{:S(2)}) %collective-permute-start.1) | collective-permute-done | bytes 3145760 | tf_op jit(solution)/shard_map/ppermute | solution.py:19
  109.9 32.9 %collective-permute-done = bf16[64,6,2,2048]{3,2,1,0:T(2,128)(2,1)S(1)} collective-permute-done((bf16[64,6,2,2048]{3,2,1,0:T(2,128)(2,1)S(1)}, bf16[64,6,2,2048]{3,2,1,0:T(2,128)(2,1)S(1)}, u32[]{:S(2)}, u32[]{:S(2)}) %collective-permute-start) | collective-permute-done | bytes 3145760 | tf_op jit(solution)/shard_map/ppermute | solution.py:19
  142.8 35.3 %pad_maximum_fusion = bf16[192,6,2,2048]{3,2,1,0:T(2,128)(2,1)} fusion(bf16[64,6,2,2048]{3,2,1,0:T(2,128)(2,1)S(1)} %collective-permute-done.1, bf16[64,6,2,2048]{3,2,1,0:T(2,128)(2,1)S(1)} %collective-permute-done, bf16[64,6,2,2048]{3,2,1,0:T(2,128)(2,1)S(1)} %fusion.11), kind=kLoop, calls=%fused_computation.15 | loop fusion | flops 9437184 | bytes 18874368 | tf_op jit(solution)/shard_map/concatenate | solution.py:55
  178.1 19.5 %gather_fusion.1 = bf16[128,6,2,2048]{3,2,1,0:T(2,128)(2,1)} fusion(bf16[192,6,2,2048]{3,2,1,0:T(2,128)(2,1)} %pad_maximum_fusion, s32[1024]{0:T(1024)S(1)} %pad_clamp_fusion), kind=kCustom, calls=%fused_computation.1.clone | custom fusion | bytes 12583424 | tf_op jit(solution)/shard_map/jit(_take)/gather | solution.py:41
  197.7 19.6 %gather_fusion = bf16[128,6,2,2048]{3,2,1,0:T(2,128)(2,1)} fusion(bf16[192,6,2,2048]{3,2,1,0:T(2,128)(2,1)} %pad_maximum_fusion, s32[1024]{0:T(1024)S(1)} %pad_clamp_fusion.1), kind=kCustom, calls=%fused_computation.clone | custom fusion | bytes 12583424 | tf_op jit(solution)/shard_map/jit(_take)/gather | solution.py:40
  217.2 24.8 %copy_select_fusion = (bf16[128,6,2,2048]{3,0,2,1:T(8,128)(2,1)S(1)}, bf16[128,6,2,2048]{3,0,2,1:T(8,128)(2,1)S(1)}) fusion(bf16[128,6,2,2048]{3,2,1,0:T(2,128)(2,1)} %gather_fusion.1, pred[128]{0:T(512)(128)(4,1)S(1)} %get-tuple-element.14, bf16[128,6,2,2048]{3,2,1,0:T(2,128)(2,1)} %gather_fusion, pred[128]{0:T(512)(128)(4,1)S(1)} %get-tuple-element.8), kind=kLoop, calls=%fused_computation.28 | loop fusion | flops 6291456 | bytes 25166080 | tf_op jit(solution)/shard_map/jit(_take)/select_n | solution.py:41
  242.0 3.0 fusion.13
  245.1 1.6 maximum_multiply_fusion
  246.7 0.0 reduce-scatter.2.cloned.1.call-update
  246.7 84.9 %fusion.8 = (f32[2048,2432]{1,0:T(8,128)}, f32[2048,2432]{1,0:T(8,128)}) fusion(s32[2432]{0:T(1024)S(1)} %iota_add_fusion, s32[2048]{0:T(1024)S(1)} %iota_add_fusion.1), kind=kLoop, calls=%fused_computation.13 | loop fusion | flops 49807360 | bytes 39863808 | tf_op jit(solution)/shard_map/cos | solution.py:36
  331.6 26.1 %fusion.16 = f32[16,2432]{1,0:T(8,128)} fusion(f32[16,4096]{1,0:T(8,128)} %reduce-scatter.2.cloned.1.call-done, f32[2048,2432]{1,0:T(8,128)} %get-tuple-element.13, f32[2048,2432]{1,0:T(8,128)} %get-tuple-element.12), kind=kOutput, calls=%fused_computation.30 | convolution fusion | flops 1922603008 | bytes 40263680 | tf_op jit(solution)/shard_map/dot_general | solution.py:67
  (11 shorter events, 0.1 us)
Async XLA Ops:
  6.5 325.0 %reduce-scatter.2.cloned.1.call-start = ((), (), s32[]{:S(2)}) async-start(), calls=%async_computation.1 | async-start | bytes 2359296 | tf_op jit(solution)/shard_map/reduce_scatter | solution.py:65
  28.5 1.9 copy-start
  30.5 5.9 %copy-start.1 = (s32[1,2,128]{2,1,0:T(2,128)S(1)}, s32[1,2,128]{2,1,0:T(2,128)}, u32[]{:S(2)}) copy-start(s32[1,2,128]{2,1,0:T(2,128)} %param.6) | copy-start | bytes 3076
  34.0 75.9 %collective-permute-start.1 = (bf16[64,6,2,2048]{3,2,1,0:T(2,128)(2,1)S(1)}, bf16[64,6,2,2048]{3,2,1,0:T(2,128)(2,1)S(1)}, u32[]{:S(2)}, u32[]{:S(2)}) collective-permute-start(bf16[64,6,2,2048]{3,2,1,0:T(2,128)(2,1)S(1)} %fusion.11), channel_id=1, source_target_pairs={{0,16},{8,24},{16,32},{24,40},{32,48},{40,56},{48,64},{56,72},{64,... | collective-permute-start | bytes 9437192 | tf_op jit(solution)/shard_map/ppermute | solution.py:19
  35.7 107.1 %collective-permute-start = (bf16[64,6,2,2048]{3,2,1,0:T(2,128)(2,1)S(1)}, bf16[64,6,2,2048]{3,2,1,0:T(2,128)(2,1)S(1)}, u32[]{:S(2)}, u32[]{:S(2)}) collective-permute-start(bf16[64,6,2,2048]{3,2,1,0:T(2,128)(2,1)S(1)} %fusion.11), channel_id=1, source_target_pairs={{0,8},{8,16},{16,24},{24,32},{32,40},{40,48},{48,56},{56,64},{64,7... | collective-permute-start | bytes 9437192 | tf_op jit(solution)/shard_map/ppermute | solution.py:19
Sparse Core Ops, SparseCore 0:
  246.8 79.9 reduce-scatter.1
where the time goes:
time: 372 us; the launch traced here: 365 us
  other arithmetic  166 us (45%)
  waiting for transfers between devices  106 us (28%)
  local copies, waits for them, and re-layouts  49.9 us (13%)
  matrix products  26.1 us (7%)
  between operations  14.4 us (4%)
    ppermute x2, waiting for transfers between devices, from_behind(): return lax.ppermute(value, axis, pairs)  106 us
    cos x1, other arithmetic, lag_table(): return jnp.concatenate([jnp.cos(angles), -jnp.sin(angles)], axis=0)  84.9 us
    concatenate x1, other arithmetic, on_device(): buffer = jnp.concatenate([whitened, first_round, second_round], axis=0)  35.3 us
    dot_general x1, matrix products, on_device(): jnp.dot(owned_share, phase_table, precision=lax.Precision.HIGHEST, prefer...  26.1 us
    select_n x1, other arithmetic, cross_tile(): right_spec = jnp.take(buffer, second_index, axis=0)  24.8 us
    gather x1, local copies, waits for them, and re-layouts, cross_tile(): left_spec = jnp.take(buffer, first_index, axis=0)  19.6 us
    gather x1, local copies, waits for them, and re-layouts, cross_tile(): right_spec = jnp.take(buffer, second_index, axis=0)  19.5 us
    reduce_sum x2, other arithmetic, whiten(): band_power = jnp.sum(grouped * grouped, axis=(2, 4), keepdims=True) / BAND  13.1 us
  transfers between devices with their start and end apart: 3, of which 2 were waited for; matrix products, arithmetic and copies ran while one was open for 23% of the time, Pallas kernels for 0%

commit v1 on v0

v1 whole, which is shorter than its diff:
```python
import functools
import math

import jax
import jax.numpy as jnp
import numpy as np
from jax import lax
from jax.experimental import pallas as pl
from jax.experimental.pallas import tpu as pltpu
from jax.sharding import Mesh
from jax.sharding import PartitionSpec as P
import ml_dtypes

F = 2048
BAND = 128
HALF = 1216
SAMPLES = 36000
K0 = 90
LAGS = 2432
SEGS = 6
CHUNKS = 2
PARTS = 4
WIDE = F // CHUNKS
PIECE = WIDE // PARTS
BANDS = PIECE // BAND
ROWS = 16


def whiten_kernel(me_ref, x_ref, *out_refs):
    for m in range(PARTS):
        start = pl.multiple_of((me_ref[0] ^ m) * PIECE, PIECE)
        for s in range(SEGS):
            x = x_ref[:, s, :, pl.ds(start, PIECE)].astype(jnp.float32)
            re = x[:, 0, :]
            im = x[:, 1, :]
            for b in range(BANDS):
                a = re[:, b * BAND : (b + 1) * BAND]
                c = im[:, b * BAND : (b + 1) * BAND]
                power = jnp.sum(a * a + c * c, axis=-1, keepdims=True) / BAND
                gain = lax.rsqrt(power + 1e-06)
                lane = 2 * s * PIECE + b * BAND
                out_refs[m][:, lane : lane + BAND] = (a * gain).astype(jnp.bfloat16)
                lane += PIECE
                out_refs[m][:, lane : lane + BAND] = (c * gain).astype(jnp.bfloat16)


def whiten(me, spectra, chunk):
    stations = spectra.shape[0]
    width = 2 * SEGS * PIECE
    return pl.pallas_call(
        whiten_kernel,
        grid_spec=pltpu.PrefetchScalarGridSpec(
            num_scalar_prefetch=1,
            grid=(stations // ROWS,),
            in_specs=[pl.BlockSpec((ROWS, SEGS, 2, WIDE), lambda i, me: (i, 0, 0, chunk))],
            out_specs=[pl.BlockSpec((ROWS, width), lambda i, me: (i, 0))] * PARTS,
        ),
        out_shape=[jax.ShapeDtypeStruct((stations, width), jnp.bfloat16)] * PARTS,
        name="whiten",
    )(me, spectra)


def pair_kernel(me_ref, rows_ref, *refs):
    sources, out_ref, held, sems = refs[:6], refs[6], refs[7], refs[8]
    me = me_ref[0]
    core = me & 1
    places = [2 + (me ^ m) for m in range(PARTS)] + [core, 1 - core]
    copies = []
    for n, (source, place) in enumerate(zip(sources, places)):
        start = pl.multiple_of(place * 64, 64)
        copies.append(pltpu.make_async_copy(source, held.at[pl.ds(start, 64)], sems.at[n]))
        copies[-1].start()
    for copy in copies:
        copy.wait()
    for j in range(PARTS):
        column = lax.broadcasted_iota(jnp.int32, (256, 192), 1)
        pick = jnp.where(rows_ref[j] == column, 1.0, 0.0).astype(jnp.bfloat16)
        cross_re = jnp.zeros((128, PIECE), jnp.float32)
        cross_im = jnp.zeros((128, PIECE), jnp.float32)
        for s in range(SEGS):
            taken = jnp.dot(
                pick,
                held[j * 64 : j * 64 + 192, 2 * s * PIECE : 2 * (s + 1) * PIECE],
                preferred_element_type=jnp.float32,
            )
            a_re, a_im = taken[:128, :PIECE], taken[:128, PIECE:]
            b_re, b_im = taken[128:, :PIECE], taken[128:, PIECE:]
            cross_re += a_re * b_re + a_im * b_im
            cross_im += a_im * b_re - a_re * b_im
        out_ref[j, :, :PIECE] = cross_re.astype(out_ref.dtype)
        out_ref[j, :, PIECE:] = cross_im.astype(out_ref.dtype)


def pair_products(me, rows, sources):
    width = 2 * SEGS * PIECE
    return pl.pallas_call(
        pair_kernel,
        in_specs=[
            pl.BlockSpec(memory_space=pltpu.SMEM),
            pl.BlockSpec(memory_space=pltpu.VMEM),
        ]
        + [pl.BlockSpec(memory_space=pl.ANY)] * 6,
        out_specs=pl.BlockSpec(memory_space=pltpu.VMEM),
        out_shape=jax.ShapeDtypeStruct((PARTS, 128, 2 * PIECE), jnp.bfloat16),
        scratch_shapes=[
            pltpu.VMEM((6 * 64, width), jnp.bfloat16),
            pltpu.SemaphoreType.DMA((6,)),
        ],
        compiler_params=pltpu.CompilerParams(vmem_limit_bytes=32 * 1024 * 1024),
        name="pair_products",
    )(me, rows, *sources)


def lag_table():
    freq = np.arange(F, dtype=np.int64).reshape(CHUNKS, PARTS, PIECE)
    lag = np.arange(LAGS, dtype=np.int64) - HALF
    turns = np.remainder((K0 + freq)[..., None] * lag, SAMPLES)
    angles = turns * (2.0 * math.pi / SAMPLES)
    table = np.stack([np.cos(angles), -np.sin(angles)], axis=2)
    return table.reshape(2 * F, LAGS).astype(ml_dtypes.bfloat16)


def on_device(table, spectra, pair_list, pair_count):
    y, c = lax.axis_index("y"), lax.axis_index("c")
    me = (2 * y + c).reshape(1).astype(jnp.int32)
    z_count = lax.axis_size("z")
    z_pairs = [(n, (n + 1) % z_count) for n in range(z_count)]
    live = jnp.arange(128, dtype=jnp.int32)[None, None] < pair_count[:, None, None]
    first = 128 + pair_list[:, 0:1]
    second = pair_list[:, 1:2]
    second = jnp.where(second < 64, second + 128, jnp.where(second < 128, second, second - 128))
    rows = jnp.where(live, jnp.concatenate([first, second], axis=1), -1)
    rows = lax.all_gather(rows, ("y", "c"), axis=0, tiled=True).reshape(PARTS, 256, 1)

    received = []
    for chunk in range(CHUNKS):
        pieces = whiten(me, spectra, chunk)
        blocks = [pieces[0]] + [
            lax.ppermute(pieces[m], ("y", "c"), [(n, n ^ m) for n in range(PARTS)]) for m in (1, 2, 3)
        ]
        behind = [jnp.where(y == 1, blocks[m], blocks[m + 2]) for m in (0, 1)]
        blocks += [lax.ppermute(block, "z", z_pairs) for block in behind]
        cross = pair_products(me, rows, blocks)
        cross = cross.reshape(PARTS * 128, 2 * PIECE)
        got = lax.all_to_all(cross, ("y", "c", "h"), 0, 0, tiled=True)
        got = got.reshape(PARTS, 8, 16, 2 * PIECE).astype(jnp.float32)
        received.append(jnp.sum(got, axis=1))
    total = jnp.stack(received).reshape(2 * F // (2 * PIECE), 16, 2 * PIECE)
    total = jnp.transpose(total, (1, 0, 2)).reshape(16, 2 * F).astype(jnp.bfloat16)
    scale = 1.0 / math.sqrt(48 * F)
    return jnp.dot(total, table, preferred_element_type=jnp.float32) * scale


def solution(mesh):
    inner = Mesh(mesh.devices.reshape(-1, 2, 2, 8), ("z", "y", "c", "h"))
    sta = ("z", "y", "c")
    table = lag_table()

    def run(spectra, pair_list, pair_count):
        return jax.shard_map(
            on_device,
            mesh=inner,
            in_specs=(P(), P(sta, "h", None, None), P(sta, None, None), P(sta)),
            out_specs=P(sta + ("h",), None),
            check_vma=False,
        )(jnp.asarray(table), spectra, pair_list, pair_count)

    return run
```

time: 372 us -> 122 us (0.33)
  the two profiles are of different devices: /device:TPU:2 before, /device:TPU:1 now
where the time goes in v1:
time: 122 us
  waiting for transfers between devices  39.8 us (33%)
  starting transfers between devices  26.7 us (22%)
  Pallas kernels  20.5 us (17%)
  blocking collectives  19.7 us (16%)
  matrix products  8.76 us (7%)
  other arithmetic  2.91 us (2%)
  local copies, waits for them, and re-layouts  2.35 us (2%)
    ppermute x4, waiting for transfers between devices, on_device(): blocks += [lax.ppermute(block, 'z', z_pairs) for block in behind]  29 us
    all_gather x1, blocking collectives, on_device(): lax.all_gather(rows, ('y', 'c'), axis=0, tiled=True).reshape(PARTS, 256, 1)  19.7 us
    all_to_all x2, starting transfers between devices, on_device(): got = lax.all_to_all(cross, ('y', 'c', 'h'), 0, 0, tiled=True)  16.5 us
    pallas_call x2, Pallas kernels, whiten(): pl.pallas_call(whiten_kernel, grid_spec=pltpu.PrefetchScalarGridSpec(num_...  12.6 us
    all_to_all x2, waiting for transfers between devices, on_device(): got = lax.all_to_all(cross, ('y', 'c', 'h'), 0, 0, tiled=True)  10.8 us
    dot_general x1, matrix products, on_device(): return jnp.dot(total, table, preferred_element_type=jnp.float32) * scale  8.76 us
    pallas_call x2, Pallas kernels, pair_products(): pl.pallas_call(pair_kernel, in_specs=[pl.BlockSpec(memory_space=pltpu.SME...  7.87 us
    ppermute x6, starting transfers between devices, on_device(): lax.ppermute(pieces[m], ('y', 'c'), [(n, n ^ m) for n in range(PARTS)])  5.3 us
  transfers between devices with their start and end apart: 12, of which 4 were waited for; matrix products, arithmetic and copies ran while one was open for 3% of the time, Pallas kernels for 12%

profile of v1, /device:TPU:1, one launch (start us, length us, event | category | flops | bytes accessed | tf_op | source)
XLA Modules:
  0.0 121.5 jit_solution(13055991182801299101)
XLA Ops:
  0.0 6.3 %whiten.3 = (bf16[64,3072]{1,0:T(8,128)(2,1)}, bf16[64,3072]{1,0:T(8,128)(2,1)}, bf16[64,3072]{1,0:T(8,128)(2,1)}, bf16[64,3072]{1,0:T(8,128)(2,1)}) custom-call(s32[1]{0:T(128)} %bitcast.me_ref, bf16[64,6,2,2048]{3,2,1,0:T(2,128)(2,1)} %x_ref.3), custom_call_target="tpu_custom_call" | custom-call | tf_op jit(solution)/shard_map/whiten/pallas_call | solution.py:50
  6.3 3.2 %collective-permute-start.5 = (bf16[64,3072]{1,0:T(8,128)(2,1)}, bf16[64,3072]{1,0:T(8,128)(2,1)S(1)}, u32[]{:S(2)}, u32[]{:S(2)}) collective-permute-start(bf16[64,3072]{1,0:T(8,128)(2,1)} %get-tuple-element.18), channel_id=1, source_target_pairs={{0,8},{8,0},{16,24},{24,16},{1,9},{9,1},{17,25},{25,17},{2,10},{10... | collective-permute-start | bytes 1179656 | tf_op jit(solution)/shard_map/ppermute | solution.py:139
  9.5 1.7 %collective-permute-start.7 = (bf16[64,3072]{1,0:T(8,128)(2,1)}, bf16[64,3072]{1,0:T(8,128)(2,1)S(1)}, u32[]{:S(2)}, u32[]{:S(2)}) collective-permute-start(bf16[64,3072]{1,0:T(8,128)(2,1)} %get-tuple-element.20), channel_id=1, source_target_pairs={{0,24},{8,16},{16,8},{24,0},{1,25},{9,17},{17,9},{25,1},{2,26},{10... | collective-permute-start | bytes 1179656 | tf_op jit(solution)/shard_map/ppermute | solution.py:139
  11.2 6.3 %whiten.2 = (bf16[64,3072]{1,0:T(8,128)(2,1)}, bf16[64,3072]{1,0:T(8,128)(2,1)}, bf16[64,3072]{1,0:T(8,128)(2,1)}, bf16[64,3072]{1,0:T(8,128)(2,1)}) custom-call(s32[1]{0:T(128)} %bitcast.me_ref, bf16[64,6,2,2048]{3,2,1,0:T(2,128)(2,1)} %x_ref.3), custom_call_target="tpu_custom_call" | custom-call | tf_op jit(solution)/shard_map/whiten/pallas_call | solution.py:50
  17.7 0.8 slice_add_fusion
  19.2 19.7 %all_gather.3 = s32[4,2,128]{2,1,0:T(2,128)S(1)} all-gather(s32[1,2,128]{2,1,0:T(2,128)S(1)} %add_select_fusion), channel_id=1, replica_groups=mesh['z'=8,'y'=2,'c'=2,'h'=8] {'y','c'}, dimensions={0}, use_global_device_ids=true | all-gather | bytes 5120 | tf_op jit(solution)/shard_map/all_gather | solution.py:133
  38.8 0.3 reshape.87.rows_ref
  39.4 1.3 %collective-permute-start.8 = (bf16[64,3072]{1,0:T(8,128)(2,1)S(1)}, bf16[64,3072]{1,0:T(8,128)(2,1)S(1)}, u32[]{:S(2)}, u32[]{:S(2)}) collective-permute-start(bf16[64,3072]{1,0:T(8,128)(2,1)S(1)} %broadcast_select_fusion.1), channel_id=1, source_target_pairs={{0,32},{32,64},{64,96},{96,128},{128,160},{160,192},{192,224},{224... | collective-permute-start | bytes 1179656 | tf_op jit(solution)/shard_map/ppermute | solution.py:142
  40.7 1.7 %collective-permute-start.9 = (bf16[64,3072]{1,0:T(8,128)(2,1)S(1)}, bf16[64,3072]{1,0:T(8,128)(2,1)S(1)}, u32[]{:S(2)}, u32[]{:S(2)}) collective-permute-start(bf16[64,3072]{1,0:T(8,128)(2,1)S(1)} %broadcast_select_fusion), channel_id=1, source_target_pairs={{0,32},{32,64},{64,96},{96,128},{128,160},{160,192},{192,224},{224... | collective-permute-start | bytes 1179656 | tf_op jit(solution)/shard_map/ppermute | solution.py:142
  42.4 0.8 broadcast_select_fusion.3
  43.2 1.6 %collective-permute-start.3 = (bf16[64,3072]{1,0:T(8,128)(2,1)}, bf16[64,3072]{1,0:T(8,128)(2,1)S(1)}, u32[]{:S(2)}, u32[]{:S(2)}) collective-permute-start(bf16[64,3072]{1,0:T(8,128)(2,1)} %broadcast_select_fusion.3), channel_id=1, source_target_pairs={{0,32},{32,64},{64,96},{96,128},{128,160},{160,192},{192,224},{224... | collective-permute-start | bytes 1179656 | tf_op jit(solution)/shard_map/ppermute | solution.py:142
  44.9 9.0 %collective-permute-done.8.refs_4_ = bf16[64,3072]{1,0:T(8,128)(2,1)S(1)} collective-permute-done((bf16[64,3072]{1,0:T(8,128)(2,1)S(1)}, bf16[64,3072]{1,0:T(8,128)(2,1)S(1)}, u32[]{:S(2)}, u32[]{:S(2)}) %collective-permute-start.8) | collective-permute-done | bytes 393248 | tf_op jit(solution)/shard_map/ppermute | solution.py:142
  53.9 8.4 %collective-permute-done.9.refs_5_ = bf16[64,3072]{1,0:T(8,128)(2,1)S(1)} collective-permute-done((bf16[64,3072]{1,0:T(8,128)(2,1)S(1)}, bf16[64,3072]{1,0:T(8,128)(2,1)S(1)}, u32[]{:S(2)}, u32[]{:S(2)}) %collective-permute-start.9) | collective-permute-done | bytes 393248 | tf_op jit(solution)/shard_map/ppermute | solution.py:142
  62.3 1.0 copy-done.1
  63.3 3.9 %pair_products.3 = bf16[4,128,512]{2,1,0:T(8,128)(2,1)} custom-call(s32[1]{0:T(128)} %bitcast.me_ref, s32[4,256,1]{2,1,0:T(8,128)S(1)} %reshape.87.rows_ref, bf16[64,3072]{1,0:T(8,128)(2,1)S(1)} %copy-done.1, bf16[64,3072]{1,0:T(8,128)(2,1)S(1)} %collective-permute-done.5.refs_1_, bf16[64,3072]{1,0:T(8,128)(2,1)S(1)} %collective-permute-done.6.refs_2_, ...), custom_call_target="tpu_custom_call" | custom-call | tf_op jit(solution)/shard_map/pair_products/pallas_call | solution.py:96
  67.2 8.4 %all-to-all-start.1 = ((bf16[32,16,512]{2,1,0:T(8,128)(2,1)}), bf16[32,16,512]{2,1,0:T(8,128)(2,1)}, u32[]{:S(2)}, u32[]{:S(2)}) async-start(bf16[32,16,512]{2,1,0:T(8,128)(2,1)} %bitcast.5), calls=%async_computation.1 | async-start | bytes 1048576 | tf_op jit(solution)/shard_map/all_to_all | solution.py:145
  75.7 0.3 collective-permute-start.4
  76.0 11.6 %collective-permute-done.4.refs_5_ = bf16[64,3072]{1,0:T(8,128)(2,1)S(1)} collective-permute-done((bf16[64,3072]{1,0:T(8,128)(2,1)S(1)}, bf16[64,3072]{1,0:T(8,128)(2,1)S(1)}, u32[]{:S(2)}, u32[]{:S(2)}) %collective-permute-start.4) | collective-permute-done | bytes 393248 | tf_op jit(solution)/shard_map/ppermute | solution.py:142
  87.6 1.0 copy-done
  88.6 3.9 %pair_products.2 = bf16[4,128,512]{2,1,0:T(8,128)(2,1)} custom-call(s32[1]{0:T(128)} %bitcast.me_ref, s32[4,256,1]{2,1,0:T(8,128)S(1)} %reshape.87.rows_ref, bf16[64,3072]{1,0:T(8,128)(2,1)S(1)} %copy-done, bf16[64,3072]{1,0:T(8,128)(2,1)S(1)} %collective-permute-done.refs_1_, bf16[64,3072]{1,0:T(8,128)(2,1)S(1)} %collective-permute-done.1.refs_2_, ...), custom_call_target="tpu_custom_call" | custom-call | tf_op jit(solution)/shard_map/pair_products/pallas_call | solution.py:96
  92.5 8.1 %all-to-all-start = ((bf16[32,16,512]{2,1,0:T(8,128)(2,1)}), bf16[32,16,512]{2,1,0:T(8,128)(2,1)S(1)}, u32[]{:S(2)}, u32[]{:S(2)}) async-start(bf16[32,16,512]{2,1,0:T(8,128)(2,1)} %bitcast.2), calls=%async_computation | async-start | bytes 1048576 | tf_op jit(solution)/shard_map/all_to_all | solution.py:145
  100.7 1.1 bitcast_reduce_fusion
  101.8 10.8 %all-to-all-done = bf16[32,16,512]{2,1,0:T(8,128)(2,1)S(1)} async-done(((bf16[32,16,512]{2,1,0:T(8,128)(2,1)}), bf16[32,16,512]{2,1,0:T(8,128)(2,1)S(1)}, u32[]{:S(2)}, u32[]{:S(2)}) %all-to-all-start) | async-done | bytes 524320 | tf_op jit(solution)/shard_map/all_to_all | solution.py:145
  112.7 8.8 %convolution_multiply_fusion = f32[16,2432]{1,0:T(8,128)} fusion(bf16[16,4096]{1,0:T(8,128)(2,1)S(1)} %bitcast.19, bf16[4096,2432]{1,0:T(8,128)(2,1)} %constant.28.clone), kind=kOutput, calls=%fused_computation | convolution fusion | flops 318806016 | bytes 20209664 | tf_op jit(solution)/shard_map/dot_general | solution.py:151
  (22 shorter events, 0.7 us)
Async XLA Ops:
  6.3 33.1 %collective-permute-start.5 = (bf16[64,3072]{1,0:T(8,128)(2,1)}, bf16[64,3072]{1,0:T(8,128)(2,1)S(1)}, u32[]{:S(2)}, u32[]{:S(2)}) collective-permute-start(bf16[64,3072]{1,0:T(8,128)(2,1)} %get-tuple-element.18), channel_id=1, source_target_pairs={{0,8},{8,0},{16,24},{24,16},{1,9},{9,1},{17,25},{25,17},{2,10},{10... | collective-permute-start | bytes 1179656 | tf_op jit(solution)/shard_map/ppermute | solution.py:139
  9.5 29.6 %collective-permute-start.6 = (bf16[64,3072]{1,0:T(8,128)(2,1)}, bf16[64,3072]{1,0:T(8,128)(2,1)S(1)}, u32[]{:S(2)}, u32[]{:S(2)}) collective-permute-start(bf16[64,3072]{1,0:T(8,128)(2,1)} %get-tuple-element.19), channel_id=1, source_target_pairs={{0,16},{8,24},{16,0},{24,8},{1,17},{9,25},{17,1},{25,9},{2,18},{10... | collective-permute-start | bytes 1179656 | tf_op jit(solution)/shard_map/ppermute | solution.py:139
  9.5 31.1 %collective-permute-start.7 = (bf16[64,3072]{1,0:T(8,128)(2,1)}, bf16[64,3072]{1,0:T(8,128)(2,1)S(1)}, u32[]{:S(2)}, u32[]{:S(2)}) collective-permute-start(bf16[64,3072]{1,0:T(8,128)(2,1)} %get-tuple-element.20), channel_id=1, source_target_pairs={{0,24},{8,16},{16,8},{24,0},{1,25},{9,17},{17,9},{25,1},{2,26},{10... | collective-permute-start | bytes 1179656 | tf_op jit(solution)/shard_map/ppermute | solution.py:139
  17.5 58.1 %collective-permute-start = (bf16[64,3072]{1,0:T(8,128)(2,1)}, bf16[64,3072]{1,0:T(8,128)(2,1)S(1)}, u32[]{:S(2)}, u32[]{:S(2)}) collective-permute-start(bf16[64,3072]{1,0:T(8,128)(2,1)} %get-tuple-element.14), channel_id=1, source_target_pairs={{0,8},{8,0},{16,24},{24,16},{1,9},{9,1},{17,25},{25,17},{2,10},{10... | collective-permute-start | bytes 1179656 | tf_op jit(solution)/shard_map/ppermute | solution.py:139
  17.7 24.8 %collective-permute-start.1 = (bf16[64,3072]{1,0:T(8,128)(2,1)}, bf16[64,3072]{1,0:T(8,128)(2,1)S(1)}, u32[]{:S(2)}, u32[]{:S(2)}) collective-permute-start(bf16[64,3072]{1,0:T(8,128)(2,1)} %get-tuple-element.15), channel_id=1, source_target_pairs={{0,16},{8,24},{16,0},{24,8},{1,17},{9,25},{17,1},{25,9},{2,18},{10... | collective-permute-start | bytes 1179656 | tf_op jit(solution)/shard_map/ppermute | solution.py:139
  39.2 36.5 %collective-permute-start.2 = (bf16[64,3072]{1,0:T(8,128)(2,1)}, bf16[64,3072]{1,0:T(8,128)(2,1)S(1)}, u32[]{:S(2)}, u32[]{:S(2)}) collective-permute-start(bf16[64,3072]{1,0:T(8,128)(2,1)} %get-tuple-element.16), channel_id=1, source_target_pairs={{0,24},{8,16},{16,8},{24,0},{1,25},{9,17},{17,9},{25,1},{2,26},{10... | collective-permute-start | bytes 1179656 | tf_op jit(solution)/shard_map/ppermute | solution.py:139
  39.4 14.5 %collective-permute-start.8 = (bf16[64,3072]{1,0:T(8,128)(2,1)S(1)}, bf16[64,3072]{1,0:T(8,128)(2,1)S(1)}, u32[]{:S(2)}, u32[]{:S(2)}) collective-permute-start(bf16[64,3072]{1,0:T(8,128)(2,1)S(1)} %broadcast_select_fusion.1), channel_id=1, source_target_pairs={{0,32},{32,64},{64,96},{96,128},{128,160},{160,192},{192,224},{224... | collective-permute-start | bytes 1179656 | tf_op jit(solution)/shard_map/ppermute | solution.py:142
  40.7 21.6 %collective-permute-start.9 = (bf16[64,3072]{1,0:T(8,128)(2,1)S(1)}, bf16[64,3072]{1,0:T(8,128)(2,1)S(1)}, u32[]{:S(2)}, u32[]{:S(2)}) collective-permute-start(bf16[64,3072]{1,0:T(8,128)(2,1)S(1)} %broadcast_select_fusion), channel_id=1, source_target_pairs={{0,32},{32,64},{64,96},{96,128},{128,160},{160,192},{192,224},{224... | collective-permute-start | bytes 1179656 | tf_op jit(solution)/shard_map/ppermute | solution.py:142
  43.2 32.7 %collective-permute-start.3 = (bf16[64,3072]{1,0:T(8,128)(2,1)}, bf16[64,3072]{1,0:T(8,128)(2,1)S(1)}, u32[]{:S(2)}, u32[]{:S(2)}) collective-permute-start(bf16[64,3072]{1,0:T(8,128)(2,1)} %broadcast_select_fusion.3), channel_id=1, source_target_pairs={{0,32},{32,64},{64,96},{96,128},{128,160},{160,192},{192,224},{224... | collective-permute-start | bytes 1179656 | tf_op jit(solution)/shard_map/ppermute | solution.py:142
  62.3 1.0 copy-start.1
  67.2 25.3 %all-to-all-start.1 = ((bf16[32,16,512]{2,1,0:T(8,128)(2,1)}), bf16[32,16,512]{2,1,0:T(8,128)(2,1)}, u32[]{:S(2)}, u32[]{:S(2)}) async-start(bf16[32,16,512]{2,1,0:T(8,128)(2,1)} %bitcast.5), calls=%async_computation.1 | async-start | bytes 1048576 | tf_op jit(solution)/shard_map/all_to_all | solution.py:145
  75.7 11.9 %collective-permute-start.4 = (bf16[64,3072]{1,0:T(8,128)(2,1)S(1)}, bf16[64,3072]{1,0:T(8,128)(2,1)S(1)}, u32[]{:S(2)}, u32[]{:S(2)}) collective-permute-start(bf16[64,3072]{1,0:T(8,128)(2,1)S(1)} %broadcast_select_fusion.2), channel_id=1, source_target_pairs={{0,32},{32,64},{64,96},{96,128},{128,160},{160,192},{192,224},{224... | collective-permute-start | bytes 1179656 | tf_op jit(solution)/shard_map/ppermute | solution.py:142
  87.6 1.0 copy-start
  92.5 20.1 %all-to-all-start = ((bf16[32,16,512]{2,1,0:T(8,128)(2,1)}), bf16[32,16,512]{2,1,0:T(8,128)(2,1)S(1)}, u32[]{:S(2)}, u32[]{:S(2)}) async-start(bf16[32,16,512]{2,1,0:T(8,128)(2,1)} %bitcast.2), calls=%async_computation | async-start | bytes 1048576 | tf_op jit(solution)/shard_map/all_to_all | solution.py:145

commit v2 on v1

--- a/solution.py
+++ b/solution.py
@@ -24,6 +24,8 @@
 PIECE = WIDE // PARTS
 BANDS = PIECE // BAND
 ROWS = 16
+SPAN = 256
+TURNS = -(-LAGS // SPAN)
 
 
 def whiten_kernel(me_ref, x_ref, *out_refs):
@@ -60,8 +62,9 @@
     )(me, spectra)
 
 
-def pair_kernel(me_ref, rows_ref, *refs):
-    sources, out_ref, held, sems = refs[:6], refs[6], refs[7], refs[8]
+def pair_kernel(me_ref, pick_ref, *refs):
+    *near_refs, behind_ref, out_ref, held, sems = refs
+    sources = list(near_refs) + [behind_ref.at[0], behind_ref.at[1]]
     me = me_ref[0]
     core = me & 1
     places = [2 + (me ^ m) for m in range(PARTS)] + [core, 1 - core]
@@ -73,8 +76,7 @@
     for copy in copies:
         copy.wait()
     for j in range(PARTS):
-        column = lax.broadcasted_iota(jnp.int32, (256, 192), 1)
-        pick = jnp.where(rows_ref[j] == column, 1.0, 0.0).astype(jnp.bfloat16)
+        pick = pick_ref[j ^ me]
         cross_re = jnp.zeros((128, PIECE), jnp.float32)
         cross_im = jnp.zeros((128, PIECE), jnp.float32)
         for s in range(SEGS):
@@ -91,7 +93,7 @@
         out_ref[j, :, PIECE:] = cross_im.astype(out_ref.dtype)
 
 
-def pair_products(me, rows, sources):
+def pair_products(me, picks, sources):
     width = 2 * SEGS * PIECE
     return pl.pallas_call(
         pair_kernel,
@@ -99,7 +101,7 @@
             pl.BlockSpec(memory_space=pltpu.SMEM),
             pl.BlockSpec(memory_space=pltpu.VMEM),
         ]
-        + [pl.BlockSpec(memory_space=pl.ANY)] * 6,
+        + [pl.BlockSpec(memory_space=pltpu.HBM)] * 5,
         out_specs=pl.BlockSpec(memory_space=pltpu.VMEM),
         out_shape=jax.ShapeDtypeStruct((PARTS, 128, 2 * PIECE), jnp.bfloat16),
         scratch_shapes=[
@@ -108,19 +110,65 @@
         ],
         compiler_params=pltpu.CompilerParams(vmem_limit_bytes=32 * 1024 * 1024),
         name="pair_products",
-    )(me, rows, *sources)
-
-
-def lag_table():
-    freq = np.arange(F, dtype=np.int64).reshape(CHUNKS, PARTS, PIECE)
-    lag = np.arange(LAGS, dtype=np.int64) - HALF
-    turns = np.remainder((K0 + freq)[..., None] * lag, SAMPLES)
-    angles = turns * (2.0 * math.pi / SAMPLES)
-    table = np.stack([np.cos(angles), -np.sin(angles)], axis=2)
-    return table.reshape(2 * F, LAGS).astype(ml_dtypes.bfloat16)
-
-
-def on_device(table, spectra, pair_list, pair_count):
+    )(me, picks, *sources)
+
+
+def lag_kernel(cos_ref, sin_ref, table_ref, *refs):
+    got_refs, out_ref = refs[:-1], refs[-1]
+    total = jnp.zeros((16 * TURNS, SPAN), jnp.float32)
+    for g, got_ref in enumerate(got_refs):
+        for j in range(PARTS):
+            cross = got_ref[8 * j].astype(jnp.float32)
+            for h in range(1, 8):
+                cross += got_ref[8 * j + h].astype(jnp.float32)
+            re, im = cross[:, :PIECE], cross[:, PIECE:]
+            bins = slice((g * PARTS + j) * PIECE, (g * PARTS + j + 1) * PIECE)
+            turned_re, turned_im = [], []
+            for r in range(TURNS):
+                cos, sin = cos_ref[r : r + 1, bins], sin_ref[r : r + 1, bins]
+                turned_re.append(re * cos - im * sin)
+                turned_im.append(re * sin + im * cos)
+            for k, turned in enumerate((turned_re, turned_im)):
+                start = (2 * (g * PARTS + j) + k) * PIECE
+                total += jnp.dot(
+                    jnp.concatenate(turned).astype(jnp.bfloat16),
+                    table_ref[start : start + PIECE],
+                    preferred_element_type=jnp.float32,
+                )
+    total = total * (1.0 / math.sqrt(48 * F))
+    for r in range(TURNS):
+        width = min(SPAN, LAGS - r * SPAN)
+        out_ref[:, r * SPAN : r * SPAN + width] = total[16 * r : 16 * (r + 1), :width]
+
+
+def lag_sums(tables, got):
+    return pl.pallas_call(
+        lag_kernel,
+        out_shape=jax.ShapeDtypeStruct((16, LAGS), jnp.float32),
+        compiler_params=pltpu.CompilerParams(vmem_limit_bytes=32 * 1024 * 1024),
+        name="lag_sums",
+    )(*tables, *got)
+
+
+def angles(freq, lag):
+    turns = np.remainder((K0 + freq) * lag, SAMPLES)
+    return turns * (2.0 * math.pi / SAMPLES)
+
+
+def lag_tables():
+    freq = np.arange(F, dtype=np.int64)
+    turn = angles(freq, SPAN * np.arange(TURNS, dtype=np.int64)[:, None])
+    near = angles(freq[:, None], np.arange(SPAN, dtype=np.int64) - HALF)
+    near = near.reshape(CHUNKS * PARTS, PIECE, SPAN)
+    table = np.stack([np.cos(near), -np.sin(near)], axis=1).reshape(2 * F, SPAN)
+    return (
+        np.cos(turn).astype(np.float32),
+        np.sin(turn).astype(np.float32),
+        table.astype(ml_dtypes.bfloat16),
+    )
+
+
+def on_device(tables, spectra, pair_list, pair_count):
     y, c = lax.axis_index("y"), lax.axis_index("c")
     me = (2 * y + c).reshape(1).astype(jnp.int32)
     z_count = lax.axis_size("z")
@@ -130,39 +178,49 @@
     second = pair_list[:, 1:2]
     second = jnp.where(second < 64, second + 128, jnp.where(second < 128, second, second - 128))
     rows = jnp.where(live, jnp.concatenate([first, second], axis=1), -1)
-    rows = lax.all_gather(rows, ("y", "c"), axis=0, tiled=True).reshape(PARTS, 256, 1)
-
-    received = []
+    yc_pairs = [[(n, n ^ m) for n in range(PARTS)] for m in range(PARTS)]
+    rows = rows.reshape(1, 256)
+    spectra, rows = lax.optimization_barrier((spectra, rows))
+    near = [rows] + [lax.ppermute(rows, ("y", "c"), yc_pairs[m]) for m in (1, 2, 3)]
+    column = jnp.arange(192, dtype=jnp.int32)
+    picks = (jnp.concatenate(near)[:, :, None] == column).astype(jnp.bfloat16)
+
+    arrived = []
     for chunk in range(CHUNKS):
         pieces = whiten(me, spectra, chunk)
-        blocks = [pieces[0]] + [
-            lax.ppermute(pieces[m], ("y", "c"), [(n, n ^ m) for n in range(PARTS)]) for m in (1, 2, 3)
-        ]
-        behind = [jnp.where(y == 1, blocks[m], blocks[m + 2]) for m in (0, 1)]
-        blocks += [lax.ppermute(block, "z", z_pairs) for block in behind]
-        cross = pair_products(me, rows, blocks)
-        cross = cross.reshape(PARTS * 128, 2 * PIECE)
-        got = lax.all_to_all(cross, ("y", "c", "h"), 0, 0, tiled=True)
-        got = got.reshape(PARTS, 8, 16, 2 * PIECE).astype(jnp.float32)
-        received.append(jnp.sum(got, axis=1))
-    total = jnp.stack(received).reshape(2 * F // (2 * PIECE), 16, 2 * PIECE)
-    total = jnp.transpose(total, (1, 0, 2)).reshape(16, 2 * F).astype(jnp.bfloat16)
-    scale = 1.0 / math.sqrt(48 * F)
-    return jnp.dot(total, table, preferred_element_type=jnp.float32) * scale
+        if chunk == 0:
+            pieces, picks = lax.optimization_barrier((pieces, picks))
+        arrived.append(
+            [pieces[0]] + [lax.ppermute(pieces[m], ("y", "c"), yc_pairs[m]) for m in (2, 3, 1)]
+        )
+    moved, behind = [], []
+    for own, far, cross, side in arrived:
+        ahead = [jnp.where(y == 1, own, far), jnp.where(y == 1, side, cross)]
+        moved.append(jnp.stack(ahead))
+        behind.append(lax.ppermute(moved[-1], "z", z_pairs))
+    got = []
+    for chunk in range(CHUNKS):
+        own, far, cross, side = arrived[chunk]
+        product = pair_products(me, picks, [own, side, far, cross, behind[chunk]])
+        product = product.reshape(PARTS * 128, 2 * PIECE)
+        if chunk == 0:
+            product, _ = lax.optimization_barrier((product, moved[1]))
+        got.append(lax.all_to_all(product, ("y", "c", "h"), 0, 0, tiled=True).reshape(32, 16, 2 * PIECE))
+    return lag_sums(tables, got)
 
 
 def solution(mesh):
     inner = Mesh(mesh.devices.reshape(-1, 2, 2, 8), ("z", "y", "c", "h"))
     sta = ("z", "y", "c")
-    table = lag_table()
+    tables = lag_tables()
 
     def run(spectra, pair_list, pair_count):
         return jax.shard_map(
             on_device,
             mesh=inner,
-            in_specs=(P(), P(sta, "h", None, None), P(sta, None, None), P(sta)),
+            in_specs=((P(),) * 3, P(sta, "h", None, None), P(sta, None, None), P(sta)),
             out_specs=P(sta + ("h",), None),
             check_vma=False,
-        )(jnp.asarray(table), spectra, pair_list, pair_count)
+        )(tuple(jnp.asarray(table) for table in tables), spectra, pair_list, pair_count)
 
     return run

time: 122 us -> 104 us (0.85)
  starting transfers between devices: 26.7 us -> 17.4 us
  matrix products: 8.76 us -> 0 us
  local copies, waits for them, and re-layouts: 2.35 us -> 6.41 us
  waiting for transfers between devices: 39.8 us -> 36.8 us
    all_gather x1 -> x0, blocking collectives: 19.7 us -> none  [on_device(): lax.all_gather(rows, ('y', 'c'), axis=0, tiled=True).reshape(PARTS, 256, 1)]
    all_to_all x0 -> x1, blocking collectives: none -> 19.5 us  [on_device(): lax.all_to_all(product, ('y', 'c', 'h'), 0, 0, tiled=True)]
    all_to_all x2 -> x1, waiting for transfers between devices: 10.8 us -> 0.01 us  [on_device(): lax.all_to_all(product, ('y', 'c', 'h'), 0, 0, tiled=True)]
    dot_general x1 -> x0, matrix products: 8.76 us -> none  [on_device(): return jnp.dot(total, table, preferred_element_type=jnp.float32) * scale]
    ppermute x10 -> x11, waiting for transfers between devices: 29 us -> 36.8 us  [the longest x6 25.2 us: on_device(): lax.ppermute(pieces[m], ('y', 'c'), yc_pairs[m])]
    all_to_all x2 -> x1, starting transfers between devices: 16.5 us -> 9.36 us  [on_device(): lax.all_to_all(product, ('y', 'c', 'h'), 0, 0, tiled=True)]
    unnamed x5 -> x27, local copies, waits for them, and re-layouts: 2 us -> 6.41 us
    ppermute x10 -> x11, starting transfers between devices: 10.2 us -> 8.04 us  [the longest x6 5.77 us: on_device(): lax.ppermute(pieces[m], ('y', 'c'), yc_pairs[m])]
  transfers between devices with their start and end apart: 12 -> 12, of which waited for: 4 -> 5; matrix products, arithmetic and copies ran while one was open for 3% -> 1% of each run, Pallas kernels for 12% -> 13%
where the time goes in v2:
time: 104 us
  waiting for transfers between devices  36.8 us (35%)
  Pallas kernels  20.8 us (20%)
  blocking collectives  19.5 us (19%)
  starting transfers between devices  17.4 us (17%)
  local copies, waits for them, and re-layouts  6.41 us (6%)
  other arithmetic  2.29 us (2%)
    ppermute x6, waiting for transfers between devices, on_device(): lax.ppermute(pieces[m], ('y', 'c'), yc_pairs[m])  25.2 us
    all_to_all x1, blocking collectives, on_device(): lax.all_to_all(product, ('y', 'c', 'h'), 0, 0, tiled=True)  19.5 us
    pallas_call x2, Pallas kernels, whiten(): pl.pallas_call(whiten_kernel, grid_spec=pltpu.PrefetchScalarGridSpec(num_...  12.6 us
    all_to_all x1, starting transfers between devices, on_device(): lax.all_to_all(product, ('y', 'c', 'h'), 0, 0, tiled=True)  9.36 us
    ppermute x2, waiting for transfers between devices, on_device(): behind.append(lax.ppermute(moved[-1], 'z', z_pairs))  8.99 us
    pallas_call x2, Pallas kernels, pair_products(): pl.pallas_call(pair_kernel, in_specs=[pl.BlockSpec(memory_space=pltpu.SME...  6.85 us
    unnamed x27, local copies, waits for them, and re-layouts  6.41 us
    ppermute x6, starting transfers between devices, on_device(): lax.ppermute(pieces[m], ('y', 'c'), yc_pairs[m])  5.77 us
  transfers between devices with their start and end apart: 12, of which 5 were waited for; matrix products, arithmetic and copies ran while one was open for 1% of the time, Pallas kernels for 13%

profile of v2, /device:TPU:1, one launch (start us, length us, event | category | flops | bytes accessed | tf_op | source)
XLA Modules:
  0.0 104.0 jit_solution(629980006260933734)
XLA Ops:
  1.5 6.3 %whiten.3 = (bf16[64,3072]{1,0:T(8,128)(2,1)}, bf16[64,3072]{1,0:T(8,128)(2,1)}, bf16[64,3072]{1,0:T(8,128)(2,1)}, bf16[64,3072]{1,0:T(8,128)(2,1)}) custom-call(s32[1]{0:T(128)} %bitcast.me_ref, bf16[64,6,2,2048]{3,2,1,0:T(2,128)(2,1)} %x_ref.1), custom_call_target="tpu_custom_call" | custom-call | tf_op jit(solution)/shard_map/whiten/pallas_call | solution.py:52
  7.8 3.2 %collective-permute-start.8 = (bf16[64,3072]{1,0:T(8,128)(2,1)}, bf16[64,3072]{1,0:T(8,128)(2,1)S(1)}, u32[]{:S(2)}, u32[]{:S(2)}) collective-permute-start(bf16[64,3072]{1,0:T(8,128)(2,1)} %get-tuple-element.34), channel_id=1, source_target_pairs={{0,8},{8,0},{16,24},{24,16},{1,9},{9,1},{17,25},{25,17},{2,10},{10... | collective-permute-start | bytes 1179656 | tf_op jit(solution)/shard_map/ppermute | solution.py:194
  11.0 1.8 %collective-permute-start.2 = (s32[1,256]{1,0:T(1,128)S(1)}, s32[1,256]{1,0:T(1,128)S(1)}, u32[]{:S(2)}, u32[]{:S(2)}) collective-permute-start(s32[1,256]{1,0:T(1,128)S(1)} %bitcast_select_fusion), channel_id=1, source_target_pairs={{0,24},{8,16},{16,8},{24,0},{1,25},{9,17},{17,9},{25,1},{2,26},{10... | collective-permute-start | bytes 3080 | tf_op jit(solution)/shard_map/ppermute | solution.py:184
  13.2 6.3 %whiten.2 = (bf16[64,3072]{1,0:T(8,128)(2,1)}, bf16[64,3072]{1,0:T(8,128)(2,1)}, bf16[64,3072]{1,0:T(8,128)(2,1)}, bf16[64,3072]{1,0:T(8,128)(2,1)}) custom-call(s32[1]{0:T(128)} %bitcast.me_ref, bf16[64,6,2,2048]{3,2,1,0:T(2,128)(2,1)} %x_ref.1), custom_call_target="tpu_custom_call" | custom-call | tf_op jit(solution)/shard_map/whiten/pallas_call | solution.py:52
  19.5 2.6 %collective-permute-done.2 = s32[1,256]{1,0:T(1,128)S(1)} collective-permute-done((s32[1,256]{1,0:T(1,128)S(1)}, s32[1,256]{1,0:T(1,128)S(1)}, u32[]{:S(2)}, u32[]{:S(2)}) %collective-permute-start.2) | collective-permute-done | bytes 1056 | tf_op jit(solution)/shard_map/ppermute | solution.py:184
  22.4 0.8 collective-permute-start.3
  23.2 1.2 %collective-permute-start.4 = (bf16[64,3072]{1,0:T(8,128)(2,1)}, bf16[64,3072]{1,0:T(8,128)(2,1)S(1)}, u32[]{:S(2)}, u32[]{:S(2)}) collective-permute-start(bf16[64,3072]{1,0:T(8,128)(2,1)} %get-tuple-element.30), channel_id=1, source_target_pairs={{0,16},{8,24},{16,0},{24,8},{1,17},{9,25},{17,1},{25,9},{2,18},{10... | collective-permute-start | bytes 1179656 | tf_op jit(solution)/shard_map/ppermute | solution.py:194
  24.9 8.0 %collective-permute-done.7.refs_2_ = bf16[64,3072]{1,0:T(8,128)(2,1)S(1)} collective-permute-done((bf16[64,3072]{1,0:T(8,128)(2,1)}, bf16[64,3072]{1,0:T(8,128)(2,1)S(1)}, u32[]{:S(2)}, u32[]{:S(2)}) %collective-permute-start.7) | collective-permute-done | bytes 393248 | tf_op jit(solution)/shard_map/ppermute | solution.py:194
  33.2 17.2 %collective-permute-done.5.refs_3_ = bf16[64,3072]{1,0:T(8,128)(2,1)S(1)} collective-permute-done((bf16[64,3072]{1,0:T(8,128)(2,1)}, bf16[64,3072]{1,0:T(8,128)(2,1)S(1)}, u32[]{:S(2)}, u32[]{:S(2)}) %collective-permute-start.5) | collective-permute-done | bytes 393248 | tf_op jit(solution)/shard_map/ppermute | solution.py:194
  50.5 1.0 %pad_maximum_fusion = bf16[2,64,3072]{2,1,0:T(8,128)(2,1)} fusion(bf16[1,64,3072]{2,1,0:T(8,128)(2,1)S(1)} %select_bitcast_fusion.2, bf16[1,64,3072]{2,1,0:T(8,128)(2,1)S(1)} %select_bitcast_fusion.3), kind=kLoop, calls=%fused_computation.2 | loop fusion | flops 393216 | bytes 1572864 | tf_op jit(solution)/shard_map/stack | solution.py:199
  51.5 1.8 %collective-permute-done.10.refs_4_ = bf16[2,64,3072]{2,1,0:T(8,128)(2,1)S(1)} collective-permute-done((bf16[2,64,3072]{2,1,0:T(8,128)(2,1)S(1)}, bf16[2,64,3072]{2,1,0:T(8,128)(2,1)S(1)}, u32[]{:S(2)}, u32[]{:S(2)}) %collective-permute-start.10) | collective-permute-done | bytes 786464 | tf_op jit(solution)/shard_map/ppermute | solution.py:200
  53.3 3.1 %pair_products.3 = bf16[4,128,512]{2,1,0:T(8,128)(2,1)S(1)} custom-call(s32[1]{0:T(128)} %bitcast.me_ref, bf16[4,256,192]{2,1,0:T(8,128)(2,1)S(1)} %fusion.pick_ref, bf16[64,3072]{1,0:T(8,128)(2,1)S(1)} %copy-done.3, bf16[64,3072]{1,0:T(8,128)(2,1)S(1)} %collective-permute-done.8.refs_1_, bf16[64,3072]{1,0:T(8,128)(2,1)S(1)} %collective-permute-done.7.refs_2_, ...), custom_call_target="tpu_custom_call" | custom-call | tf_op jit(solution)/shard_map/pair_products/pallas_call | solution.py:98
  56.4 0.8 copy-done.1
  57.2 9.4 %all-to-all-start.1 = ((bf16[32,16,512]{2,1,0:T(8,128)(2,1)}), bf16[32,16,512]{2,1,0:T(8,128)(2,1)S(1)}, u32[]{:S(2)}, u32[]{:S(2)}) async-start(bf16[32,16,512]{2,1,0:T(8,128)(2,1)} %bitcast.20), calls=%async_computation.1 | async-start | bytes 1048576 | tf_op jit(solution)/shard_map/all_to_all | solution.py:208
  66.6 7.2 %collective-permute-done.6.refs_4_ = bf16[2,64,3072]{2,1,0:T(8,128)(2,1)} collective-permute-done((bf16[2,64,3072]{2,1,0:T(8,128)(2,1)}, bf16[2,64,3072]{2,1,0:T(8,128)(2,1)}, u32[]{:S(2)}, u32[]{:S(2)}) %collective-permute-start.6) | collective-permute-done | bytes 786464 | tf_op jit(solution)/shard_map/ppermute | solution.py:200
  73.7 1.0 copy-done.6
  74.7 1.0 copy-done.8
  75.7 1.0 copy-done.10
  76.7 3.8 %pair_products.2 = bf16[4,128,512]{2,1,0:T(8,128)(2,1)S(1)} custom-call(s32[1]{0:T(128)} %bitcast.me_ref, bf16[4,256,192]{2,1,0:T(8,128)(2,1)S(1)} %fusion.pick_ref, bf16[64,3072]{1,0:T(8,128)(2,1)S(1)} %copy-done.4, bf16[64,3072]{1,0:T(8,128)(2,1)S(1)} %copy-done.6, bf16[64,3072]{1,0:T(8,128)(2,1)S(1)} %copy-done.8, bf16[64,3072]{1,0:T(8,128)(2,1)S(1)} %copy-done.10, ...), custom_call_target="tpu_custom_call" | custom-call | tf_op jit(solution)/shard_map/pair_products/pallas_call | solution.py:98
  80.5 0.8 copy-done.2
  81.3 19.5 %all_to_all.18.refs_0_ = bf16[32,16,512]{2,1,0:T(8,128)(2,1)S(1)} all-to-all(bf16[32,16,512]{2,1,0:T(8,128)(2,1)} %bitcast.21), channel_id=1, replica_groups=mesh['z'=8,'y'=2,'c'=2,'h'=8] {'y','c','h'}, dimensions={0} | all-to-all | bytes 1048576 | tf_op jit(solution)/shard_map/all_to_all | solution.py:208
  100.8 0.9 copy-done.11
  101.7 0.9 copy-done.12
  102.6 1.4 %lag_sums.1 = f32[16,2432]{1,0:T(8,128)} custom-call(f32[10,2048]{1,0:T(8,128)S(1)} %copy-done.11, f32[10,2048]{1,0:T(8,128)S(1)} %copy-done.12, bf16[4096,256]{1,0:T(8,128)(2,1)S(1)} %copy-done, bf16[32,16,512]{2,1,0:T(8,128)(2,1)S(1)} %all_to_all.18.refs_0_, bf16[32,16,512]{2,1,0:T(8,128)(2,1)S(1)} %all-to-all-done.1.refs_1_), custom_call_target="tpu_custom_call" | custom-call | tf_op jit(solution)/shard_map/lag_sums/pallas_call | solution.py:145
  (45 shorter events, 2.4 us)
Async XLA Ops:
  7.8 25.1 %copy-start.3 = (bf16[64,3072]{1,0:T(8,128)(2,1)S(1)}, bf16[64,3072]{1,0:T(8,128)(2,1)}, u32[]{:S(2)}) copy-start(bf16[64,3072]{1,0:T(8,128)(2,1)} %get-tuple-element.32.refs_0_) | copy-start | bytes 1179652
  7.8 16.6 %collective-permute-start.8 = (bf16[64,3072]{1,0:T(8,128)(2,1)}, bf16[64,3072]{1,0:T(8,128)(2,1)S(1)}, u32[]{:S(2)}, u32[]{:S(2)}) collective-permute-start(bf16[64,3072]{1,0:T(8,128)(2,1)} %get-tuple-element.34), channel_id=1, source_target_pairs={{0,8},{8,0},{16,24},{24,16},{1,9},{9,1},{17,25},{25,17},{2,10},{10... | collective-permute-start | bytes 1179656 | tf_op jit(solution)/shard_map/ppermute | solution.py:194
  11.0 13.9 %collective-permute-start.9 = (bf16[64,3072]{1,0:T(8,128)(2,1)}, bf16[64,3072]{1,0:T(8,128)(2,1)S(1)}, u32[]{:S(2)}, u32[]{:S(2)}) collective-permute-start(bf16[64,3072]{1,0:T(8,128)(2,1)} %get-tuple-element.35), channel_id=1, source_target_pairs={{0,24},{8,16},{16,8},{24,0},{1,25},{9,17},{17,9},{25,1},{2,26},{10... | collective-permute-start | bytes 1179656 | tf_op jit(solution)/shard_map/ppermute | solution.py:194
  11.0 11.1 %collective-permute-start.2 = (s32[1,256]{1,0:T(1,128)S(1)}, s32[1,256]{1,0:T(1,128)S(1)}, u32[]{:S(2)}, u32[]{:S(2)}) collective-permute-start(s32[1,256]{1,0:T(1,128)S(1)} %bitcast_select_fusion), channel_id=1, source_target_pairs={{0,24},{8,16},{16,8},{24,0},{1,25},{9,17},{17,9},{25,1},{2,26},{10... | collective-permute-start | bytes 3080 | tf_op jit(solution)/shard_map/ppermute | solution.py:184
  12.8 9.4 %collective-permute-start.1 = (s32[1,256]{1,0:T(1,128)S(1)}, s32[1,256]{1,0:T(1,128)S(1)}, u32[]{:S(2)}, u32[]{:S(2)}) collective-permute-start(s32[1,256]{1,0:T(1,128)S(1)} %bitcast_select_fusion), channel_id=1, source_target_pairs={{0,16},{8,24},{16,0},{24,8},{1,17},{9,25},{17,1},{25,9},{2,18},{10... | collective-permute-start | bytes 3080 | tf_op jit(solution)/shard_map/ppermute | solution.py:184
  12.8 9.4 %collective-permute-start = (s32[1,256]{1,0:T(1,128)S(1)}, s32[1,256]{1,0:T(1,128)S(1)}, u32[]{:S(2)}, u32[]{:S(2)}) collective-permute-start(s32[1,256]{1,0:T(1,128)S(1)} %bitcast_select_fusion), channel_id=1, source_target_pairs={{0,8},{8,0},{16,24},{24,16},{1,9},{9,1},{17,25},{25,17},{2,10},{10... | collective-permute-start | bytes 3080 | tf_op jit(solution)/shard_map/ppermute | solution.py:184
  19.5 30.9 %copy-start.4 = (bf16[64,3072]{1,0:T(8,128)(2,1)S(1)}, bf16[64,3072]{1,0:T(8,128)(2,1)}, u32[]{:S(2)}) copy-start(bf16[64,3072]{1,0:T(8,128)(2,1)} %get-tuple-element.28.refs_0_) | copy-start | bytes 1179652
  22.1 10.8 %collective-permute-start.7 = (bf16[64,3072]{1,0:T(8,128)(2,1)}, bf16[64,3072]{1,0:T(8,128)(2,1)S(1)}, u32[]{:S(2)}, u32[]{:S(2)}) collective-permute-start(bf16[64,3072]{1,0:T(8,128)(2,1)} %get-tuple-element.33), channel_id=1, source_target_pairs={{0,16},{8,24},{16,0},{24,8},{1,17},{9,25},{17,1},{25,9},{2,18},{10... | collective-permute-start | bytes 1179656 | tf_op jit(solution)/shard_map/ppermute | solution.py:194
  22.4 10.8 %collective-permute-start.3 = (bf16[64,3072]{1,0:T(8,128)(2,1)}, bf16[64,3072]{1,0:T(8,128)(2,1)S(1)}, u32[]{:S(2)}, u32[]{:S(2)}) collective-permute-start(bf16[64,3072]{1,0:T(8,128)(2,1)} %get-tuple-element.29), channel_id=1, source_target_pairs={{0,8},{8,0},{16,24},{24,16},{1,9},{9,1},{17,25},{25,17},{2,10},{10... | collective-permute-start | bytes 1179656 | tf_op jit(solution)/shard_map/ppermute | solution.py:194
  23.2 27.2 %collective-permute-start.4 = (bf16[64,3072]{1,0:T(8,128)(2,1)}, bf16[64,3072]{1,0:T(8,128)(2,1)S(1)}, u32[]{:S(2)}, u32[]{:S(2)}) collective-permute-start(bf16[64,3072]{1,0:T(8,128)(2,1)} %get-tuple-element.30), channel_id=1, source_target_pairs={{0,16},{8,24},{16,0},{24,8},{1,17},{9,25},{17,1},{25,9},{2,18},{10... | collective-permute-start | bytes 1179656 | tf_op jit(solution)/shard_map/ppermute | solution.py:194
  24.4 26.0 %collective-permute-start.5 = (bf16[64,3072]{1,0:T(8,128)(2,1)}, bf16[64,3072]{1,0:T(8,128)(2,1)S(1)}, u32[]{:S(2)}, u32[]{:S(2)}) collective-permute-start(bf16[64,3072]{1,0:T(8,128)(2,1)} %get-tuple-element.31), channel_id=1, source_target_pairs={{0,24},{8,16},{16,8},{24,0},{1,25},{9,17},{17,9},{25,1},{2,26},{10... | collective-permute-start | bytes 1179656 | tf_op jit(solution)/shard_map/ppermute | solution.py:194
  33.1 20.3 %collective-permute-start.10 = (bf16[2,64,3072]{2,1,0:T(8,128)(2,1)S(1)}, bf16[2,64,3072]{2,1,0:T(8,128)(2,1)S(1)}, u32[]{:S(2)}, u32[]{:S(2)}) collective-permute-start(bf16[2,64,3072]{2,1,0:T(8,128)(2,1)S(1)} %pad_maximum_fusion.1), channel_id=1, source_target_pairs={{0,32},{32,64},{64,96},{96,128},{128,160},{160,192},{192,224},{224... | collective-permute-start | bytes 2359304 | tf_op jit(solution)/shard_map/ppermute | solution.py:200
  33.2 20.2 %copy-start.5 = (bf16[64,3072]{1,0:T(8,128)(2,1)}, bf16[64,3072]{1,0:T(8,128)(2,1)S(1)}, u32[]{:S(2)}) copy-start(bf16[64,3072]{1,0:T(8,128)(2,1)S(1)} %collective-permute-done.3.refs_1_) | copy-start | bytes 1179652
  50.3 3.0 %copy-start.9 = (bf16[64,3072]{1,0:T(8,128)(2,1)}, bf16[64,3072]{1,0:T(8,128)(2,1)S(1)}, u32[]{:S(2)}) copy-start(bf16[64,3072]{1,0:T(8,128)(2,1)S(1)} %collective-permute-done.5.refs_3_) | copy-start | bytes 1179652
  50.4 2.9 %copy-start.7 = (bf16[64,3072]{1,0:T(8,128)(2,1)}, bf16[64,3072]{1,0:T(8,128)(2,1)S(1)}, u32[]{:S(2)}) copy-start(bf16[64,3072]{1,0:T(8,128)(2,1)S(1)} %collective-permute-done.4.refs_2_) | copy-start | bytes 1179652
  51.5 22.2 %collective-permute-start.6 = (bf16[2,64,3072]{2,1,0:T(8,128)(2,1)}, bf16[2,64,3072]{2,1,0:T(8,128)(2,1)}, u32[]{:S(2)}, u32[]{:S(2)}) collective-permute-start(bf16[2,64,3072]{2,1,0:T(8,128)(2,1)} %pad_maximum_fusion), channel_id=1, source_target_pairs={{0,32},{32,64},{64,96},{96,128},{128,160},{160,192},{192,224},{224... | collective-permute-start | bytes 2359304 | tf_op jit(solution)/shard_map/ppermute | solution.py:200
  57.2 43.6 %copy-start = (bf16[4096,256]{1,0:T(8,128)(2,1)S(1)}, bf16[4096,256]{1,0:T(8,128)(2,1)}, u32[]{:S(2)}) copy-start(bf16[4096,256]{1,0:T(8,128)(2,1)} %constant.30.clone.table_ref) | copy-start | bytes 6291460
  57.2 24.1 %all-to-all-start.1 = ((bf16[32,16,512]{2,1,0:T(8,128)(2,1)}), bf16[32,16,512]{2,1,0:T(8,128)(2,1)S(1)}, u32[]{:S(2)}, u32[]{:S(2)}) async-start(bf16[32,16,512]{2,1,0:T(8,128)(2,1)} %bitcast.20), calls=%async_computation.1 | async-start | bytes 1048576 | tf_op jit(solution)/shard_map/all_to_all | solution.py:208
  73.7 1.0 copy-start.6
  74.7 1.0 copy-start.8
  75.7 1.0 copy-start.10
  80.5 0.8 copy-start.2
  100.8 0.9 copy-start.11
  101.7 0.9 copy-start.12
  (1 other events, 0.8 us)

commit v3 on v2

--- a/solution.py
+++ b/solution.py
@@ -62,12 +62,10 @@
     )(me, spectra)
 
 
-def pair_kernel(me_ref, pick_ref, *refs):
-    *near_refs, behind_ref, out_ref, held, sems = refs
-    sources = list(near_refs) + [behind_ref.at[0], behind_ref.at[1]]
+def pair_kernel(numbers, me_ref, pick_ref, *refs):
+    *sources, out_ref, held, sems = refs
     me = me_ref[0]
-    core = me & 1
-    places = [2 + (me ^ m) for m in range(PARTS)] + [core, 1 - core]
+    places = [1 + (me ^ m) for m in range(PARTS)] + [0, 5]
     copies = []
     for n, (source, place) in enumerate(zip(sources, places)):
         start = pl.multiple_of(place * 64, 64)
@@ -75,35 +73,39 @@
         copies[-1].start()
     for copy in copies:
         copy.wait()
-    for j in range(PARTS):
-        pick = pick_ref[j ^ me]
+    for n, j in enumerate(numbers):
+        if j == 0:
+            pick, rows = pick_ref[me, :, 64:], slice(0, 128)
+        else:
+            pick = pick_ref[j ^ me if j < PARTS else PARTS]
+            rows = slice((j - 1) * 64, (j + 2) * 64)
         cross_re = jnp.zeros((128, PIECE), jnp.float32)
         cross_im = jnp.zeros((128, PIECE), jnp.float32)
         for s in range(SEGS):
             taken = jnp.dot(
                 pick,
-                held[j * 64 : j * 64 + 192, 2 * s * PIECE : 2 * (s + 1) * PIECE],
+                held[rows, 2 * s * PIECE : 2 * (s + 1) * PIECE],
                 preferred_element_type=jnp.float32,
             )
             a_re, a_im = taken[:128, :PIECE], taken[:128, PIECE:]
             b_re, b_im = taken[128:, :PIECE], taken[128:, PIECE:]
             cross_re += a_re * b_re + a_im * b_im
             cross_im += a_im * b_re - a_re * b_im
-        out_ref[j, :, :PIECE] = cross_re.astype(out_ref.dtype)
-        out_ref[j, :, PIECE:] = cross_im.astype(out_ref.dtype)
-
-
-def pair_products(me, picks, sources):
+        out_ref[n, :, :PIECE] = cross_re.astype(out_ref.dtype)
+        out_ref[n, :, PIECE:] = cross_im.astype(out_ref.dtype)
+
+
+def pair_products(numbers, me, picks, sources):
     width = 2 * SEGS * PIECE
     return pl.pallas_call(
-        pair_kernel,
+        functools.partial(pair_kernel, numbers),
         in_specs=[
             pl.BlockSpec(memory_space=pltpu.SMEM),
             pl.BlockSpec(memory_space=pltpu.VMEM),
         ]
-        + [pl.BlockSpec(memory_space=pltpu.HBM)] * 5,
+        + [pl.BlockSpec(memory_space=pltpu.HBM)] * 6,
         out_specs=pl.BlockSpec(memory_space=pltpu.VMEM),
-        out_shape=jax.ShapeDtypeStruct((PARTS, 128, 2 * PIECE), jnp.bfloat16),
+        out_shape=jax.ShapeDtypeStruct((len(numbers), 128, 2 * PIECE), jnp.bfloat16),
         scratch_shapes=[
             pltpu.VMEM((6 * 64, width), jnp.bfloat16),
             pltpu.SemaphoreType.DMA((6,)),
@@ -172,7 +174,8 @@
     y, c = lax.axis_index("y"), lax.axis_index("c")
     me = (2 * y + c).reshape(1).astype(jnp.int32)
     z_count = lax.axis_size("z")
-    z_pairs = [(n, (n + 1) % z_count) for n in range(z_count)]
+    z_up = [(n, (n + 1) % z_count) for n in range(z_count)]
+    z_down = [((n + 1) % z_count, n) for n in range(z_count)]
     live = jnp.arange(128, dtype=jnp.int32)[None, None] < pair_count[:, None, None]
     first = 128 + pair_list[:, 0:1]
     second = pair_list[:, 1:2]
@@ -182,26 +185,35 @@
     rows = rows.reshape(1, 256)
     spectra, rows = lax.optimization_barrier((spectra, rows))
     near = [rows] + [lax.ppermute(rows, ("y", "c"), yc_pairs[m]) for m in (1, 2, 3)]
+    near = jnp.concatenate(near)
+    above = lax.ppermute(lax.dynamic_slice_in_dim(near, me[0], 1, 0), "z", z_down)
+    is_first = (jnp.arange(256) < 128)[None]
+    above = jnp.where(is_first | (above < 64), above, -1)
     column = jnp.arange(192, dtype=jnp.int32)
-    picks = (jnp.concatenate(near)[:, :, None] == column).astype(jnp.bfloat16)
+    picks = (jnp.concatenate([near, above])[:, :, None] == column).astype(jnp.bfloat16)
 
     arrived = []
     for chunk in range(CHUNKS):
         pieces = whiten(me, spectra, chunk)
         if chunk == 0:
-            pieces, picks = lax.optimization_barrier((pieces, picks))
+            pieces, near = lax.optimization_barrier((pieces, near))
         arrived.append(
             [pieces[0]] + [lax.ppermute(pieces[m], ("y", "c"), yc_pairs[m]) for m in (2, 3, 1)]
         )
-    moved, behind = [], []
+    crossed, moved = [], []
     for own, far, cross, side in arrived:
-        ahead = [jnp.where(y == 1, own, far), jnp.where(y == 1, side, cross)]
-        moved.append(jnp.stack(ahead))
-        behind.append(lax.ppermute(moved[-1], "z", z_pairs))
+        blocks = [own, side, far, cross]
+        top = jnp.where(y == 1, jnp.where(c == 1, own, side), jnp.where(c == 1, far, cross))
+        low = jnp.where(y == 0, jnp.where(c == 0, own, side), jnp.where(c == 0, far, cross))
+        moved.append(top)
+        crossed.append(blocks + [lax.ppermute(top, "z", z_up), lax.ppermute(low, "z", z_down)])
     got = []
     for chunk in range(CHUNKS):
-        own, far, cross, side = arrived[chunk]
-        product = pair_products(me, picks, [own, side, far, cross, behind[chunk]])
+        other = pair_products((PARTS,), me, picks, crossed[chunk])
+        below = lax.ppermute(other, "z", z_up)
+        picks, other = lax.optimization_barrier((picks, other))
+        product = pair_products(tuple(range(PARTS)), me, picks, crossed[chunk])
+        product = product + jnp.pad(below, ((0, PARTS - 1), (0, 0), (0, 0)))
         product = product.reshape(PARTS * 128, 2 * PIECE)
         if chunk == 0:
             product, _ = lax.optimization_barrier((product, moved[1]))

time: 104 us -> 99.9 us (0.961)
  waiting for transfers between devices: 36.8 us -> 19.1 us
  starting transfers between devices: 17.4 us -> 30.1 us
  Pallas kernels: 20.8 us -> 26.3 us
  local copies, waits for them, and re-layouts: 6.41 us -> 1.65 us
  blocking collectives: 19.5 us -> 16.5 us
  other arithmetic: 2.29 us -> 4.87 us
    ppermute x6, waiting for transfers between devices: 25.2 us -> 6.18 us  [on_device(): lax.ppermute(pieces[m], ('y', 'c'), yc_pairs[m])]
    ppermute x2 -> x7, starting transfers between devices: 0.09 us -> 13 us  [the longest x2 4.62 us: on_device(): lax.ppermute(low, 'z', z_down)]
    pallas_call x2 -> x4, Pallas kernels: 6.85 us -> 12.3 us  [pair_products(): pl.pallas_call(functools.partial(pair_kernel, numbers), in_specs=[pl.Bloc...]
    unnamed x27 -> x11, local copies, waits for them, and re-layouts: 6.41 us -> 1.62 us
    all_to_all x1, waiting for transfers between devices: 0.01 us -> 3.35 us  [on_device(): lax.all_to_all(product, ('y', 'c', 'h'), 0, 0, tiled=True)]
    all_to_all x1, blocking collectives: 19.5 us -> 16.5 us  [on_device(): lax.all_to_all(product, ('y', 'c', 'h'), 0, 0, tiled=True)]
    select_n x0 -> x3, other arithmetic: none -> 2.96 us  [the longest x2 2.96 us: on_device(): jnp.where(y == 0, jnp.where(c == 0, own, side), jnp.where(c == 0, far, cr...]
    ppermute x3, starting transfers between devices: 2.19 us -> 5.06 us  [on_device(): lax.ppermute(rows, ('y', 'c'), yc_pairs[m])]
  transfers between devices with their start and end apart: 12 -> 17, of which waited for: 5 -> 4; matrix products, arithmetic and copies ran while one was open for 1% -> 4% of each run, Pallas kernels for 13% -> 25%
where the time goes in v3:
time: 99.9 us; the launch traced here: 99.4 us
  starting transfers between devices  30.1 us (30%)
  Pallas kernels  26.3 us (26%)
  waiting for transfers between devices  19.1 us (19%)
  blocking collectives  16.5 us (17%)
  other arithmetic  4.87 us (5%)
  local copies, waits for them, and re-layouts  1.65 us (2%)
    all_to_all x1, blocking collectives, on_device(): lax.all_to_all(product, ('y', 'c', 'h'), 0, 0, tiled=True)  16.5 us
    pallas_call x2, Pallas kernels, whiten(): pl.pallas_call(whiten_kernel, grid_spec=pltpu.PrefetchScalarGridSpec(num_...  12.6 us
    pallas_call x4, Pallas kernels, pair_products(): pl.pallas_call(functools.partial(pair_kernel, numbers), in_specs=[pl.Bloc...  12.3 us
    ppermute x2, waiting for transfers between devices, on_device(): lax.ppermute(top, 'z', z_up)  9.56 us
    all_to_all x1, starting transfers between devices, on_device(): lax.all_to_all(product, ('y', 'c', 'h'), 0, 0, tiled=True)  7.91 us
    ppermute x6, waiting for transfers between devices, on_device(): lax.ppermute(pieces[m], ('y', 'c'), yc_pairs[m])  6.18 us
    ppermute x3, starting transfers between devices, on_device(): lax.ppermute(rows, ('y', 'c'), yc_pairs[m])  5.06 us
    ppermute x2, starting transfers between devices, on_device(): lax.ppermute(low, 'z', z_down)  4.62 us
  transfers between devices with their start and end apart: 17, of which 4 were waited for; matrix products, arithmetic and copies ran while one was open for 4% of the time, Pallas kernels for 25%

profile of v3, /device:TPU:1, one launch (start us, length us, event | category | flops | bytes accessed | tf_op | source)
XLA Modules:
  0.0 99.4 jit_solution(1558182457377295588)
XLA Ops:
  1.5 3.3 %collective-permute-start = (s32[1,256]{1,0:T(1,128)S(1)}, s32[1,256]{1,0:T(1,128)S(1)}, u32[]{:S(2)}, u32[]{:S(2)}) collective-permute-start(s32[1,256]{1,0:T(1,128)S(1)} %bitcast_select_fusion), channel_id=1, source_target_pairs={{0,8},{8,0},{16,24},{24,16},{1,9},{9,1},{17,25},{25,17},{2,10},{10... | collective-permute-start | bytes 3080 | tf_op jit(solution)/shard_map/ppermute | solution.py:187
  4.8 1.7 %collective-permute-start.2 = (s32[1,256]{1,0:T(1,128)S(1)}, s32[1,256]{1,0:T(1,128)S(1)}, u32[]{:S(2)}, u32[]{:S(2)}) collective-permute-start(s32[1,256]{1,0:T(1,128)S(1)} %bitcast_select_fusion), channel_id=1, source_target_pairs={{0,24},{8,16},{16,8},{24,0},{1,25},{9,17},{17,9},{25,1},{2,26},{10... | collective-permute-start | bytes 3080 | tf_op jit(solution)/shard_map/ppermute | solution.py:187
  6.5 6.3 %whiten.2 = (bf16[64,3072]{1,0:T(8,128)(2,1)}, bf16[64,3072]{1,0:T(8,128)(2,1)}, bf16[64,3072]{1,0:T(8,128)(2,1)}, bf16[64,3072]{1,0:T(8,128)(2,1)}) custom-call(s32[1]{0:T(128)} %bitcast.me_ref, bf16[64,6,2,2048]{3,2,1,0:T(2,128)(2,1)} %x_ref.1), custom_call_target="tpu_custom_call" | custom-call | tf_op jit(solution)/shard_map/whiten/pallas_call | solution.py:52
  13.1 2.0 %collective-permute-start.6 = (bf16[64,3072]{1,0:T(8,128)(2,1)}, bf16[64,3072]{1,0:T(8,128)(2,1)S(1)}, u32[]{:S(2)}, u32[]{:S(2)}) collective-permute-start(bf16[64,3072]{1,0:T(8,128)(2,1)} %get-tuple-element.31), channel_id=1, source_target_pairs={{0,24},{8,16},{16,8},{24,0},{1,25},{9,17},{17,9},{25,1},{2,26},{10... | collective-permute-start | bytes 1179656 | tf_op jit(solution)/shard_map/ppermute | solution.py:201
  15.1 6.3 %whiten.3 = (bf16[64,3072]{1,0:T(8,128)(2,1)}, bf16[64,3072]{1,0:T(8,128)(2,1)}, bf16[64,3072]{1,0:T(8,128)(2,1)}, bf16[64,3072]{1,0:T(8,128)(2,1)}) custom-call(s32[1]{0:T(128)} %bitcast.me_ref, bf16[64,6,2,2048]{3,2,1,0:T(2,128)(2,1)} %x_ref.1), custom_call_target="tpu_custom_call" | custom-call | tf_op jit(solution)/shard_map/whiten/pallas_call | solution.py:52
  21.4 1.5 %collective-permute-start.12 = (bf16[64,3072]{1,0:T(8,128)(2,1)}, bf16[64,3072]{1,0:T(8,128)(2,1)S(1)}, u32[]{:S(2)}, u32[]{:S(2)}) collective-permute-start(bf16[64,3072]{1,0:T(8,128)(2,1)} %get-tuple-element.36), channel_id=1, source_target_pairs={{0,24},{8,16},{16,8},{24,0},{1,25},{9,17},{17,9},{25,1},{2,26},{10... | collective-permute-start | bytes 1179656 | tf_op jit(solution)/shard_map/ppermute | solution.py:201
  23.7 3.8 %collective-permute-start.3 = (s32[1,256]{1,0:T(1,128)S(1)}, s32[1,256]{1,0:T(1,128)S(1)}, u32[]{:S(2)}, u32[]{:S(2)}) collective-permute-start(s32[1,256]{1,0:T(1,128)S(1)} %constant_dynamic-slice_fusion), channel_id=1, source_target_pairs={{32,0},{64,32},{96,64},{128,96},{160,128},{192,160},{224,192},{0,2... | collective-permute-start | bytes 3080 | tf_op jit(solution)/shard_map/ppermute | solution.py:189
  27.5 5.9 %collective-permute-done.6.refs_3_ = bf16[64,3072]{1,0:T(8,128)(2,1)S(1)} collective-permute-done((bf16[64,3072]{1,0:T(8,128)(2,1)}, bf16[64,3072]{1,0:T(8,128)(2,1)S(1)}, u32[]{:S(2)}, u32[]{:S(2)}) %collective-permute-start.6) | collective-permute-done | bytes 393248 | tf_op jit(solution)/shard_map/ppermute | solution.py:201
  33.4 1.0 select_select_fusion.2
  34.4 3.9 %collective-permute-start.8 = (bf16[64,3072]{1,0:T(8,128)(2,1)}, bf16[64,3072]{1,0:T(8,128)(2,1)}, u32[]{:S(2)}, u32[]{:S(2)}) collective-permute-start(bf16[64,3072]{1,0:T(8,128)(2,1)} %get-tuple-element.41), channel_id=1, source_target_pairs={{32,0},{64,32},{96,64},{128,96},{160,128},{192,160},{224,192},{0,2... | collective-permute-start | bytes 1179656 | tf_op jit(solution)/shard_map/ppermute | solution.py:209
  38.5 9.6 %collective-permute-done.7.refs_4_ = bf16[64,3072]{1,0:T(8,128)(2,1)} collective-permute-done((bf16[64,3072]{1,0:T(8,128)(2,1)}, bf16[64,3072]{1,0:T(8,128)(2,1)}, u32[]{:S(2)}, u32[]{:S(2)}) %collective-permute-start.7) | collective-permute-done | bytes 393248 | tf_op jit(solution)/shard_map/ppermute | solution.py:209
  48.1 2.5 %pair_products.4 = bf16[1,128,512]{2,1,0:T(8,128)(2,1)S(1)} custom-call(s32[1]{0:T(128)} %bitcast.me_ref, bf16[5,256,192]{2,1,0:T(8,128)(2,1)S(1)} %fusion.pick_ref, bf16[64,3072]{1,0:T(8,128)(2,1)S(1)} %copy-done.1, bf16[64,3072]{1,0:T(8,128)(2,1)S(1)} %collective-permute-done.4.refs_1_, bf16[64,3072]{1,0:T(8,128)(2,1)S(1)} %collective-permute-done.5.refs_2_, ...), custom_call_target="tpu_custom_call" | custom-call | tf_op jit(solution)/shard_map/pair_products/pallas_call | solution.py:100
  50.8 2.0 %select_select_fusion = (bf16[64,3072]{1,0:T(8,128)(2,1)}, bf16[64,3072]{1,0:T(8,128)(2,1)}) fusion(bf16[64,3072]{1,0:T(8,128)(2,1)S(1)} %collective-permute-done.11.refs_2_, bf16[64,3072]{1,0:T(8,128)(2,1)S(1)} %collective-permute-done.12.refs_3_, bf16[64,3072]{1,0:T(8,128)(2,1)S(1)} %copy-done, bf16[64,3072]{1,0:T(8,128)(2,1)} %collective-permute-done.10.refs_1_, ...), kind=kLoop, calls=%fused_computation.4 | loop fusion | flops 1179648 | bytes 2359300 | tf_op jit(solution)/shard_map/jit(_where)/select_n | solution.py:207
  52.7 2.0 %collective-permute-start.13 = (bf16[64,3072]{1,0:T(8,128)(2,1)}, bf16[64,3072]{1,0:T(8,128)(2,1)}, u32[]{:S(2)}, u32[]{:S(2)}) collective-permute-start(bf16[64,3072]{1,0:T(8,128)(2,1)} %get-tuple-element.40), channel_id=1, source_target_pairs={{0,32},{32,64},{64,96},{96,128},{128,160},{160,192},{192,224},{224... | collective-permute-start | bytes 1179656 | tf_op jit(solution)/shard_map/ppermute | solution.py:209
  55.4 3.8 %pair_products.5 = bf16[4,128,512]{2,1,0:T(8,128)(2,1)S(1)} custom-call(s32[1]{0:T(128)} %bitcast.me_ref, bf16[5,256,192]{2,1,0:T(8,128)(2,1)S(1)} %fusion.pick_ref, bf16[64,3072]{1,0:T(8,128)(2,1)S(1)} %copy-done.1, bf16[64,3072]{1,0:T(8,128)(2,1)S(1)} %collective-permute-done.4.refs_1_, bf16[64,3072]{1,0:T(8,128)(2,1)S(1)} %collective-permute-done.5.refs_2_, ...), custom_call_target="tpu_custom_call" | custom-call | tf_op jit(solution)/shard_map/pair_products/pallas_call | solution.py:100
  59.3 0.8 pad_add_fusion.1
  60.1 7.9 %all-to-all-start = ((bf16[32,16,512]{2,1,0:T(8,128)(2,1)}), bf16[32,16,512]{2,1,0:T(8,128)(2,1)S(1)}, u32[]{:S(2)}, u32[]{:S(2)}) async-start(bf16[32,16,512]{2,1,0:T(8,128)(2,1)} %bitcast.4), calls=%async_computation | async-start | bytes 1048576 | tf_op jit(solution)/shard_map/all_to_all | solution.py:220
  68.0 2.4 %pair_products.6 = bf16[1,128,512]{2,1,0:T(8,128)(2,1)S(1)} custom-call(s32[1]{0:T(128)} %bitcast.me_ref, bf16[5,256,192]{2,1,0:T(8,128)(2,1)S(1)} %fusion.pick_ref, bf16[64,3072]{1,0:T(8,128)(2,1)S(1)} %copy-done, bf16[64,3072]{1,0:T(8,128)(2,1)} %collective-permute-done.10.refs_1_, bf16[64,3072]{1,0:T(8,128)(2,1)S(1)} %collective-permute-done.11.refs_2_, ...), custom_call_target="tpu_custom_call" | custom-call | tf_op jit(solution)/shard_map/pair_products/pallas_call | solution.py:100
  70.4 2.4 %collective-permute-start.15 = (bf16[1,128,512]{2,1,0:T(8,128)(2,1)S(1)}, bf16[1,128,512]{2,1,0:T(8,128)(2,1)S(1)}, u32[]{:S(2)}, u32[]{:S(2)}) collective-permute-start(bf16[1,128,512]{2,1,0:T(8,128)(2,1)S(1)} %pair_products.6), channel_id=1, source_target_pairs={{0,32},{32,64},{64,96},{96,128},{128,160},{160,192},{192,224},{224... | collective-permute-start | bytes 393224 | tf_op jit(solution)/shard_map/ppermute | solution.py:213
  72.9 3.7 %pair_products.7 = bf16[4,128,512]{2,1,0:T(8,128)(2,1)S(1)} custom-call(s32[1]{0:T(128)} %bitcast.me_ref, bf16[5,256,192]{2,1,0:T(8,128)(2,1)S(1)} %fusion.pick_ref, bf16[64,3072]{1,0:T(8,128)(2,1)S(1)} %copy-done, bf16[64,3072]{1,0:T(8,128)(2,1)} %collective-permute-done.10.refs_1_, bf16[64,3072]{1,0:T(8,128)(2,1)S(1)} %collective-permute-done.11.refs_2_, ...), custom_call_target="tpu_custom_call" | custom-call | tf_op jit(solution)/shard_map/pair_products/pallas_call | solution.py:100
  76.6 3.3 %all-to-all-done.refs_0_ = bf16[32,16,512]{2,1,0:T(8,128)(2,1)S(1)} async-done(((bf16[32,16,512]{2,1,0:T(8,128)(2,1)}), bf16[32,16,512]{2,1,0:T(8,128)(2,1)S(1)}, u32[]{:S(2)}, u32[]{:S(2)}) %all-to-all-start) | async-done | bytes 524320 | tf_op jit(solution)/shard_map/all_to_all | solution.py:220
  80.0 16.5 %all_to_all.18.refs_1_ = bf16[32,16,512]{2,1,0:T(8,128)(2,1)S(1)} all-to-all(bf16[32,16,512]{2,1,0:T(8,128)(2,1)S(1)} %bitcast.12), channel_id=1, replica_groups=mesh['z'=8,'y'=2,'c'=2,'h'=8] {'y','c','h'}, dimensions={0} | all-to-all | bytes 1048576 | tf_op jit(solution)/shard_map/all_to_all | solution.py:220
  96.4 1.6 %copy-done.2 = bf16[4096,256]{1,0:T(8,128)(2,1)S(1)} copy-done((bf16[4096,256]{1,0:T(8,128)(2,1)S(1)}, bf16[4096,256]{1,0:T(8,128)(2,1)}, u32[]{:S(2)}) %copy-start.2) | copy-done | bytes 2097176
  98.0 1.4 %lag_sums.1 = f32[16,2432]{1,0:T(8,128)} custom-call(f32[10,2048]{1,0:T(8,128)S(1)} %copy-done.3, f32[10,2048]{1,0:T(8,128)S(1)} %copy-done.4, bf16[4096,256]{1,0:T(8,128)(2,1)S(1)} %copy-done.2, bf16[32,16,512]{2,1,0:T(8,128)(2,1)S(1)} %all-to-all-done.refs_0_, bf16[32,16,512]{2,1,0:T(8,128)(2,1)S(1)} %all_to_all.18.refs_1_), custom_call_target="tpu_custom_call" | custom-call | tf_op jit(solution)/shard_map/lag_sums/pallas_call | solution.py:147
  (42 shorter events, 3.0 us)
Async XLA Ops:
  1.5 11.4 %collective-permute-start = (s32[1,256]{1,0:T(1,128)S(1)}, s32[1,256]{1,0:T(1,128)S(1)}, u32[]{:S(2)}, u32[]{:S(2)}) collective-permute-start(s32[1,256]{1,0:T(1,128)S(1)} %bitcast_select_fusion), channel_id=1, source_target_pairs={{0,8},{8,0},{16,24},{24,16},{1,9},{9,1},{17,25},{25,17},{2,10},{10... | collective-permute-start | bytes 3080 | tf_op jit(solution)/shard_map/ppermute | solution.py:187
  4.8 8.0 %collective-permute-start.1 = (s32[1,256]{1,0:T(1,128)S(1)}, s32[1,256]{1,0:T(1,128)S(1)}, u32[]{:S(2)}, u32[]{:S(2)}) collective-permute-start(s32[1,256]{1,0:T(1,128)S(1)} %bitcast_select_fusion), channel_id=1, source_target_pairs={{0,16},{8,24},{16,0},{24,8},{1,17},{9,25},{17,1},{25,9},{2,18},{10... | collective-permute-start | bytes 3080 | tf_op jit(solution)/shard_map/ppermute | solution.py:187
  4.8 8.1 %collective-permute-start.2 = (s32[1,256]{1,0:T(1,128)S(1)}, s32[1,256]{1,0:T(1,128)S(1)}, u32[]{:S(2)}, u32[]{:S(2)}) collective-permute-start(s32[1,256]{1,0:T(1,128)S(1)} %bitcast_select_fusion), channel_id=1, source_target_pairs={{0,24},{8,16},{16,8},{24,0},{1,25},{9,17},{17,9},{25,1},{2,26},{10... | collective-permute-start | bytes 3080 | tf_op jit(solution)/shard_map/ppermute | solution.py:187
  12.8 20.6 %copy-start.1 = (bf16[64,3072]{1,0:T(8,128)(2,1)S(1)}, bf16[64,3072]{1,0:T(8,128)(2,1)}, u32[]{:S(2)}) copy-start(bf16[64,3072]{1,0:T(8,128)(2,1)} %get-tuple-element.28.refs_0_) | copy-start | bytes 1179652
  12.9 10.1 %collective-permute-start.4 = (bf16[64,3072]{1,0:T(8,128)(2,1)}, bf16[64,3072]{1,0:T(8,128)(2,1)S(1)}, u32[]{:S(2)}, u32[]{:S(2)}) collective-permute-start(bf16[64,3072]{1,0:T(8,128)(2,1)} %get-tuple-element.29), channel_id=1, source_target_pairs={{0,8},{8,0},{16,24},{24,16},{1,9},{9,1},{17,25},{25,17},{2,10},{10... | collective-permute-start | bytes 1179656 | tf_op jit(solution)/shard_map/ppermute | solution.py:201
  13.1 10.6 %collective-permute-start.5 = (bf16[64,3072]{1,0:T(8,128)(2,1)}, bf16[64,3072]{1,0:T(8,128)(2,1)S(1)}, u32[]{:S(2)}, u32[]{:S(2)}) collective-permute-start(bf16[64,3072]{1,0:T(8,128)(2,1)} %get-tuple-element.30), channel_id=1, source_target_pairs={{0,16},{8,24},{16,0},{24,8},{1,17},{9,25},{17,1},{25,9},{2,18},{10... | collective-permute-start | bytes 1179656 | tf_op jit(solution)/shard_map/ppermute | solution.py:201
  13.1 20.2 %collective-permute-start.6 = (bf16[64,3072]{1,0:T(8,128)(2,1)}, bf16[64,3072]{1,0:T(8,128)(2,1)S(1)}, u32[]{:S(2)}, u32[]{:S(2)}) collective-permute-start(bf16[64,3072]{1,0:T(8,128)(2,1)} %get-tuple-element.31), channel_id=1, source_target_pairs={{0,24},{8,16},{16,8},{24,0},{1,25},{9,17},{17,9},{25,1},{2,26},{10... | collective-permute-start | bytes 1179656 | tf_op jit(solution)/shard_map/ppermute | solution.py:201
  21.4 29.3 %collective-permute-start.11 = (bf16[64,3072]{1,0:T(8,128)(2,1)}, bf16[64,3072]{1,0:T(8,128)(2,1)S(1)}, u32[]{:S(2)}, u32[]{:S(2)}) collective-permute-start(bf16[64,3072]{1,0:T(8,128)(2,1)} %get-tuple-element.35), channel_id=1, source_target_pairs={{0,16},{8,24},{16,0},{24,8},{1,17},{9,25},{17,1},{25,9},{2,18},{10... | collective-permute-start | bytes 1179656 | tf_op jit(solution)/shard_map/ppermute | solution.py:201
  21.4 29.3 %collective-permute-start.12 = (bf16[64,3072]{1,0:T(8,128)(2,1)}, bf16[64,3072]{1,0:T(8,128)(2,1)S(1)}, u32[]{:S(2)}, u32[]{:S(2)}) collective-permute-start(bf16[64,3072]{1,0:T(8,128)(2,1)} %get-tuple-element.36), channel_id=1, source_target_pairs={{0,24},{8,16},{16,8},{24,0},{1,25},{9,17},{17,9},{25,1},{2,26},{10... | collective-permute-start | bytes 1179656 | tf_op jit(solution)/shard_map/ppermute | solution.py:201
  22.9 27.8 %collective-permute-start.10 = (bf16[64,3072]{1,0:T(8,128)(2,1)}, bf16[64,3072]{1,0:T(8,128)(2,1)}, u32[]{:S(2)}, u32[]{:S(2)}) collective-permute-start(bf16[64,3072]{1,0:T(8,128)(2,1)} %get-tuple-element.34), channel_id=1, source_target_pairs={{0,8},{8,0},{16,24},{24,16},{1,9},{9,1},{17,25},{25,17},{2,10},{10... | collective-permute-start | bytes 1179656 | tf_op jit(solution)/shard_map/ppermute | solution.py:201
  23.7 10.7 %collective-permute-start.3 = (s32[1,256]{1,0:T(1,128)S(1)}, s32[1,256]{1,0:T(1,128)S(1)}, u32[]{:S(2)}, u32[]{:S(2)}) collective-permute-start(s32[1,256]{1,0:T(1,128)S(1)} %constant_dynamic-slice_fusion), channel_id=1, source_target_pairs={{32,0},{64,32},{96,64},{128,96},{160,128},{192,160},{224,192},{0,2... | collective-permute-start | bytes 3080 | tf_op jit(solution)/shard_map/ppermute | solution.py:189
  34.3 16.4 %copy-start = (bf16[64,3072]{1,0:T(8,128)(2,1)S(1)}, bf16[64,3072]{1,0:T(8,128)(2,1)}, u32[]{:S(2)}) copy-start(bf16[64,3072]{1,0:T(8,128)(2,1)} %get-tuple-element.33.refs_0_) | copy-start | bytes 1179652
  34.3 13.8 %collective-permute-start.7 = (bf16[64,3072]{1,0:T(8,128)(2,1)}, bf16[64,3072]{1,0:T(8,128)(2,1)}, u32[]{:S(2)}, u32[]{:S(2)}) collective-permute-start(bf16[64,3072]{1,0:T(8,128)(2,1)} %get-tuple-element.42), channel_id=1, source_target_pairs={{0,32},{32,64},{64,96},{96,128},{128,160},{160,192},{192,224},{224... | collective-permute-start | bytes 1179656 | tf_op jit(solution)/shard_map/ppermute | solution.py:209
  34.4 13.7 %collective-permute-start.8 = (bf16[64,3072]{1,0:T(8,128)(2,1)}, bf16[64,3072]{1,0:T(8,128)(2,1)}, u32[]{:S(2)}, u32[]{:S(2)}) collective-permute-start(bf16[64,3072]{1,0:T(8,128)(2,1)} %get-tuple-element.41), channel_id=1, source_target_pairs={{32,0},{64,32},{96,64},{128,96},{160,128},{192,160},{224,192},{0,2... | collective-permute-start | bytes 1179656 | tf_op jit(solution)/shard_map/ppermute | solution.py:209
  50.6 8.6 %collective-permute-start.9 = (bf16[1,128,512]{2,1,0:T(8,128)(2,1)S(1)}, bf16[1,128,512]{2,1,0:T(8,128)(2,1)S(1)}, u32[]{:S(2)}, u32[]{:S(2)}) collective-permute-start(bf16[1,128,512]{2,1,0:T(8,128)(2,1)S(1)} %pair_products.4), channel_id=1, source_target_pairs={{0,32},{32,64},{64,96},{96,128},{128,160},{160,192},{192,224},{224... | collective-permute-start | bytes 393224 | tf_op jit(solution)/shard_map/ppermute | solution.py:213
  52.7 15.3 %collective-permute-start.13 = (bf16[64,3072]{1,0:T(8,128)(2,1)}, bf16[64,3072]{1,0:T(8,128)(2,1)}, u32[]{:S(2)}, u32[]{:S(2)}) collective-permute-start(bf16[64,3072]{1,0:T(8,128)(2,1)} %get-tuple-element.40), channel_id=1, source_target_pairs={{0,32},{32,64},{64,96},{96,128},{128,160},{160,192},{192,224},{224... | collective-permute-start | bytes 1179656 | tf_op jit(solution)/shard_map/ppermute | solution.py:209
  54.7 13.3 %collective-permute-start.14 = (bf16[64,3072]{1,0:T(8,128)(2,1)}, bf16[64,3072]{1,0:T(8,128)(2,1)}, u32[]{:S(2)}, u32[]{:S(2)}) collective-permute-start(bf16[64,3072]{1,0:T(8,128)(2,1)} %get-tuple-element.39), channel_id=1, source_target_pairs={{32,0},{64,32},{96,64},{128,96},{160,128},{192,160},{224,192},{0,2... | collective-permute-start | bytes 1179656 | tf_op jit(solution)/shard_map/ppermute | solution.py:209
  60.1 19.9 %all-to-all-start = ((bf16[32,16,512]{2,1,0:T(8,128)(2,1)}), bf16[32,16,512]{2,1,0:T(8,128)(2,1)S(1)}, u32[]{:S(2)}, u32[]{:S(2)}) async-start(bf16[32,16,512]{2,1,0:T(8,128)(2,1)} %bitcast.4), calls=%async_computation | async-start | bytes 1048576 | tf_op jit(solution)/shard_map/all_to_all | solution.py:220
  70.4 26.0 %copy-start.3 = (f32[10,2048]{1,0:T(8,128)S(1)}, f32[10,2048]{1,0:T(8,128)}, u32[]{:S(2)}) copy-start(f32[10,2048]{1,0:T(8,128)} %constant.36.clone.cos_ref) | copy-start | bytes 245764
  70.4 26.0 %copy-start.4 = (f32[10,2048]{1,0:T(8,128)S(1)}, f32[10,2048]{1,0:T(8,128)}, u32[]{:S(2)}) copy-start(f32[10,2048]{1,0:T(8,128)} %constant.37.clone.sin_ref) | copy-start | bytes 245764
  70.4 6.1 %collective-permute-start.15 = (bf16[1,128,512]{2,1,0:T(8,128)(2,1)S(1)}, bf16[1,128,512]{2,1,0:T(8,128)(2,1)S(1)}, u32[]{:S(2)}, u32[]{:S(2)}) collective-permute-start(bf16[1,128,512]{2,1,0:T(8,128)(2,1)S(1)} %pair_products.6), channel_id=1, source_target_pairs={{0,32},{32,64},{64,96},{96,128},{128,160},{160,192},{192,224},{224... | collective-permute-start | bytes 393224 | tf_op jit(solution)/shard_map/ppermute | solution.py:213
  96.4 1.6 %copy-start.2 = (bf16[4096,256]{1,0:T(8,128)(2,1)S(1)}, bf16[4096,256]{1,0:T(8,128)(2,1)}, u32[]{:S(2)}) copy-start(bf16[4096,256]{1,0:T(8,128)(2,1)} %constant.38.clone.table_ref) | copy-start | bytes 6291460

commit v4 on v3

--- a/solution.py
+++ b/solution.py
@@ -24,7 +24,7 @@
 PIECE = WIDE // PARTS
 BANDS = PIECE // BAND
 ROWS = 16
-SPAN = 256
+SPAN = 128
 TURNS = -(-LAGS // SPAN)
 
 
@@ -66,13 +66,18 @@
     *sources, out_ref, held, sems = refs
     me = me_ref[0]
     places = [1 + (me ^ m) for m in range(PARTS)] + [0, 5]
+    needed = {place for j in numbers for place in range(max(j - 1, 0), j + 2)}
+    if numbers == (PARTS,):
+        needed.remove(PARTS)
     copies = []
     for n, (source, place) in enumerate(zip(sources, places)):
+        wanted = functools.reduce(lambda a, b: a | b, [jnp.equal(place, p) for p in sorted(needed)])
         start = pl.multiple_of(place * 64, 64)
-        copies.append(pltpu.make_async_copy(source, held.at[pl.ds(start, 64)], sems.at[n]))
-        copies[-1].start()
-    for copy in copies:
-        copy.wait()
+        copies.append((wanted, pltpu.make_async_copy(source, held.at[pl.ds(start, 64)], sems.at[n])))
+    for wanted, copy in copies:
+        pl.when(wanted)(copy.start)
+    for wanted, copy in copies:
+        pl.when(wanted)(copy.wait)
     for n, j in enumerate(numbers):
         if j == 0:
             pick, rows = pick_ref[me, :, 64:], slice(0, 128)
@@ -82,11 +87,16 @@
         cross_re = jnp.zeros((128, PIECE), jnp.float32)
         cross_im = jnp.zeros((128, PIECE), jnp.float32)
         for s in range(SEGS):
-            taken = jnp.dot(
-                pick,
-                held[rows, 2 * s * PIECE : 2 * (s + 1) * PIECE],
-                preferred_element_type=jnp.float32,
-            )
+            lanes = slice(2 * s * PIECE, 2 * (s + 1) * PIECE)
+            if j < PARTS:
+                taken = jnp.dot(pick, held[rows, lanes], preferred_element_type=jnp.float32)
+            else:
+                taken = jnp.concatenate(
+                    [
+                        jnp.dot(pick[:128, 128:], held[320:384, lanes], preferred_element_type=jnp.float32),
+                        jnp.dot(pick[128:, :64], held[192:256, lanes], preferred_element_type=jnp.float32),
+                    ]
+                )
             a_re, a_im = taken[:128, :PIECE], taken[:128, PIECE:]
             b_re, b_im = taken[128:, :PIECE], taken[128:, PIECE:]
             cross_re += a_re * b_re + a_im * b_im

time: 99.9 us -> 97.1 us (0.972)
  local copies, waits for them, and re-layouts: 1.65 us -> 0.06 us
  Pallas kernels: 26.3 us -> 25.1 us
    unnamed x11, local copies, waits for them, and re-layouts: 1.62 us -> 0.03 us
    pallas_call x4, Pallas kernels: 12.3 us -> 10.9 us  [pair_products(): pl.pallas_call(functools.partial(pair_kernel, numbers), in_specs=[pl.Bloc...]
  transfers between devices with their start and end apart: 17 -> 17, of which waited for: 4 -> 5; matrix products, arithmetic and copies ran while one was open for 4% -> 4% of each run, Pallas kernels for 25% -> 24%
where the time goes in v4:
time: 97.1 us; the launch traced here: 96.6 us
  starting transfers between devices  30 us (31%)
  Pallas kernels  25.1 us (26%)
  waiting for transfers between devices  19.8 us (20%)
  blocking collectives  15.9 us (16%)
  other arithmetic  4.87 us (5%)
    all_to_all x1, blocking collectives, on_device(): lax.all_to_all(product, ('y', 'c', 'h'), 0, 0, tiled=True)  15.9 us
    pallas_call x2, Pallas kernels, whiten(): pl.pallas_call(whiten_kernel, grid_spec=pltpu.PrefetchScalarGridSpec(num_...  12.6 us
    pallas_call x4, Pallas kernels, pair_products(): pl.pallas_call(functools.partial(pair_kernel, numbers), in_specs=[pl.Bloc...  10.9 us
    ppermute x2, waiting for transfers between devices, on_device(): lax.ppermute(top, 'z', z_up)  9.62 us
    all_to_all x1, starting transfers between devices, on_device(): lax.all_to_all(product, ('y', 'c', 'h'), 0, 0, tiled=True)  7.28 us
    ppermute x6, waiting for transfers between devices, on_device(): lax.ppermute(pieces[m], ('y', 'c'), yc_pairs[m])  6.18 us
    ppermute x2, starting transfers between devices, on_device(): lax.ppermute(low, 'z', z_down)  5.12 us
    ppermute x3, starting transfers between devices, on_device(): lax.ppermute(rows, ('y', 'c'), yc_pairs[m])  5.06 us
  transfers between devices with their start and end apart: 17, of which 5 were waited for; matrix products, arithmetic and copies ran while one was open for 4% of the time, Pallas kernels for 24%

profile of v4, /device:TPU:1, one launch (start us, length us, event | category | flops | bytes accessed | tf_op | source)
XLA Modules:
  0.0 96.6 jit_solution(8685537240042694839)
XLA Ops:
  1.5 3.3 %collective-permute-start = (s32[1,256]{1,0:T(1,128)S(1)}, s32[1,256]{1,0:T(1,128)S(1)}, u32[]{:S(2)}, u32[]{:S(2)}) collective-permute-start(s32[1,256]{1,0:T(1,128)S(1)} %bitcast_select_fusion), channel_id=1, source_target_pairs={{0,8},{8,0},{16,24},{24,16},{1,9},{9,1},{17,25},{25,17},{2,10},{10... | collective-permute-start | bytes 3080 | tf_op jit(solution)/shard_map/ppermute | solution.py:197
  4.8 1.7 %collective-permute-start.2 = (s32[1,256]{1,0:T(1,128)S(1)}, s32[1,256]{1,0:T(1,128)S(1)}, u32[]{:S(2)}, u32[]{:S(2)}) collective-permute-start(s32[1,256]{1,0:T(1,128)S(1)} %bitcast_select_fusion), channel_id=1, source_target_pairs={{0,24},{8,16},{16,8},{24,0},{1,25},{9,17},{17,9},{25,1},{2,26},{10... | collective-permute-start | bytes 3080 | tf_op jit(solution)/shard_map/ppermute | solution.py:197
  6.5 6.3 %whiten.2 = (bf16[64,3072]{1,0:T(8,128)(2,1)}, bf16[64,3072]{1,0:T(8,128)(2,1)}, bf16[64,3072]{1,0:T(8,128)(2,1)}, bf16[64,3072]{1,0:T(8,128)(2,1)}) custom-call(s32[1]{0:T(128)} %bitcast.me_ref, bf16[64,6,2,2048]{3,2,1,0:T(2,128)(2,1)} %x_ref.1), custom_call_target="tpu_custom_call" | custom-call | tf_op jit(solution)/shard_map/whiten/pallas_call | solution.py:52
  13.1 2.0 %collective-permute-start.6 = (bf16[64,3072]{1,0:T(8,128)(2,1)}, bf16[64,3072]{1,0:T(8,128)(2,1)S(1)}, u32[]{:S(2)}, u32[]{:S(2)}) collective-permute-start(bf16[64,3072]{1,0:T(8,128)(2,1)} %get-tuple-element.31), channel_id=1, source_target_pairs={{0,24},{8,16},{16,8},{24,0},{1,25},{9,17},{17,9},{25,1},{2,26},{10... | collective-permute-start | bytes 1179656 | tf_op jit(solution)/shard_map/ppermute | solution.py:211
  15.1 6.3 %whiten.3 = (bf16[64,3072]{1,0:T(8,128)(2,1)}, bf16[64,3072]{1,0:T(8,128)(2,1)}, bf16[64,3072]{1,0:T(8,128)(2,1)}, bf16[64,3072]{1,0:T(8,128)(2,1)}) custom-call(s32[1]{0:T(128)} %bitcast.me_ref, bf16[64,6,2,2048]{3,2,1,0:T(2,128)(2,1)} %x_ref.1), custom_call_target="tpu_custom_call" | custom-call | tf_op jit(solution)/shard_map/whiten/pallas_call | solution.py:52
  21.4 1.5 %collective-permute-start.12 = (bf16[64,3072]{1,0:T(8,128)(2,1)}, bf16[64,3072]{1,0:T(8,128)(2,1)S(1)}, u32[]{:S(2)}, u32[]{:S(2)}) collective-permute-start(bf16[64,3072]{1,0:T(8,128)(2,1)} %get-tuple-element.36), channel_id=1, source_target_pairs={{0,24},{8,16},{16,8},{24,0},{1,25},{9,17},{17,9},{25,1},{2,26},{10... | collective-permute-start | bytes 1179656 | tf_op jit(solution)/shard_map/ppermute | solution.py:211
  23.7 3.8 %collective-permute-start.3 = (s32[1,256]{1,0:T(1,128)S(1)}, s32[1,256]{1,0:T(1,128)S(1)}, u32[]{:S(2)}, u32[]{:S(2)}) collective-permute-start(s32[1,256]{1,0:T(1,128)S(1)} %constant_dynamic-slice_fusion), channel_id=1, source_target_pairs={{32,0},{64,32},{96,64},{128,96},{160,128},{192,160},{224,192},{0,2... | collective-permute-start | bytes 3080 | tf_op jit(solution)/shard_map/ppermute | solution.py:199
  27.5 5.9 %collective-permute-done.6.refs_3_ = bf16[64,3072]{1,0:T(8,128)(2,1)S(1)} collective-permute-done((bf16[64,3072]{1,0:T(8,128)(2,1)}, bf16[64,3072]{1,0:T(8,128)(2,1)S(1)}, u32[]{:S(2)}, u32[]{:S(2)}) %collective-permute-start.6) | collective-permute-done | bytes 393248 | tf_op jit(solution)/shard_map/ppermute | solution.py:211
  33.4 1.0 %select_select_fusion.2 = (bf16[64,3072]{1,0:T(8,128)(2,1)}, bf16[64,3072]{1,0:T(8,128)(2,1)}) fusion(bf16[64,3072]{1,0:T(8,128)(2,1)S(1)} %collective-permute-done.5.refs_2_, bf16[64,3072]{1,0:T(8,128)(2,1)S(1)} %collective-permute-done.6.refs_3_, bf16[64,3072]{1,0:T(8,128)(2,1)S(1)} %copy-done.1, bf16[64,3072]{1,0:T(8,128)(2,1)S(1)} %collective-permute-done.4.refs_1_, ...), kind=kLoop, calls=%fused_computation.6 | loop fusion | flops 1179648 | bytes 2359300 | tf_op jit(solution)/shard_map/jit(_where)/select_n | solution.py:217
  34.4 3.8 %collective-permute-start.8 = (bf16[64,3072]{1,0:T(8,128)(2,1)}, bf16[64,3072]{1,0:T(8,128)(2,1)}, u32[]{:S(2)}, u32[]{:S(2)}) collective-permute-start(bf16[64,3072]{1,0:T(8,128)(2,1)} %get-tuple-element.41), channel_id=1, source_target_pairs={{32,0},{64,32},{96,64},{128,96},{160,128},{192,160},{224,192},{0,2... | collective-permute-start | bytes 1179656 | tf_op jit(solution)/shard_map/ppermute | solution.py:219
  38.5 9.6 %collective-permute-done.7.refs_4_ = bf16[64,3072]{1,0:T(8,128)(2,1)} collective-permute-done((bf16[64,3072]{1,0:T(8,128)(2,1)}, bf16[64,3072]{1,0:T(8,128)(2,1)}, u32[]{:S(2)}, u32[]{:S(2)}) %collective-permute-start.7) | collective-permute-done | bytes 393248 | tf_op jit(solution)/shard_map/ppermute | solution.py:219
  48.1 1.8 %pair_products.4 = bf16[1,128,512]{2,1,0:T(8,128)(2,1)S(1)} custom-call(s32[1]{0:T(128)} %bitcast.me_ref, bf16[5,256,192]{2,1,0:T(8,128)(2,1)S(1)} %fusion.pick_ref, bf16[64,3072]{1,0:T(8,128)(2,1)S(1)} %copy-done.1, bf16[64,3072]{1,0:T(8,128)(2,1)S(1)} %collective-permute-done.4.refs_1_, bf16[64,3072]{1,0:T(8,128)(2,1)S(1)} %collective-permute-done.5.refs_2_, ...), custom_call_target="tpu_custom_call" | custom-call | tf_op jit(solution)/shard_map/pair_products/pallas_call | solution.py:110
  50.0 2.0 %select_select_fusion = (bf16[64,3072]{1,0:T(8,128)(2,1)}, bf16[64,3072]{1,0:T(8,128)(2,1)}) fusion(bf16[64,3072]{1,0:T(8,128)(2,1)S(1)} %collective-permute-done.11.refs_2_, bf16[64,3072]{1,0:T(8,128)(2,1)S(1)} %collective-permute-done.12.refs_3_, bf16[64,3072]{1,0:T(8,128)(2,1)S(1)} %copy-done, bf16[64,3072]{1,0:T(8,128)(2,1)} %collective-permute-done.10.refs_1_, ...), kind=kLoop, calls=%fused_computation.4 | loop fusion | flops 1179648 | bytes 2359300 | tf_op jit(solution)/shard_map/jit(_where)/select_n | solution.py:217
  52.0 2.0 %collective-permute-start.13 = (bf16[64,3072]{1,0:T(8,128)(2,1)}, bf16[64,3072]{1,0:T(8,128)(2,1)}, u32[]{:S(2)}, u32[]{:S(2)}) collective-permute-start(bf16[64,3072]{1,0:T(8,128)(2,1)} %get-tuple-element.40), channel_id=1, source_target_pairs={{0,32},{32,64},{64,96},{96,128},{128,160},{160,192},{192,224},{224... | collective-permute-start | bytes 1179656 | tf_op jit(solution)/shard_map/ppermute | solution.py:219
  54.0 1.3 %collective-permute-start.14 = (bf16[64,3072]{1,0:T(8,128)(2,1)}, bf16[64,3072]{1,0:T(8,128)(2,1)}, u32[]{:S(2)}, u32[]{:S(2)}) collective-permute-start(bf16[64,3072]{1,0:T(8,128)(2,1)} %get-tuple-element.39), channel_id=1, source_target_pairs={{32,0},{64,32},{96,64},{128,96},{160,128},{192,160},{224,192},{0,2... | collective-permute-start | bytes 1179656 | tf_op jit(solution)/shard_map/ppermute | solution.py:219
  55.3 3.7 %pair_products.5 = bf16[4,128,512]{2,1,0:T(8,128)(2,1)S(1)} custom-call(s32[1]{0:T(128)} %bitcast.me_ref, bf16[5,256,192]{2,1,0:T(8,128)(2,1)S(1)} %fusion.pick_ref, bf16[64,3072]{1,0:T(8,128)(2,1)S(1)} %copy-done.1, bf16[64,3072]{1,0:T(8,128)(2,1)S(1)} %collective-permute-done.4.refs_1_, bf16[64,3072]{1,0:T(8,128)(2,1)S(1)} %collective-permute-done.5.refs_2_, ...), custom_call_target="tpu_custom_call" | custom-call | tf_op jit(solution)/shard_map/pair_products/pallas_call | solution.py:110
  59.0 0.8 pad_add_fusion.1
  59.8 7.3 %all-to-all-start = ((bf16[32,16,512]{2,1,0:T(8,128)(2,1)}), bf16[32,16,512]{2,1,0:T(8,128)(2,1)S(1)}, u32[]{:S(2)}, u32[]{:S(2)}) async-start(bf16[32,16,512]{2,1,0:T(8,128)(2,1)} %bitcast.4), calls=%async_computation | async-start | bytes 1048576 | tf_op jit(solution)/shard_map/all_to_all | solution.py:230
  67.1 1.8 %pair_products.6 = bf16[1,128,512]{2,1,0:T(8,128)(2,1)S(1)} custom-call(s32[1]{0:T(128)} %bitcast.me_ref, bf16[5,256,192]{2,1,0:T(8,128)(2,1)S(1)} %fusion.pick_ref, bf16[64,3072]{1,0:T(8,128)(2,1)S(1)} %copy-done, bf16[64,3072]{1,0:T(8,128)(2,1)} %collective-permute-done.10.refs_1_, bf16[64,3072]{1,0:T(8,128)(2,1)S(1)} %collective-permute-done.11.refs_2_, ...), custom_call_target="tpu_custom_call" | custom-call | tf_op jit(solution)/shard_map/pair_products/pallas_call | solution.py:110
  69.0 2.5 %collective-permute-start.15 = (bf16[1,128,512]{2,1,0:T(8,128)(2,1)S(1)}, bf16[1,128,512]{2,1,0:T(8,128)(2,1)S(1)}, u32[]{:S(2)}, u32[]{:S(2)}) collective-permute-start(bf16[1,128,512]{2,1,0:T(8,128)(2,1)S(1)} %pair_products.6), channel_id=1, source_target_pairs={{0,32},{32,64},{64,96},{96,128},{128,160},{160,192},{192,224},{224... | collective-permute-start | bytes 393224 | tf_op jit(solution)/shard_map/ppermute | solution.py:223
  71.5 3.5 %pair_products.7 = bf16[4,128,512]{2,1,0:T(8,128)(2,1)S(1)} custom-call(s32[1]{0:T(128)} %bitcast.me_ref, bf16[5,256,192]{2,1,0:T(8,128)(2,1)S(1)} %fusion.pick_ref, bf16[64,3072]{1,0:T(8,128)(2,1)S(1)} %copy-done, bf16[64,3072]{1,0:T(8,128)(2,1)} %collective-permute-done.10.refs_1_, bf16[64,3072]{1,0:T(8,128)(2,1)S(1)} %collective-permute-done.11.refs_2_, ...), custom_call_target="tpu_custom_call" | custom-call | tf_op jit(solution)/shard_map/pair_products/pallas_call | solution.py:110
  75.2 3.9 %all-to-all-done.refs_0_ = bf16[32,16,512]{2,1,0:T(8,128)(2,1)S(1)} async-done(((bf16[32,16,512]{2,1,0:T(8,128)(2,1)}), bf16[32,16,512]{2,1,0:T(8,128)(2,1)S(1)}, u32[]{:S(2)}, u32[]{:S(2)}) %all-to-all-start) | async-done | bytes 524320 | tf_op jit(solution)/shard_map/all_to_all | solution.py:230
  79.1 15.9 %all_to_all.18.refs_1_ = bf16[32,16,512]{2,1,0:T(8,128)(2,1)S(1)} all-to-all(bf16[32,16,512]{2,1,0:T(8,128)(2,1)S(1)} %bitcast.12), channel_id=1, replica_groups=mesh['z'=8,'y'=2,'c'=2,'h'=8] {'y','c','h'}, dimensions={0} | all-to-all | bytes 1048576 | tf_op jit(solution)/shard_map/all_to_all | solution.py:230
  95.0 1.6 %lag_sums.1 = f32[16,2432]{1,0:T(8,128)} custom-call(f32[19,2048]{1,0:T(8,128)S(1)} %copy-done.3, f32[19,2048]{1,0:T(8,128)S(1)} %copy-done.4, bf16[4096,128]{1,0:T(8,128)(2,1)S(1)} %copy-done.2, bf16[32,16,512]{2,1,0:T(8,128)(2,1)S(1)} %all-to-all-done.refs_0_, bf16[32,16,512]{2,1,0:T(8,128)(2,1)S(1)} %all_to_all.18.refs_1_), custom_call_target="tpu_custom_call" | custom-call | tf_op jit(solution)/shard_map/lag_sums/pallas_call | solution.py:157
  (42 shorter events, 2.3 us)
Async XLA Ops:
  1.5 11.4 %collective-permute-start = (s32[1,256]{1,0:T(1,128)S(1)}, s32[1,256]{1,0:T(1,128)S(1)}, u32[]{:S(2)}, u32[]{:S(2)}) collective-permute-start(s32[1,256]{1,0:T(1,128)S(1)} %bitcast_select_fusion), channel_id=1, source_target_pairs={{0,8},{8,0},{16,24},{24,16},{1,9},{9,1},{17,25},{25,17},{2,10},{10... | collective-permute-start | bytes 3080 | tf_op jit(solution)/shard_map/ppermute | solution.py:197
  4.8 8.0 %collective-permute-start.1 = (s32[1,256]{1,0:T(1,128)S(1)}, s32[1,256]{1,0:T(1,128)S(1)}, u32[]{:S(2)}, u32[]{:S(2)}) collective-permute-start(s32[1,256]{1,0:T(1,128)S(1)} %bitcast_select_fusion), channel_id=1, source_target_pairs={{0,16},{8,24},{16,0},{24,8},{1,17},{9,25},{17,1},{25,9},{2,18},{10... | collective-permute-start | bytes 3080 | tf_op jit(solution)/shard_map/ppermute | solution.py:197
  4.8 8.0 %collective-permute-start.2 = (s32[1,256]{1,0:T(1,128)S(1)}, s32[1,256]{1,0:T(1,128)S(1)}, u32[]{:S(2)}, u32[]{:S(2)}) collective-permute-start(s32[1,256]{1,0:T(1,128)S(1)} %bitcast_select_fusion), channel_id=1, source_target_pairs={{0,24},{8,16},{16,8},{24,0},{1,25},{9,17},{17,9},{25,1},{2,26},{10... | collective-permute-start | bytes 3080 | tf_op jit(solution)/shard_map/ppermute | solution.py:197
  12.9 20.5 %copy-start.1 = (bf16[64,3072]{1,0:T(8,128)(2,1)S(1)}, bf16[64,3072]{1,0:T(8,128)(2,1)}, u32[]{:S(2)}) copy-start(bf16[64,3072]{1,0:T(8,128)(2,1)} %get-tuple-element.28.refs_0_) | copy-start | bytes 1179652
  12.9 10.1 %collective-permute-start.4 = (bf16[64,3072]{1,0:T(8,128)(2,1)}, bf16[64,3072]{1,0:T(8,128)(2,1)S(1)}, u32[]{:S(2)}, u32[]{:S(2)}) collective-permute-start(bf16[64,3072]{1,0:T(8,128)(2,1)} %get-tuple-element.29), channel_id=1, source_target_pairs={{0,8},{8,0},{16,24},{24,16},{1,9},{9,1},{17,25},{25,17},{2,10},{10... | collective-permute-start | bytes 1179656 | tf_op jit(solution)/shard_map/ppermute | solution.py:211
  13.1 10.6 %collective-permute-start.5 = (bf16[64,3072]{1,0:T(8,128)(2,1)}, bf16[64,3072]{1,0:T(8,128)(2,1)S(1)}, u32[]{:S(2)}, u32[]{:S(2)}) collective-permute-start(bf16[64,3072]{1,0:T(8,128)(2,1)} %get-tuple-element.30), channel_id=1, source_target_pairs={{0,16},{8,24},{16,0},{24,8},{1,17},{9,25},{17,1},{25,9},{2,18},{10... | collective-permute-start | bytes 1179656 | tf_op jit(solution)/shard_map/ppermute | solution.py:211
  13.1 20.2 %collective-permute-start.6 = (bf16[64,3072]{1,0:T(8,128)(2,1)}, bf16[64,3072]{1,0:T(8,128)(2,1)S(1)}, u32[]{:S(2)}, u32[]{:S(2)}) collective-permute-start(bf16[64,3072]{1,0:T(8,128)(2,1)} %get-tuple-element.31), channel_id=1, source_target_pairs={{0,24},{8,16},{16,8},{24,0},{1,25},{9,17},{17,9},{25,1},{2,26},{10... | collective-permute-start | bytes 1179656 | tf_op jit(solution)/shard_map/ppermute | solution.py:211
  21.4 28.6 %collective-permute-start.11 = (bf16[64,3072]{1,0:T(8,128)(2,1)}, bf16[64,3072]{1,0:T(8,128)(2,1)S(1)}, u32[]{:S(2)}, u32[]{:S(2)}) collective-permute-start(bf16[64,3072]{1,0:T(8,128)(2,1)} %get-tuple-element.35), channel_id=1, source_target_pairs={{0,16},{8,24},{16,0},{24,8},{1,17},{9,25},{17,1},{25,9},{2,18},{10... | collective-permute-start | bytes 1179656 | tf_op jit(solution)/shard_map/ppermute | solution.py:211
  21.4 28.6 %collective-permute-start.12 = (bf16[64,3072]{1,0:T(8,128)(2,1)}, bf16[64,3072]{1,0:T(8,128)(2,1)S(1)}, u32[]{:S(2)}, u32[]{:S(2)}) collective-permute-start(bf16[64,3072]{1,0:T(8,128)(2,1)} %get-tuple-element.36), channel_id=1, source_target_pairs={{0,24},{8,16},{16,8},{24,0},{1,25},{9,17},{17,9},{25,1},{2,26},{10... | collective-permute-start | bytes 1179656 | tf_op jit(solution)/shard_map/ppermute | solution.py:211
  22.9 27.1 %collective-permute-start.10 = (bf16[64,3072]{1,0:T(8,128)(2,1)}, bf16[64,3072]{1,0:T(8,128)(2,1)}, u32[]{:S(2)}, u32[]{:S(2)}) collective-permute-start(bf16[64,3072]{1,0:T(8,128)(2,1)} %get-tuple-element.34), channel_id=1, source_target_pairs={{0,8},{8,0},{16,24},{24,16},{1,9},{9,1},{17,25},{25,17},{2,10},{10... | collective-permute-start | bytes 1179656 | tf_op jit(solution)/shard_map/ppermute | solution.py:211
  23.7 10.7 %collective-permute-start.3 = (s32[1,256]{1,0:T(1,128)S(1)}, s32[1,256]{1,0:T(1,128)S(1)}, u32[]{:S(2)}, u32[]{:S(2)}) collective-permute-start(s32[1,256]{1,0:T(1,128)S(1)} %constant_dynamic-slice_fusion), channel_id=1, source_target_pairs={{32,0},{64,32},{96,64},{128,96},{160,128},{192,160},{224,192},{0,2... | collective-permute-start | bytes 3080 | tf_op jit(solution)/shard_map/ppermute | solution.py:199
  34.3 13.8 %collective-permute-start.7 = (bf16[64,3072]{1,0:T(8,128)(2,1)}, bf16[64,3072]{1,0:T(8,128)(2,1)}, u32[]{:S(2)}, u32[]{:S(2)}) collective-permute-start(bf16[64,3072]{1,0:T(8,128)(2,1)} %get-tuple-element.42), channel_id=1, source_target_pairs={{0,32},{32,64},{64,96},{96,128},{128,160},{160,192},{192,224},{224... | collective-permute-start | bytes 1179656 | tf_op jit(solution)/shard_map/ppermute | solution.py:219
  34.4 13.8 %collective-permute-start.8 = (bf16[64,3072]{1,0:T(8,128)(2,1)}, bf16[64,3072]{1,0:T(8,128)(2,1)}, u32[]{:S(2)}, u32[]{:S(2)}) collective-permute-start(bf16[64,3072]{1,0:T(8,128)(2,1)} %get-tuple-element.41), channel_id=1, source_target_pairs={{32,0},{64,32},{96,64},{128,96},{160,128},{192,160},{224,192},{0,2... | collective-permute-start | bytes 1179656 | tf_op jit(solution)/shard_map/ppermute | solution.py:219
  38.5 11.6 %copy-start = (bf16[64,3072]{1,0:T(8,128)(2,1)S(1)}, bf16[64,3072]{1,0:T(8,128)(2,1)}, u32[]{:S(2)}) copy-start(bf16[64,3072]{1,0:T(8,128)(2,1)} %get-tuple-element.33.refs_0_) | copy-start | bytes 1179652
  49.9 9.1 %collective-permute-start.9 = (bf16[1,128,512]{2,1,0:T(8,128)(2,1)S(1)}, bf16[1,128,512]{2,1,0:T(8,128)(2,1)S(1)}, u32[]{:S(2)}, u32[]{:S(2)}) collective-permute-start(bf16[1,128,512]{2,1,0:T(8,128)(2,1)S(1)} %pair_products.4), channel_id=1, source_target_pairs={{0,32},{32,64},{64,96},{96,128},{128,160},{160,192},{192,224},{224... | collective-permute-start | bytes 393224 | tf_op jit(solution)/shard_map/ppermute | solution.py:223
  52.0 15.1 %collective-permute-start.13 = (bf16[64,3072]{1,0:T(8,128)(2,1)}, bf16[64,3072]{1,0:T(8,128)(2,1)}, u32[]{:S(2)}, u32[]{:S(2)}) collective-permute-start(bf16[64,3072]{1,0:T(8,128)(2,1)} %get-tuple-element.40), channel_id=1, source_target_pairs={{0,32},{32,64},{64,96},{96,128},{128,160},{160,192},{192,224},{224... | collective-permute-start | bytes 1179656 | tf_op jit(solution)/shard_map/ppermute | solution.py:219
  54.0 13.1 %collective-permute-start.14 = (bf16[64,3072]{1,0:T(8,128)(2,1)}, bf16[64,3072]{1,0:T(8,128)(2,1)}, u32[]{:S(2)}, u32[]{:S(2)}) collective-permute-start(bf16[64,3072]{1,0:T(8,128)(2,1)} %get-tuple-element.39), channel_id=1, source_target_pairs={{32,0},{64,32},{96,64},{128,96},{160,128},{192,160},{224,192},{0,2... | collective-permute-start | bytes 1179656 | tf_op jit(solution)/shard_map/ppermute | solution.py:219
  59.8 19.2 %all-to-all-start = ((bf16[32,16,512]{2,1,0:T(8,128)(2,1)}), bf16[32,16,512]{2,1,0:T(8,128)(2,1)S(1)}, u32[]{:S(2)}, u32[]{:S(2)}) async-start(bf16[32,16,512]{2,1,0:T(8,128)(2,1)} %bitcast.4), calls=%async_computation | async-start | bytes 1048576 | tf_op jit(solution)/shard_map/all_to_all | solution.py:230
  69.0 6.2 %collective-permute-start.15 = (bf16[1,128,512]{2,1,0:T(8,128)(2,1)S(1)}, bf16[1,128,512]{2,1,0:T(8,128)(2,1)S(1)}, u32[]{:S(2)}, u32[]{:S(2)}) collective-permute-start(bf16[1,128,512]{2,1,0:T(8,128)(2,1)S(1)} %pair_products.6), channel_id=1, source_target_pairs={{0,32},{32,64},{64,96},{96,128},{128,160},{160,192},{192,224},{224... | collective-permute-start | bytes 393224 | tf_op jit(solution)/shard_map/ppermute | solution.py:223
  75.0 19.9 %copy-start.2 = (bf16[4096,128]{1,0:T(8,128)(2,1)S(1)}, bf16[4096,128]{1,0:T(8,128)(2,1)}, u32[]{:S(2)}) copy-start(bf16[4096,128]{1,0:T(8,128)(2,1)} %constant.38.clone.table_ref) | copy-start | bytes 3145732
  75.1 19.9 %copy-start.3 = (f32[19,2048]{1,0:T(8,128)S(1)}, f32[19,2048]{1,0:T(8,128)}, u32[]{:S(2)}) copy-start(f32[19,2048]{1,0:T(8,128)} %constant.36.clone.cos_ref) | copy-start | bytes 466948
  75.1 19.9 %copy-start.4 = (f32[19,2048]{1,0:T(8,128)S(1)}, f32[19,2048]{1,0:T(8,128)}, u32[]{:S(2)}) copy-start(f32[19,2048]{1,0:T(8,128)} %constant.37.clone.sin_ref) | copy-start | bytes 466948

commit v5 on v4

--- a/solution.py
+++ b/solution.py
@@ -65,7 +65,7 @@
 def pair_kernel(numbers, me_ref, pick_ref, *refs):
     *sources, out_ref, held, sems = refs
     me = me_ref[0]
-    places = [1 + (me ^ m) for m in range(PARTS)] + [0, 5]
+    places = [1 + (me ^ m) for m in range(PARTS)] + [5 - 5 * (me & 1), 5 * (me & 1)]
     needed = {place for j in numbers for place in range(max(j - 1, 0), j + 2)}
     if numbers == (PARTS,):
         needed.remove(PARTS)
@@ -186,6 +186,9 @@
     z_count = lax.axis_size("z")
     z_up = [(n, (n + 1) % z_count) for n in range(z_count)]
     z_down = [((n + 1) % z_count, n) for n in range(z_count)]
+    zc = [(n, k) for n in range(z_count) for k in (0, 1)]
+    one_way = [(2 * n + k, 2 * ((n + 2 * k - 1) % z_count) + k) for n, k in zc]
+    other_way = [(2 * n + k, 2 * ((n + 1 - 2 * k) % z_count) + k) for n, k in zc]
     live = jnp.arange(128, dtype=jnp.int32)[None, None] < pair_count[:, None, None]
     first = 128 + pair_list[:, 0:1]
     second = pair_list[:, 1:2]
@@ -206,23 +209,29 @@
     for chunk in range(CHUNKS):
         pieces = whiten(me, spectra, chunk)
         if chunk == 0:
-            pieces, near = lax.optimization_barrier((pieces, near))
+            pieces, near, spectra = lax.optimization_barrier((pieces, near, spectra))
         arrived.append(
             [pieces[0]] + [lax.ppermute(pieces[m], ("y", "c"), yc_pairs[m]) for m in (2, 3, 1)]
         )
-    crossed, moved = [], []
-    for own, far, cross, side in arrived:
-        blocks = [own, side, far, cross]
-        top = jnp.where(y == 1, jnp.where(c == 1, own, side), jnp.where(c == 1, far, cross))
-        low = jnp.where(y == 0, jnp.where(c == 0, own, side), jnp.where(c == 0, far, cross))
-        moved.append(top)
-        crossed.append(blocks + [lax.ppermute(top, "z", z_up), lax.ppermute(low, "z", z_down)])
-    got = []
+    products, moved = [], []
     for chunk in range(CHUNKS):
-        other = pair_products((PARTS,), me, picks, crossed[chunk])
+        own, far, cross, side = arrived[chunk]
+        if chunk:
+            product = products[-1][0]
+            far, cross, side = [
+                lax.optimization_barrier((block, product))[0] for block in (far, cross, side)
+            ]
+        moved.append(jnp.where(y == c, own, far))
+        sources = [own, side, far, cross] + [
+            lax.ppermute(moved[-1], ("z", "c"), one_way),
+            lax.ppermute(jnp.where(y == c, cross, side), ("z", "c"), other_way),
+        ]
+        other = pair_products((PARTS,), me, picks, sources)
         below = lax.ppermute(other, "z", z_up)
         picks, other = lax.optimization_barrier((picks, other))
-        product = pair_products(tuple(range(PARTS)), me, picks, crossed[chunk])
+        products.append((pair_products(tuple(range(PARTS)), me, picks, sources), below))
+    got = []
+    for chunk, (product, below) in enumerate(products):
         product = product + jnp.pad(below, ((0, PARTS - 1), (0, 0), (0, 0)))
         product = product.reshape(PARTS * 128, 2 * PIECE)
         if chunk == 0:

time: 97.1 us -> 96.3 us (level)
  starting transfers between devices: 30 us -> 28.2 us
  waiting for transfers between devices: 19.8 us -> 21.2 us
  Pallas kernels: 25.1 us -> 23.9 us
  local copies, waits for them, and re-layouts: 0.06 us -> 1.09 us
    ppermute x2, waiting for transfers between devices: 0.06 us -> 3.55 us  [on_device(): below = lax.ppermute(other, 'z', z_up)]
    ppermute x2, starting transfers between devices: 2.59 us -> 0.17 us  [on_device(): below = lax.ppermute(other, 'z', z_up)]
    ppermute x6, waiting for transfers between devices: 6.18 us -> 4.91 us  [on_device(): lax.ppermute(pieces[m], ('y', 'c'), yc_pairs[m])]
    pallas_call x4, Pallas kernels: 10.9 us -> 9.65 us  [pair_products(): pl.pallas_call(functools.partial(pair_kernel, numbers), in_specs=[pl.Bloc...]
    unnamed x11 -> x15, local copies, waits for them, and re-layouts: 0.03 us -> 1.06 us
    select_n x2 -> x4, other arithmetic: 2.96 us -> 3.28 us  [the longest x2 1.65 us: on_device(): jnp.where(y == c, cross, side)]
  transfers between devices with their start and end apart: 17 -> 17, of which waited for: 5 -> 6; matrix products, arithmetic and copies ran while one was open for 4% -> 5% of each run, Pallas kernels for 24% -> 23%
where the time goes in v5:
time: 96.3 us; the launch traced here: 95.9 us
  starting transfers between devices  28.2 us (29%)
  Pallas kernels  23.9 us (25%)
  waiting for transfers between devices  21.2 us (22%)
  blocking collectives  15.5 us (16%)
  other arithmetic  5.21 us (5%)
  local copies, waits for them, and re-layouts  1.09 us (1%)
    all_to_all x1, blocking collectives, on_device(): lax.all_to_all(product, ('y', 'c', 'h'), 0, 0, tiled=True)  15.5 us
    pallas_call x2, Pallas kernels, whiten(): pl.pallas_call(whiten_kernel, grid_spec=pltpu.PrefetchScalarGridSpec(num_...  12.6 us
    pallas_call x4, Pallas kernels, pair_products(): pl.pallas_call(functools.partial(pair_kernel, numbers), in_specs=[pl.Bloc...  9.65 us
    all_to_all x1, starting transfers between devices, on_device(): lax.all_to_all(product, ('y', 'c', 'h'), 0, 0, tiled=True)  7.95 us
    ppermute x2, starting transfers between devices, on_device(): lax.ppermute(jnp.where(y == c, cross, side), ('z', 'c'), other_way)  6.91 us
    ppermute x6, waiting for transfers between devices, on_device(): lax.ppermute(pieces[m], ('y', 'c'), yc_pairs[m])  4.91 us
    ppermute x1, starting transfers between devices, on_device(): lax.ppermute(lax.dynamic_slice_in_dim(near, me[0], 1, 0), 'z', z_down)  4.76 us
    ppermute x3, starting transfers between devices, on_device(): lax.ppermute(rows, ('y', 'c'), yc_pairs[m])  4.68 us
  transfers between devices with their start and end apart: 17, of which 6 were waited for; matrix products, arithmetic and copies ran while one was open for 5% of the time, Pallas kernels for 23%

profile of v5, /device:TPU:1, one launch (start us, length us, event | category | flops | bytes accessed | tf_op | source)
XLA Modules:
  0.0 95.9 jit_solution(2491365541348304740)
XLA Ops:
  1.5 2.8 %collective-permute-start.2 = (s32[1,256]{1,0:T(1,128)S(1)}, s32[1,256]{1,0:T(1,128)S(1)}, u32[]{:S(2)}, u32[]{:S(2)}) collective-permute-start(s32[1,256]{1,0:T(1,128)S(1)} %bitcast_select_fusion), channel_id=1, source_target_pairs={{0,24},{8,16},{16,8},{24,0},{1,25},{9,17},{17,9},{25,1},{2,26},{10... | collective-permute-start | bytes 3080 | tf_op jit(solution)/shard_map/ppermute | solution.py:200
  4.2 1.9 %collective-permute-start.1 = (s32[1,256]{1,0:T(1,128)S(1)}, s32[1,256]{1,0:T(1,128)S(1)}, u32[]{:S(2)}, u32[]{:S(2)}) collective-permute-start(s32[1,256]{1,0:T(1,128)S(1)} %bitcast_select_fusion), channel_id=1, source_target_pairs={{0,16},{8,24},{16,0},{24,8},{1,17},{9,25},{17,1},{25,9},{2,18},{10... | collective-permute-start | bytes 3080 | tf_op jit(solution)/shard_map/ppermute | solution.py:200
  6.1 6.3 %whiten.2 = (bf16[64,3072]{1,0:T(8,128)(2,1)}, bf16[64,3072]{1,0:T(8,128)(2,1)}, bf16[64,3072]{1,0:T(8,128)(2,1)}, bf16[64,3072]{1,0:T(8,128)(2,1)}) custom-call(s32[1]{0:T(128)} %bitcast.me_ref, bf16[64,6,2,2048]{3,2,1,0:T(2,128)(2,1)} %x_ref.1), custom_call_target="tpu_custom_call" | custom-call | tf_op jit(solution)/shard_map/whiten/pallas_call | solution.py:52
  13.1 4.8 %collective-permute-start.3 = (s32[1,256]{1,0:T(1,128)S(1)}, s32[1,256]{1,0:T(1,128)S(1)}, u32[]{:S(2)}, u32[]{:S(2)}) collective-permute-start(s32[1,256]{1,0:T(1,128)S(1)} %constant_dynamic-slice_fusion), channel_id=1, source_target_pairs={{32,0},{64,32},{96,64},{128,96},{160,128},{192,160},{224,192},{0,2... | collective-permute-start | bytes 3080 | tf_op jit(solution)/shard_map/ppermute | solution.py:202
  17.8 1.0 collective-permute-start.4
  18.8 6.3 %whiten.3 = (bf16[64,3072]{1,0:T(8,128)(2,1)}, bf16[64,3072]{1,0:T(8,128)(2,1)}, bf16[64,3072]{1,0:T(8,128)(2,1)}, bf16[64,3072]{1,0:T(8,128)(2,1)}) custom-call(s32[1]{0:T(128)} %bitcast.me_ref, bf16[64,6,2,2048]{3,2,1,0:T(2,128)(2,1)} %x_ref.1), custom_call_target="tpu_custom_call" | custom-call | tf_op jit(solution)/shard_map/whiten/pallas_call | solution.py:52
  25.1 1.3 %collective-permute-start.10 = (bf16[64,3072]{1,0:T(8,128)(2,1)}, bf16[64,3072]{1,0:T(8,128)(2,1)S(1)}, u32[]{:S(2)}, u32[]{:S(2)}) collective-permute-start(bf16[64,3072]{1,0:T(8,128)(2,1)} %get-tuple-element.39), channel_id=1, source_target_pairs={{0,16},{8,24},{16,0},{24,8},{1,17},{9,25},{17,1},{25,9},{2,18},{10... | collective-permute-start | bytes 1179656 | tf_op jit(solution)/shard_map/ppermute | solution.py:214
  28.1 4.9 %collective-permute-done.6.refs_3_ = bf16[64,3072]{1,0:T(8,128)(2,1)S(1)} collective-permute-done((bf16[64,3072]{1,0:T(8,128)(2,1)}, bf16[64,3072]{1,0:T(8,128)(2,1)S(1)}, u32[]{:S(2)}, u32[]{:S(2)}) %collective-permute-start.6) | collective-permute-done | bytes 393248 | tf_op jit(solution)/shard_map/ppermute | solution.py:214
  33.0 0.9 broadcast_select_fusion.2
  33.9 3.8 %collective-permute-start.8 = (bf16[64,3072]{1,0:T(8,128)(2,1)}, bf16[64,3072]{1,0:T(8,128)(2,1)}, u32[]{:S(2)}, u32[]{:S(2)}) collective-permute-start(bf16[64,3072]{1,0:T(8,128)(2,1)} %broadcast_select_fusion.2), channel_id=1, source_target_pairs={{0,32},{8,232},{32,64},{40,8},{64,96},{72,40},{96,128},{104,72},{1... | collective-permute-start | bytes 1179656 | tf_op jit(solution)/shard_map/ppermute | solution.py:227
  37.9 4.7 %collective-permute-done.7.refs_4_ = bf16[64,3072]{1,0:T(8,128)(2,1)} collective-permute-done((bf16[64,3072]{1,0:T(8,128)(2,1)}, bf16[64,3072]{1,0:T(8,128)(2,1)}, u32[]{:S(2)}, u32[]{:S(2)}) %collective-permute-start.7) | collective-permute-done | bytes 393248 | tf_op jit(solution)/shard_map/ppermute | solution.py:226
  42.6 3.8 %collective-permute-done.8.refs_5_ = bf16[64,3072]{1,0:T(8,128)(2,1)} collective-permute-done((bf16[64,3072]{1,0:T(8,128)(2,1)}, bf16[64,3072]{1,0:T(8,128)(2,1)}, u32[]{:S(2)}, u32[]{:S(2)}) %collective-permute-start.8) | collective-permute-done | bytes 393248 | tf_op jit(solution)/shard_map/ppermute | solution.py:227
  46.4 1.8 %pair_products.4 = bf16[1,128,512]{2,1,0:T(8,128)(2,1)S(1)} custom-call(s32[1]{0:T(128)} %bitcast.me_ref, bf16[5,256,192]{2,1,0:T(8,128)(2,1)S(1)} %fusion.pick_ref, bf16[64,3072]{1,0:T(8,128)(2,1)S(1)} %copy-done.1, bf16[64,3072]{1,0:T(8,128)(2,1)S(1)} %collective-permute-done.4.refs_1_, bf16[64,3072]{1,0:T(8,128)(2,1)S(1)} %collective-permute-done.5.refs_2_, ...), custom_call_target="tpu_custom_call" | custom-call | tf_op jit(solution)/shard_map/pair_products/pallas_call | solution.py:110
  48.4 1.0 %copy-done.3 = bf16[64,3072]{1,0:T(8,128)(2,1)S(1)} copy-done((bf16[64,3072]{1,0:T(8,128)(2,1)S(1)}, bf16[64,3072]{1,0:T(8,128)(2,1)}, u32[]{:S(2)}) %copy-start.3) | copy-done | bytes 393240
  49.4 3.9 %pair_products.5 = bf16[4,128,512]{2,1,0:T(8,128)(2,1)S(1)} custom-call(s32[1]{0:T(128)} %bitcast.me_ref, bf16[5,256,192]{2,1,0:T(8,128)(2,1)S(1)} %fusion.pick_ref, bf16[64,3072]{1,0:T(8,128)(2,1)S(1)} %copy-done.1, bf16[64,3072]{1,0:T(8,128)(2,1)S(1)} %collective-permute-done.4.refs_1_, bf16[64,3072]{1,0:T(8,128)(2,1)S(1)} %collective-permute-done.5.refs_2_, ...), custom_call_target="tpu_custom_call" | custom-call | tf_op jit(solution)/shard_map/pair_products/pallas_call | solution.py:110
  54.9 3.1 %collective-permute-start.14 = (bf16[64,3072]{1,0:T(8,128)(2,1)}, bf16[64,3072]{1,0:T(8,128)(2,1)S(1)}, u32[]{:S(2)}, u32[]{:S(2)}) collective-permute-start(bf16[64,3072]{1,0:T(8,128)(2,1)} %broadcast_select_fusion), channel_id=1, source_target_pairs={{0,32},{8,232},{32,64},{40,8},{64,96},{72,40},{96,128},{104,72},{1... | collective-permute-start | bytes 1179656 | tf_op jit(solution)/shard_map/ppermute | solution.py:227
  58.0 0.9 pad_add_fusion.1
  58.9 8.0 %all-to-all-start = ((bf16[32,16,512]{2,1,0:T(8,128)(2,1)}), bf16[32,16,512]{2,1,0:T(8,128)(2,1)S(1)}, u32[]{:S(2)}, u32[]{:S(2)}) async-start(bf16[32,16,512]{2,1,0:T(8,128)(2,1)} %bitcast.12), calls=%async_computation | async-start | bytes 1048576 | tf_op jit(solution)/shard_map/all_to_all | solution.py:239
  67.1 1.0 %pair_products.6 = bf16[1,128,512]{2,1,0:T(8,128)(2,1)S(1)} custom-call(s32[1]{0:T(128)} %bitcast.me_ref, bf16[5,256,192]{2,1,0:T(8,128)(2,1)S(1)} %fusion.pick_ref, bf16[64,3072]{1,0:T(8,128)(2,1)S(1)} %copy-done, bf16[64,3072]{1,0:T(8,128)(2,1)S(1)} %collective-permute-done.11.refs_1_, bf16[64,3072]{1,0:T(8,128)(2,1)S(1)} %collective-permute-done.10.refs_2_, ...), custom_call_target="tpu_custom_call" | custom-call | tf_op jit(solution)/shard_map/pair_products/pallas_call | solution.py:110
  68.2 3.0 %pair_products.7 = bf16[4,128,512]{2,1,0:T(8,128)(2,1)S(1)} custom-call(s32[1]{0:T(128)} %bitcast.me_ref, bf16[5,256,192]{2,1,0:T(8,128)(2,1)S(1)} %fusion.pick_ref, bf16[64,3072]{1,0:T(8,128)(2,1)S(1)} %copy-done, bf16[64,3072]{1,0:T(8,128)(2,1)S(1)} %collective-permute-done.11.refs_1_, bf16[64,3072]{1,0:T(8,128)(2,1)S(1)} %collective-permute-done.10.refs_2_, ...), custom_call_target="tpu_custom_call" | custom-call | tf_op jit(solution)/shard_map/pair_products/pallas_call | solution.py:110
  71.2 3.5 %collective-permute-done.15 = bf16[1,128,512]{2,1,0:T(8,128)(2,1)S(1)} collective-permute-done((bf16[1,128,512]{2,1,0:T(8,128)(2,1)S(1)}, bf16[1,128,512]{2,1,0:T(8,128)(2,1)S(1)}, u32[]{:S(2)}, u32[]{:S(2)}) %collective-permute-start.15) | collective-permute-done | bytes 131104 | tf_op jit(solution)/shard_map/ppermute | solution.py:230
  74.8 4.0 %all-to-all-done.refs_0_ = bf16[32,16,512]{2,1,0:T(8,128)(2,1)S(1)} async-done(((bf16[32,16,512]{2,1,0:T(8,128)(2,1)}), bf16[32,16,512]{2,1,0:T(8,128)(2,1)S(1)}, u32[]{:S(2)}, u32[]{:S(2)}) %all-to-all-start) | async-done | bytes 524320 | tf_op jit(solution)/shard_map/all_to_all | solution.py:239
  78.8 15.5 %all_to_all.18.refs_1_ = bf16[32,16,512]{2,1,0:T(8,128)(2,1)S(1)} all-to-all(bf16[32,16,512]{2,1,0:T(8,128)(2,1)S(1)} %bitcast.13), channel_id=1, replica_groups=mesh['z'=8,'y'=2,'c'=2,'h'=8] {'y','c','h'}, dimensions={0} | all-to-all | bytes 1048576 | tf_op jit(solution)/shard_map/all_to_all | solution.py:239
  94.3 1.6 %lag_sums.1 = f32[16,2432]{1,0:T(8,128)} custom-call(f32[19,2048]{1,0:T(8,128)S(1)} %copy-done.6, f32[19,2048]{1,0:T(8,128)S(1)} %copy-done.5, bf16[4096,128]{1,0:T(8,128)(2,1)S(1)} %copy-done.4, bf16[32,16,512]{2,1,0:T(8,128)(2,1)S(1)} %all-to-all-done.refs_0_, bf16[32,16,512]{2,1,0:T(8,128)(2,1)S(1)} %all_to_all.18.refs_1_), custom_call_target="tpu_custom_call" | custom-call | tf_op jit(solution)/shard_map/lag_sums/pallas_call | solution.py:157
  (48 shorter events, 5.5 us)
Async XLA Ops:
  1.5 11.0 %collective-permute-start.2 = (s32[1,256]{1,0:T(1,128)S(1)}, s32[1,256]{1,0:T(1,128)S(1)}, u32[]{:S(2)}, u32[]{:S(2)}) collective-permute-start(s32[1,256]{1,0:T(1,128)S(1)} %bitcast_select_fusion), channel_id=1, source_target_pairs={{0,24},{8,16},{16,8},{24,0},{1,25},{9,17},{17,9},{25,1},{2,26},{10... | collective-permute-start | bytes 3080 | tf_op jit(solution)/shard_map/ppermute | solution.py:200
  4.2 8.2 %collective-permute-start.1 = (s32[1,256]{1,0:T(1,128)S(1)}, s32[1,256]{1,0:T(1,128)S(1)}, u32[]{:S(2)}, u32[]{:S(2)}) collective-permute-start(s32[1,256]{1,0:T(1,128)S(1)} %bitcast_select_fusion), channel_id=1, source_target_pairs={{0,16},{8,24},{16,0},{24,8},{1,17},{9,25},{17,1},{25,9},{2,18},{10... | collective-permute-start | bytes 3080 | tf_op jit(solution)/shard_map/ppermute | solution.py:200
  6.1 6.3 %collective-permute-start = (s32[1,256]{1,0:T(1,128)S(1)}, s32[1,256]{1,0:T(1,128)S(1)}, u32[]{:S(2)}, u32[]{:S(2)}) collective-permute-start(s32[1,256]{1,0:T(1,128)S(1)} %bitcast_select_fusion), channel_id=1, source_target_pairs={{0,8},{8,0},{16,24},{24,16},{1,9},{9,1},{17,25},{25,17},{2,10},{10... | collective-permute-start | bytes 3080 | tf_op jit(solution)/shard_map/ppermute | solution.py:200
  12.5 14.0 %collective-permute-start.5 = (bf16[64,3072]{1,0:T(8,128)(2,1)}, bf16[64,3072]{1,0:T(8,128)(2,1)S(1)}, u32[]{:S(2)}, u32[]{:S(2)}) collective-permute-start(bf16[64,3072]{1,0:T(8,128)(2,1)} %get-tuple-element.34), channel_id=1, source_target_pairs={{0,16},{8,24},{16,0},{24,8},{1,17},{9,25},{17,1},{25,9},{2,18},{10... | collective-permute-start | bytes 1179656 | tf_op jit(solution)/shard_map/ppermute | solution.py:214
  13.1 14.2 %copy-start.1 = (bf16[64,3072]{1,0:T(8,128)(2,1)S(1)}, bf16[64,3072]{1,0:T(8,128)(2,1)}, u32[]{:S(2)}) copy-start(bf16[64,3072]{1,0:T(8,128)(2,1)} %get-tuple-element.32.refs_0_) | copy-start | bytes 1179652
  13.1 20.8 %collective-permute-start.3 = (s32[1,256]{1,0:T(1,128)S(1)}, s32[1,256]{1,0:T(1,128)S(1)}, u32[]{:S(2)}, u32[]{:S(2)}) collective-permute-start(s32[1,256]{1,0:T(1,128)S(1)} %constant_dynamic-slice_fusion), channel_id=1, source_target_pairs={{32,0},{64,32},{96,64},{128,96},{160,128},{192,160},{224,192},{0,2... | collective-permute-start | bytes 3080 | tf_op jit(solution)/shard_map/ppermute | solution.py:202
  17.8 10.2 %collective-permute-start.4 = (bf16[64,3072]{1,0:T(8,128)(2,1)}, bf16[64,3072]{1,0:T(8,128)(2,1)S(1)}, u32[]{:S(2)}, u32[]{:S(2)}) collective-permute-start(bf16[64,3072]{1,0:T(8,128)(2,1)} %get-tuple-element.33), channel_id=1, source_target_pairs={{0,8},{8,0},{16,24},{24,16},{1,9},{9,1},{17,25},{25,17},{2,10},{10... | collective-permute-start | bytes 1179656 | tf_op jit(solution)/shard_map/ppermute | solution.py:214
  18.8 14.2 %collective-permute-start.6 = (bf16[64,3072]{1,0:T(8,128)(2,1)}, bf16[64,3072]{1,0:T(8,128)(2,1)S(1)}, u32[]{:S(2)}, u32[]{:S(2)}) collective-permute-start(bf16[64,3072]{1,0:T(8,128)(2,1)} %get-tuple-element.35), channel_id=1, source_target_pairs={{0,24},{8,16},{16,8},{24,0},{1,25},{9,17},{17,9},{25,1},{2,26},{10... | collective-permute-start | bytes 1179656 | tf_op jit(solution)/shard_map/ppermute | solution.py:214
  25.1 28.1 %collective-permute-start.10 = (bf16[64,3072]{1,0:T(8,128)(2,1)}, bf16[64,3072]{1,0:T(8,128)(2,1)S(1)}, u32[]{:S(2)}, u32[]{:S(2)}) collective-permute-start(bf16[64,3072]{1,0:T(8,128)(2,1)} %get-tuple-element.39), channel_id=1, source_target_pairs={{0,16},{8,24},{16,0},{24,8},{1,17},{9,25},{17,1},{25,9},{2,18},{10... | collective-permute-start | bytes 1179656 | tf_op jit(solution)/shard_map/ppermute | solution.py:214
  26.4 27.7 %collective-permute-start.11 = (bf16[64,3072]{1,0:T(8,128)(2,1)}, bf16[64,3072]{1,0:T(8,128)(2,1)S(1)}, u32[]{:S(2)}, u32[]{:S(2)}) collective-permute-start(bf16[64,3072]{1,0:T(8,128)(2,1)} %get-tuple-element.42), channel_id=1, source_target_pairs={{0,8},{8,0},{16,24},{24,16},{1,9},{9,1},{17,25},{25,17},{2,10},{10... | collective-permute-start | bytes 1179656 | tf_op jit(solution)/shard_map/ppermute | solution.py:214
  28.1 26.1 %collective-permute-start.12 = (bf16[64,3072]{1,0:T(8,128)(2,1)}, bf16[64,3072]{1,0:T(8,128)(2,1)S(1)}, u32[]{:S(2)}, u32[]{:S(2)}) collective-permute-start(bf16[64,3072]{1,0:T(8,128)(2,1)} %get-tuple-element.44), channel_id=1, source_target_pairs={{0,24},{8,16},{16,8},{24,0},{1,25},{9,17},{17,9},{25,1},{2,26},{10... | collective-permute-start | bytes 1179656 | tf_op jit(solution)/shard_map/ppermute | solution.py:214
  33.0 13.4 %copy-start.2 = (bf16[64,3072]{1,0:T(8,128)(2,1)}, bf16[64,3072]{1,0:T(8,128)(2,1)S(1)}, u32[]{:S(2)}) copy-start(bf16[64,3072]{1,0:T(8,128)(2,1)S(1)} %collective-permute-done.6.refs_3_) | copy-start | bytes 1179652
  33.0 9.6 %collective-permute-start.7 = (bf16[64,3072]{1,0:T(8,128)(2,1)}, bf16[64,3072]{1,0:T(8,128)(2,1)}, u32[]{:S(2)}, u32[]{:S(2)}) collective-permute-start(bf16[64,3072]{1,0:T(8,128)(2,1)} %broadcast_select_fusion.3), channel_id=1, source_target_pairs={{0,224},{8,40},{32,0},{40,72},{64,32},{72,104},{96,64},{104,136},{... | collective-permute-start | bytes 1179656 | tf_op jit(solution)/shard_map/ppermute | solution.py:226
  33.9 12.6 %collective-permute-start.8 = (bf16[64,3072]{1,0:T(8,128)(2,1)}, bf16[64,3072]{1,0:T(8,128)(2,1)}, u32[]{:S(2)}, u32[]{:S(2)}) collective-permute-start(bf16[64,3072]{1,0:T(8,128)(2,1)} %broadcast_select_fusion.2), channel_id=1, source_target_pairs={{0,32},{8,232},{32,64},{40,8},{64,96},{72,40},{96,128},{104,72},{1... | collective-permute-start | bytes 1179656 | tf_op jit(solution)/shard_map/ppermute | solution.py:227
  48.2 5.0 %copy-start = (bf16[64,3072]{1,0:T(8,128)(2,1)S(1)}, bf16[64,3072]{1,0:T(8,128)(2,1)}, u32[]{:S(2)}) copy-start(bf16[64,3072]{1,0:T(8,128)(2,1)} %get-tuple-element.38.refs_0_) | copy-start | bytes 1179652
  48.2 9.8 %collective-permute-start.9 = (bf16[1,128,512]{2,1,0:T(8,128)(2,1)S(1)}, bf16[1,128,512]{2,1,0:T(8,128)(2,1)S(1)}, u32[]{:S(2)}, u32[]{:S(2)}) collective-permute-start(bf16[1,128,512]{2,1,0:T(8,128)(2,1)S(1)} %pair_products.4), channel_id=1, source_target_pairs={{0,32},{32,64},{64,96},{96,128},{128,160},{160,192},{192,224},{224... | collective-permute-start | bytes 393224 | tf_op jit(solution)/shard_map/ppermute | solution.py:230
  48.3 1.0 %copy-start.3 = (bf16[64,3072]{1,0:T(8,128)(2,1)S(1)}, bf16[64,3072]{1,0:T(8,128)(2,1)}, u32[]{:S(2)}) copy-start(bf16[64,3072]{1,0:T(8,128)(2,1)} %copy-done.2) | copy-start | bytes 1179652
  54.1 12.7 %collective-permute-start.13 = (bf16[64,3072]{1,0:T(8,128)(2,1)}, bf16[64,3072]{1,0:T(8,128)(2,1)S(1)}, u32[]{:S(2)}, u32[]{:S(2)}) collective-permute-start(bf16[64,3072]{1,0:T(8,128)(2,1)} %broadcast_select_fusion.1), channel_id=1, source_target_pairs={{0,224},{8,40},{32,0},{40,72},{64,32},{72,104},{96,64},{104,136},{... | collective-permute-start | bytes 1179656 | tf_op jit(solution)/shard_map/ppermute | solution.py:226
  54.9 12.2 %collective-permute-start.14 = (bf16[64,3072]{1,0:T(8,128)(2,1)}, bf16[64,3072]{1,0:T(8,128)(2,1)S(1)}, u32[]{:S(2)}, u32[]{:S(2)}) collective-permute-start(bf16[64,3072]{1,0:T(8,128)(2,1)} %broadcast_select_fusion), channel_id=1, source_target_pairs={{0,32},{8,232},{32,64},{40,8},{64,96},{72,40},{96,128},{104,72},{1... | collective-permute-start | bytes 1179656 | tf_op jit(solution)/shard_map/ppermute | solution.py:227
  58.9 19.9 %all-to-all-start = ((bf16[32,16,512]{2,1,0:T(8,128)(2,1)}), bf16[32,16,512]{2,1,0:T(8,128)(2,1)S(1)}, u32[]{:S(2)}, u32[]{:S(2)}) async-start(bf16[32,16,512]{2,1,0:T(8,128)(2,1)} %bitcast.12), calls=%async_computation | async-start | bytes 1048576 | tf_op jit(solution)/shard_map/all_to_all | solution.py:239
  68.1 6.6 %collective-permute-start.15 = (bf16[1,128,512]{2,1,0:T(8,128)(2,1)S(1)}, bf16[1,128,512]{2,1,0:T(8,128)(2,1)S(1)}, u32[]{:S(2)}, u32[]{:S(2)}) collective-permute-start(bf16[1,128,512]{2,1,0:T(8,128)(2,1)S(1)} %pair_products.6), channel_id=1, source_target_pairs={{0,32},{32,64},{64,96},{96,128},{128,160},{160,192},{192,224},{224... | collective-permute-start | bytes 393224 | tf_op jit(solution)/shard_map/ppermute | solution.py:230
  71.1 23.1 %copy-start.4 = (bf16[4096,128]{1,0:T(8,128)(2,1)S(1)}, bf16[4096,128]{1,0:T(8,128)(2,1)}, u32[]{:S(2)}) copy-start(bf16[4096,128]{1,0:T(8,128)(2,1)} %constant.36.clone.table_ref) | copy-start | bytes 3145732
  71.1 23.1 %copy-start.5 = (f32[19,2048]{1,0:T(8,128)S(1)}, f32[19,2048]{1,0:T(8,128)}, u32[]{:S(2)}) copy-start(f32[19,2048]{1,0:T(8,128)} %constant.35.clone.sin_ref) | copy-start | bytes 466948
  71.2 23.1 %copy-start.6 = (f32[19,2048]{1,0:T(8,128)S(1)}, f32[19,2048]{1,0:T(8,128)}, u32[]{:S(2)}) copy-start(f32[19,2048]{1,0:T(8,128)} %constant.34.clone.cos_ref) | copy-start | bytes 466948

commit v6 on v5

--- a/solution.py
+++ b/solution.py
@@ -207,6 +207,8 @@
 
     arrived = []
     for chunk in range(CHUNKS):
+        if chunk:
+            spectra = lax.optimization_barrier((spectra, picks))[0]
         pieces = whiten(me, spectra, chunk)
         if chunk == 0:
             pieces, near, spectra = lax.optimization_barrier((pieces, near, spectra))
@@ -216,7 +218,9 @@
     products, moved = [], []
     for chunk in range(CHUNKS):
         own, far, cross, side = arrived[chunk]
-        if chunk:
+        if chunk == 0:
+            far = lax.optimization_barrier((far, arrived[1][0]))[0]
+        else:
             product = products[-1][0]
             far, cross, side = [
                 lax.optimization_barrier((block, product))[0] for block in (far, cross, side)

time: 96.3 us -> 101 us (1.049)
  waiting for transfers between devices: 21.2 us -> 29.8 us
  other arithmetic: 5.21 us -> 3.62 us
  starting transfers between devices: 28.2 us -> 26.9 us
  local copies, waits for them, and re-layouts: 1.09 us -> 0.08 us
    ppermute x6, waiting for transfers between devices: 4.91 us -> 14 us  [on_device(): lax.ppermute(pieces[m], ('y', 'c'), yc_pairs[m])]
    ppermute x2, starting transfers between devices: 6.91 us -> 2.74 us  [on_device(): lax.ppermute(jnp.where(y == c, cross, side), ('z', 'c'), other_way)]
    ppermute x6, starting transfers between devices: 3.74 us -> 6.69 us  [on_device(): lax.ppermute(pieces[m], ('y', 'c'), yc_pairs[m])]
    ppermute x2, waiting for transfers between devices: 4.66 us -> 2.72 us  [on_device(): lax.ppermute(moved[-1], ('z', 'c'), one_way)]
    ppermute x3, waiting for transfers between devices: 0.01 us -> 1.25 us  [on_device(): lax.ppermute(rows, ('y', 'c'), yc_pairs[m])]
    all_to_all x1, starting transfers between devices: 7.95 us -> 6.91 us  [on_device(): lax.all_to_all(product, ('y', 'c', 'h'), 0, 0, tiled=True)]
    unnamed x15 -> x17, local copies, waits for them, and re-layouts: 1.06 us -> 0.05 us
  transfers between devices with their start and end apart: 17 -> 17, of which waited for: 6 -> 7; matrix products, arithmetic and copies ran while one was open for 5% -> 3% of each run, Pallas kernels for 23% -> 21%
where the time goes in v6:
time: 101 us; the launch traced here: 100 us
  waiting for transfers between devices  29.8 us (30%)
  starting transfers between devices  26.9 us (27%)
  Pallas kernels  23.2 us (23%)
  blocking collectives  15.9 us (16%)
  other arithmetic  3.62 us (4%)
    all_to_all x1, blocking collectives, on_device(): lax.all_to_all(product, ('y', 'c', 'h'), 0, 0, tiled=True)  15.9 us
    ppermute x6, waiting for transfers between devices, on_device(): lax.ppermute(pieces[m], ('y', 'c'), yc_pairs[m])  14 us
    pallas_call x2, Pallas kernels, whiten(): pl.pallas_call(whiten_kernel, grid_spec=pltpu.PrefetchScalarGridSpec(num_...  12.6 us
    pallas_call x4, Pallas kernels, pair_products(): pl.pallas_call(functools.partial(pair_kernel, numbers), in_specs=[pl.Bloc...  8.92 us
    all_to_all x1, starting transfers between devices, on_device(): lax.all_to_all(product, ('y', 'c', 'h'), 0, 0, tiled=True)  6.91 us
    ppermute x6, starting transfers between devices, on_device(): lax.ppermute(pieces[m], ('y', 'c'), yc_pairs[m])  6.69 us
    ppermute x1, starting transfers between devices, on_device(): lax.ppermute(lax.dynamic_slice_in_dim(near, me[0], 1, 0), 'z', z_down)  4.92 us
    ppermute x2, waiting for transfers between devices, on_device(): lax.ppermute(jnp.where(y == c, cross, side), ('z', 'c'), other_way)  4.87 us
  transfers between devices with their start and end apart: 17, of which 7 were waited for; matrix products, arithmetic and copies ran while one was open for 3% of the time, Pallas kernels for 21%

profile of v6, /device:TPU:1, one launch (start us, length us, event | category | flops | bytes accessed | tf_op | source)
XLA Modules:
  0.0 100.4 jit_solution(10053376782814365349)
XLA Ops:
  1.5 2.8 %collective-permute-start.2 = (s32[1,256]{1,0:T(1,128)S(1)}, s32[1,256]{1,0:T(1,128)S(1)}, u32[]{:S(2)}, u32[]{:S(2)}) collective-permute-start(s32[1,256]{1,0:T(1,128)S(1)} %bitcast_select_fusion), channel_id=1, source_target_pairs={{0,24},{8,16},{16,8},{24,0},{1,25},{9,17},{17,9},{25,1},{2,26},{10... | collective-permute-start | bytes 3080 | tf_op jit(solution)/shard_map/ppermute | solution.py:200
  4.2 1.9 %collective-permute-start.1 = (s32[1,256]{1,0:T(1,128)S(1)}, s32[1,256]{1,0:T(1,128)S(1)}, u32[]{:S(2)}, u32[]{:S(2)}) collective-permute-start(s32[1,256]{1,0:T(1,128)S(1)} %bitcast_select_fusion), channel_id=1, source_target_pairs={{0,16},{8,24},{16,0},{24,8},{1,17},{9,25},{17,1},{25,9},{2,18},{10... | collective-permute-start | bytes 3080 | tf_op jit(solution)/shard_map/ppermute | solution.py:200
  6.1 1.2 %collective-permute-done.1 = s32[1,256]{1,0:T(1,128)S(1)} collective-permute-done((s32[1,256]{1,0:T(1,128)S(1)}, s32[1,256]{1,0:T(1,128)S(1)}, u32[]{:S(2)}, u32[]{:S(2)}) %collective-permute-start.1) | collective-permute-done | bytes 1056 | tf_op jit(solution)/shard_map/ppermute | solution.py:200
  7.4 4.9 %collective-permute-start.3 = (s32[1,256]{1,0:T(1,128)S(1)}, s32[1,256]{1,0:T(1,128)S(1)}, u32[]{:S(2)}, u32[]{:S(2)}) collective-permute-start(s32[1,256]{1,0:T(1,128)S(1)} %constant_dynamic-slice_fusion), channel_id=1, source_target_pairs={{32,0},{64,32},{96,64},{128,96},{160,128},{192,160},{224,192},{0,2... | collective-permute-start | bytes 3080 | tf_op jit(solution)/shard_map/ppermute | solution.py:202
  12.3 6.3 %whiten.2 = (bf16[64,3072]{1,0:T(8,128)(2,1)}, bf16[64,3072]{1,0:T(8,128)(2,1)}, bf16[64,3072]{1,0:T(8,128)(2,1)}, bf16[64,3072]{1,0:T(8,128)(2,1)}) custom-call(s32[1]{0:T(128)} %bitcast.me_ref, bf16[64,6,2,2048]{3,2,1,0:T(2,128)(2,1)} %x_ref.1), custom_call_target="tpu_custom_call" | custom-call | tf_op jit(solution)/shard_map/whiten/pallas_call | solution.py:52
  18.7 1.3 %collective-permute-start.4 = (bf16[64,3072]{1,0:T(8,128)(2,1)}, bf16[64,3072]{1,0:T(8,128)(2,1)S(1)}, u32[]{:S(2)}, u32[]{:S(2)}) collective-permute-start(bf16[64,3072]{1,0:T(8,128)(2,1)} %get-tuple-element.35), channel_id=1, source_target_pairs={{0,8},{8,0},{16,24},{24,16},{1,9},{9,1},{17,25},{25,17},{2,10},{10... | collective-permute-start | bytes 1179656 | tf_op jit(solution)/shard_map/ppermute | solution.py:216
  20.3 1.3 %collective-permute-start.6 = (bf16[64,3072]{1,0:T(8,128)(2,1)}, bf16[64,3072]{1,0:T(8,128)(2,1)S(1)}, u32[]{:S(2)}, u32[]{:S(2)}) collective-permute-start(bf16[64,3072]{1,0:T(8,128)(2,1)} %get-tuple-element.41), channel_id=1, source_target_pairs={{0,24},{8,16},{16,8},{24,0},{1,25},{9,17},{17,9},{25,1},{2,26},{10... | collective-permute-start | bytes 1179656 | tf_op jit(solution)/shard_map/ppermute | solution.py:216
  21.9 6.3 %whiten.3 = (bf16[64,3072]{1,0:T(8,128)(2,1)}, bf16[64,3072]{1,0:T(8,128)(2,1)}, bf16[64,3072]{1,0:T(8,128)(2,1)}, bf16[64,3072]{1,0:T(8,128)(2,1)}) custom-call(s32[1]{0:T(128)} %bitcast.me_ref, bf16[64,6,2,2048]{3,2,1,0:T(2,128)(2,1)} %x_ref.1), custom_call_target="tpu_custom_call" | custom-call | tf_op jit(solution)/shard_map/whiten/pallas_call | solution.py:52
  28.2 11.2 %collective-permute-done.6.refs_3_ = bf16[64,3072]{1,0:T(8,128)(2,1)S(1)} collective-permute-done((bf16[64,3072]{1,0:T(8,128)(2,1)}, bf16[64,3072]{1,0:T(8,128)(2,1)S(1)}, u32[]{:S(2)}, u32[]{:S(2)}) %collective-permute-start.6) | collective-permute-done | bytes 393248 | tf_op jit(solution)/shard_map/ppermute | solution.py:216
  41.5 2.3 %collective-permute-start.11 = (bf16[64,3072]{1,0:T(8,128)(2,1)S(1)}, bf16[64,3072]{1,0:T(8,128)(2,1)S(1)}, u32[]{:S(2)}, u32[]{:S(2)}) collective-permute-start(bf16[64,3072]{1,0:T(8,128)(2,1)S(1)} %copy-done.6), channel_id=1, source_target_pairs={{0,8},{8,0},{16,24},{24,16},{1,9},{9,1},{17,25},{25,17},{2,10},{10... | collective-permute-start | bytes 1179656 | tf_op jit(solution)/shard_map/ppermute | solution.py:216
  43.8 1.1 %collective-permute-start.12 = (bf16[64,3072]{1,0:T(8,128)(2,1)S(1)}, bf16[64,3072]{1,0:T(8,128)(2,1)S(1)}, u32[]{:S(2)}, u32[]{:S(2)}) collective-permute-start(bf16[64,3072]{1,0:T(8,128)(2,1)S(1)} %copy-done.5), channel_id=1, source_target_pairs={{0,24},{8,16},{16,8},{24,0},{1,25},{9,17},{17,9},{25,1},{2,26},{10... | collective-permute-start | bytes 1179656 | tf_op jit(solution)/shard_map/ppermute | solution.py:216
  44.9 4.9 %collective-permute-done.8.refs_5_ = bf16[64,3072]{1,0:T(8,128)(2,1)S(1)} collective-permute-done((bf16[64,3072]{1,0:T(8,128)(2,1)S(1)}, bf16[64,3072]{1,0:T(8,128)(2,1)S(1)}, u32[]{:S(2)}, u32[]{:S(2)}) %collective-permute-start.8) | collective-permute-done | bytes 393248 | tf_op jit(solution)/shard_map/ppermute | solution.py:231
  49.8 2.7 %collective-permute-done.7.refs_4_ = bf16[64,3072]{1,0:T(8,128)(2,1)S(1)} collective-permute-done((bf16[64,3072]{1,0:T(8,128)(2,1)S(1)}, bf16[64,3072]{1,0:T(8,128)(2,1)S(1)}, u32[]{:S(2)}, u32[]{:S(2)}) %collective-permute-start.7) | collective-permute-done | bytes 393248 | tf_op jit(solution)/shard_map/ppermute | solution.py:230
  52.5 1.0 pair_products.4
  53.6 3.1 %pair_products.5 = bf16[4,128,512]{2,1,0:T(8,128)(2,1)S(1)} custom-call(s32[1]{0:T(128)} %bitcast.me_ref, bf16[5,256,192]{2,1,0:T(8,128)(2,1)S(1)} %fusion.pick_ref, bf16[64,3072]{1,0:T(8,128)(2,1)S(1)} %copy-done.1, bf16[64,3072]{1,0:T(8,128)(2,1)S(1)} %collective-permute-done.4.refs_1_, bf16[64,3072]{1,0:T(8,128)(2,1)S(1)} %collective-permute-done.5.refs_2_, ...), custom_call_target="tpu_custom_call" | custom-call | tf_op jit(solution)/shard_map/pair_products/pallas_call | solution.py:110
  57.6 2.8 %collective-permute-done.12.refs_3_ = bf16[64,3072]{1,0:T(8,128)(2,1)S(1)} collective-permute-done((bf16[64,3072]{1,0:T(8,128)(2,1)S(1)}, bf16[64,3072]{1,0:T(8,128)(2,1)S(1)}, u32[]{:S(2)}, u32[]{:S(2)}) %collective-permute-start.12) | collective-permute-done | bytes 393248 | tf_op jit(solution)/shard_map/ppermute | solution.py:216
  61.2 1.9 %collective-permute-start.14 = (bf16[64,3072]{1,0:T(8,128)(2,1)}, bf16[64,3072]{1,0:T(8,128)(2,1)}, u32[]{:S(2)}, u32[]{:S(2)}) collective-permute-start(bf16[64,3072]{1,0:T(8,128)(2,1)} %broadcast_select_fusion), channel_id=1, source_target_pairs={{0,32},{8,232},{32,64},{40,8},{64,96},{72,40},{96,128},{104,72},{1... | collective-permute-start | bytes 1179656 | tf_op jit(solution)/shard_map/ppermute | solution.py:231
  64.0 6.9 %all-to-all-start = ((bf16[32,16,512]{2,1,0:T(8,128)(2,1)}), bf16[32,16,512]{2,1,0:T(8,128)(2,1)S(1)}, u32[]{:S(2)}, u32[]{:S(2)}) async-start(bf16[32,16,512]{2,1,0:T(8,128)(2,1)} %bitcast.12), calls=%async_computation | async-start | bytes 1048576 | tf_op jit(solution)/shard_map/all_to_all | solution.py:243
  70.9 1.8 %pair_products.6 = bf16[1,128,512]{2,1,0:T(8,128)(2,1)S(1)} custom-call(s32[1]{0:T(128)} %bitcast.me_ref, bf16[5,256,192]{2,1,0:T(8,128)(2,1)S(1)} %fusion.pick_ref, bf16[64,3072]{1,0:T(8,128)(2,1)S(1)} %copy-done, bf16[64,3072]{1,0:T(8,128)(2,1)S(1)} %collective-permute-done.11.refs_1_, bf16[64,3072]{1,0:T(8,128)(2,1)S(1)} %collective-permute-done.10.refs_2_, ...), custom_call_target="tpu_custom_call" | custom-call | tf_op jit(solution)/shard_map/pair_products/pallas_call | solution.py:110
  72.9 3.0 %pair_products.7 = bf16[4,128,512]{2,1,0:T(8,128)(2,1)S(1)} custom-call(s32[1]{0:T(128)} %bitcast.me_ref, bf16[5,256,192]{2,1,0:T(8,128)(2,1)S(1)} %fusion.pick_ref, bf16[64,3072]{1,0:T(8,128)(2,1)S(1)} %copy-done, bf16[64,3072]{1,0:T(8,128)(2,1)S(1)} %collective-permute-done.11.refs_1_, bf16[64,3072]{1,0:T(8,128)(2,1)S(1)} %collective-permute-done.10.refs_2_, ...), custom_call_target="tpu_custom_call" | custom-call | tf_op jit(solution)/shard_map/pair_products/pallas_call | solution.py:110
  75.9 3.7 %collective-permute-done.15 = bf16[1,128,512]{2,1,0:T(8,128)(2,1)S(1)} collective-permute-done((bf16[1,128,512]{2,1,0:T(8,128)(2,1)S(1)}, bf16[1,128,512]{2,1,0:T(8,128)(2,1)S(1)}, u32[]{:S(2)}, u32[]{:S(2)}) %collective-permute-start.15) | collective-permute-done | bytes 131104 | tf_op jit(solution)/shard_map/ppermute | solution.py:234
  79.6 3.2 %all-to-all-done.refs_0_ = bf16[32,16,512]{2,1,0:T(8,128)(2,1)S(1)} async-done(((bf16[32,16,512]{2,1,0:T(8,128)(2,1)}), bf16[32,16,512]{2,1,0:T(8,128)(2,1)S(1)}, u32[]{:S(2)}, u32[]{:S(2)}) %all-to-all-start) | async-done | bytes 524320 | tf_op jit(solution)/shard_map/all_to_all | solution.py:243
  82.9 15.9 %all_to_all.18.refs_1_ = bf16[32,16,512]{2,1,0:T(8,128)(2,1)S(1)} all-to-all(bf16[32,16,512]{2,1,0:T(8,128)(2,1)S(1)} %bitcast.13), channel_id=1, replica_groups=mesh['z'=8,'y'=2,'c'=2,'h'=8] {'y','c','h'}, dimensions={0} | all-to-all | bytes 1048576 | tf_op jit(solution)/shard_map/all_to_all | solution.py:243
  98.8 1.6 %lag_sums.1 = f32[16,2432]{1,0:T(8,128)} custom-call(f32[19,2048]{1,0:T(8,128)S(1)} %copy-done.4, f32[19,2048]{1,0:T(8,128)S(1)} %copy-done.3, bf16[4096,128]{1,0:T(8,128)(2,1)S(1)} %copy-done.2, bf16[32,16,512]{2,1,0:T(8,128)(2,1)S(1)} %all-to-all-done.refs_0_, bf16[32,16,512]{2,1,0:T(8,128)(2,1)S(1)} %all_to_all.18.refs_1_), custom_call_target="tpu_custom_call" | custom-call | tf_op jit(solution)/shard_map/lag_sums/pallas_call | solution.py:157
  (50 shorter events, 6.3 us)
Async XLA Ops:
  1.5 4.7 %collective-permute-start.2 = (s32[1,256]{1,0:T(1,128)S(1)}, s32[1,256]{1,0:T(1,128)S(1)}, u32[]{:S(2)}, u32[]{:S(2)}) collective-permute-start(s32[1,256]{1,0:T(1,128)S(1)} %bitcast_select_fusion), channel_id=1, source_target_pairs={{0,24},{8,16},{16,8},{24,0},{1,25},{9,17},{17,9},{25,1},{2,26},{10... | collective-permute-start | bytes 3080 | tf_op jit(solution)/shard_map/ppermute | solution.py:200
  4.2 3.2 %collective-permute-start.1 = (s32[1,256]{1,0:T(1,128)S(1)}, s32[1,256]{1,0:T(1,128)S(1)}, u32[]{:S(2)}, u32[]{:S(2)}) collective-permute-start(s32[1,256]{1,0:T(1,128)S(1)} %bitcast_select_fusion), channel_id=1, source_target_pairs={{0,16},{8,24},{16,0},{24,8},{1,17},{9,25},{17,1},{25,9},{2,18},{10... | collective-permute-start | bytes 3080 | tf_op jit(solution)/shard_map/ppermute | solution.py:200
  6.1 1.3 %collective-permute-start = (s32[1,256]{1,0:T(1,128)S(1)}, s32[1,256]{1,0:T(1,128)S(1)}, u32[]{:S(2)}, u32[]{:S(2)}) collective-permute-start(s32[1,256]{1,0:T(1,128)S(1)} %bitcast_select_fusion), channel_id=1, source_target_pairs={{0,8},{8,0},{16,24},{24,16},{1,9},{9,1},{17,25},{25,17},{2,10},{10... | collective-permute-start | bytes 3080 | tf_op jit(solution)/shard_map/ppermute | solution.py:200
  7.4 14.2 %collective-permute-start.3 = (s32[1,256]{1,0:T(1,128)S(1)}, s32[1,256]{1,0:T(1,128)S(1)}, u32[]{:S(2)}, u32[]{:S(2)}) collective-permute-start(s32[1,256]{1,0:T(1,128)S(1)} %constant_dynamic-slice_fusion), channel_id=1, source_target_pairs={{32,0},{64,32},{96,64},{128,96},{160,128},{192,160},{224,192},{0,2... | collective-permute-start | bytes 3080 | tf_op jit(solution)/shard_map/ppermute | solution.py:202
  18.7 9.5 %collective-permute-start.4 = (bf16[64,3072]{1,0:T(8,128)(2,1)}, bf16[64,3072]{1,0:T(8,128)(2,1)S(1)}, u32[]{:S(2)}, u32[]{:S(2)}) collective-permute-start(bf16[64,3072]{1,0:T(8,128)(2,1)} %get-tuple-element.35), channel_id=1, source_target_pairs={{0,8},{8,0},{16,24},{24,16},{1,9},{9,1},{17,25},{25,17},{2,10},{10... | collective-permute-start | bytes 1179656 | tf_op jit(solution)/shard_map/ppermute | solution.py:216
  19.9 20.3 %collective-permute-start.5 = (bf16[64,3072]{1,0:T(8,128)(2,1)}, bf16[64,3072]{1,0:T(8,128)(2,1)S(1)}, u32[]{:S(2)}, u32[]{:S(2)}) collective-permute-start(bf16[64,3072]{1,0:T(8,128)(2,1)} %get-tuple-element.36), channel_id=1, source_target_pairs={{0,16},{8,24},{16,0},{24,8},{1,17},{9,25},{17,1},{25,9},{2,18},{10... | collective-permute-start | bytes 1179656 | tf_op jit(solution)/shard_map/ppermute | solution.py:216
  20.3 19.1 %collective-permute-start.6 = (bf16[64,3072]{1,0:T(8,128)(2,1)}, bf16[64,3072]{1,0:T(8,128)(2,1)S(1)}, u32[]{:S(2)}, u32[]{:S(2)}) collective-permute-start(bf16[64,3072]{1,0:T(8,128)(2,1)} %get-tuple-element.41), channel_id=1, source_target_pairs={{0,24},{8,16},{16,8},{24,0},{1,25},{9,17},{17,9},{25,1},{2,26},{10... | collective-permute-start | bytes 1179656 | tf_op jit(solution)/shard_map/ppermute | solution.py:216
  28.2 12.1 %copy-start.1 = (bf16[64,3072]{1,0:T(8,128)(2,1)S(1)}, bf16[64,3072]{1,0:T(8,128)(2,1)}, u32[]{:S(2)}) copy-start(bf16[64,3072]{1,0:T(8,128)(2,1)} %get-tuple-element.34.refs_0_) | copy-start | bytes 1179652
  28.2 12.9 %copy-start.7 = (bf16[64,3072]{1,0:T(8,128)(2,1)S(1)}, bf16[64,3072]{1,0:T(8,128)(2,1)}, u32[]{:S(2)}) copy-start(bf16[64,3072]{1,0:T(8,128)(2,1)} %get-tuple-element.43) | copy-start | bytes 1179652
  28.2 13.3 %copy-start.6 = (bf16[64,3072]{1,0:T(8,128)(2,1)S(1)}, bf16[64,3072]{1,0:T(8,128)(2,1)}, u32[]{:S(2)}) copy-start(bf16[64,3072]{1,0:T(8,128)(2,1)} %get-tuple-element.46) | copy-start | bytes 1179652
  28.2 15.7 %copy-start.5 = (bf16[64,3072]{1,0:T(8,128)(2,1)S(1)}, bf16[64,3072]{1,0:T(8,128)(2,1)}, u32[]{:S(2)}) copy-start(bf16[64,3072]{1,0:T(8,128)(2,1)} %get-tuple-element.48) | copy-start | bytes 1179652
  39.4 10.3 %collective-permute-start.8 = (bf16[64,3072]{1,0:T(8,128)(2,1)S(1)}, bf16[64,3072]{1,0:T(8,128)(2,1)S(1)}, u32[]{:S(2)}, u32[]{:S(2)}) collective-permute-start(bf16[64,3072]{1,0:T(8,128)(2,1)S(1)} %broadcast_select_fusion.2), channel_id=1, source_target_pairs={{0,32},{8,232},{32,64},{40,8},{64,96},{72,40},{96,128},{104,72},{1... | collective-permute-start | bytes 1179656 | tf_op jit(solution)/shard_map/ppermute | solution.py:231
  40.3 12.2 %collective-permute-start.7 = (bf16[64,3072]{1,0:T(8,128)(2,1)S(1)}, bf16[64,3072]{1,0:T(8,128)(2,1)S(1)}, u32[]{:S(2)}, u32[]{:S(2)}) collective-permute-start(bf16[64,3072]{1,0:T(8,128)(2,1)S(1)} %broadcast_select_fusion.3), channel_id=1, source_target_pairs={{0,224},{8,40},{32,0},{40,72},{64,32},{72,104},{96,64},{104,136},{... | collective-permute-start | bytes 1179656 | tf_op jit(solution)/shard_map/ppermute | solution.py:230
  41.1 15.6 %collective-permute-start.10 = (bf16[64,3072]{1,0:T(8,128)(2,1)S(1)}, bf16[64,3072]{1,0:T(8,128)(2,1)S(1)}, u32[]{:S(2)}, u32[]{:S(2)}) collective-permute-start(bf16[64,3072]{1,0:T(8,128)(2,1)S(1)} %copy-done.7), channel_id=1, source_target_pairs={{0,16},{8,24},{16,0},{24,8},{1,17},{9,25},{17,1},{25,9},{2,18},{10... | collective-permute-start | bytes 1179656 | tf_op jit(solution)/shard_map/ppermute | solution.py:216
  41.5 16.1 %collective-permute-start.11 = (bf16[64,3072]{1,0:T(8,128)(2,1)S(1)}, bf16[64,3072]{1,0:T(8,128)(2,1)S(1)}, u32[]{:S(2)}, u32[]{:S(2)}) collective-permute-start(bf16[64,3072]{1,0:T(8,128)(2,1)S(1)} %copy-done.6), channel_id=1, source_target_pairs={{0,8},{8,0},{16,24},{24,16},{1,9},{9,1},{17,25},{25,17},{2,10},{10... | collective-permute-start | bytes 1179656 | tf_op jit(solution)/shard_map/ppermute | solution.py:216
  43.8 16.6 %collective-permute-start.12 = (bf16[64,3072]{1,0:T(8,128)(2,1)S(1)}, bf16[64,3072]{1,0:T(8,128)(2,1)S(1)}, u32[]{:S(2)}, u32[]{:S(2)}) collective-permute-start(bf16[64,3072]{1,0:T(8,128)(2,1)S(1)} %copy-done.5), channel_id=1, source_target_pairs={{0,24},{8,16},{16,8},{24,0},{1,25},{9,17},{17,9},{25,1},{2,26},{10... | collective-permute-start | bytes 1179656 | tf_op jit(solution)/shard_map/ppermute | solution.py:216
  53.5 9.6 %collective-permute-start.9 = (bf16[1,128,512]{2,1,0:T(8,128)(2,1)S(1)}, bf16[1,128,512]{2,1,0:T(8,128)(2,1)S(1)}, u32[]{:S(2)}, u32[]{:S(2)}) collective-permute-start(bf16[1,128,512]{2,1,0:T(8,128)(2,1)S(1)} %pair_products.4), channel_id=1, source_target_pairs={{0,32},{32,64},{64,96},{96,128},{128,160},{160,192},{192,224},{224... | collective-permute-start | bytes 393224 | tf_op jit(solution)/shard_map/ppermute | solution.py:234
  57.6 13.4 %collective-permute-start.13 = (bf16[64,3072]{1,0:T(8,128)(2,1)}, bf16[64,3072]{1,0:T(8,128)(2,1)S(1)}, u32[]{:S(2)}, u32[]{:S(2)}) collective-permute-start(bf16[64,3072]{1,0:T(8,128)(2,1)} %broadcast_select_fusion.1), channel_id=1, source_target_pairs={{0,224},{8,40},{32,0},{40,72},{64,32},{72,104},{96,64},{104,136},{... | collective-permute-start | bytes 1179656 | tf_op jit(solution)/shard_map/ppermute | solution.py:230
  61.2 9.7 %collective-permute-start.14 = (bf16[64,3072]{1,0:T(8,128)(2,1)}, bf16[64,3072]{1,0:T(8,128)(2,1)}, u32[]{:S(2)}, u32[]{:S(2)}) collective-permute-start(bf16[64,3072]{1,0:T(8,128)(2,1)} %broadcast_select_fusion), channel_id=1, source_target_pairs={{0,32},{8,232},{32,64},{40,8},{64,96},{72,40},{96,128},{104,72},{1... | collective-permute-start | bytes 1179656 | tf_op jit(solution)/shard_map/ppermute | solution.py:231
  64.0 18.9 %all-to-all-start = ((bf16[32,16,512]{2,1,0:T(8,128)(2,1)}), bf16[32,16,512]{2,1,0:T(8,128)(2,1)S(1)}, u32[]{:S(2)}, u32[]{:S(2)}) async-start(bf16[32,16,512]{2,1,0:T(8,128)(2,1)} %bitcast.12), calls=%async_computation | async-start | bytes 1048576 | tf_op jit(solution)/shard_map/all_to_all | solution.py:243
  72.8 6.8 %collective-permute-start.15 = (bf16[1,128,512]{2,1,0:T(8,128)(2,1)S(1)}, bf16[1,128,512]{2,1,0:T(8,128)(2,1)S(1)}, u32[]{:S(2)}, u32[]{:S(2)}) collective-permute-start(bf16[1,128,512]{2,1,0:T(8,128)(2,1)S(1)} %pair_products.6), channel_id=1, source_target_pairs={{0,32},{32,64},{64,96},{96,128},{128,160},{160,192},{192,224},{224... | collective-permute-start | bytes 393224 | tf_op jit(solution)/shard_map/ppermute | solution.py:234
  75.8 22.9 %copy-start.2 = (bf16[4096,128]{1,0:T(8,128)(2,1)S(1)}, bf16[4096,128]{1,0:T(8,128)(2,1)}, u32[]{:S(2)}) copy-start(bf16[4096,128]{1,0:T(8,128)(2,1)} %constant.36.clone.table_ref) | copy-start | bytes 3145732
  75.8 22.9 %copy-start.3 = (f32[19,2048]{1,0:T(8,128)S(1)}, f32[19,2048]{1,0:T(8,128)}, u32[]{:S(2)}) copy-start(f32[19,2048]{1,0:T(8,128)} %constant.35.clone.sin_ref) | copy-start | bytes 466948
  75.9 22.9 %copy-start.4 = (f32[19,2048]{1,0:T(8,128)S(1)}, f32[19,2048]{1,0:T(8,128)}, u32[]{:S(2)}) copy-start(f32[19,2048]{1,0:T(8,128)} %constant.34.clone.cos_ref) | copy-start | bytes 466948
  (1 other events, 3.3 us)

commit v7 on v5

--- a/solution.py
+++ b/solution.py
@@ -199,12 +199,6 @@
     spectra, rows = lax.optimization_barrier((spectra, rows))
     near = [rows] + [lax.ppermute(rows, ("y", "c"), yc_pairs[m]) for m in (1, 2, 3)]
     near = jnp.concatenate(near)
-    above = lax.ppermute(lax.dynamic_slice_in_dim(near, me[0], 1, 0), "z", z_down)
-    is_first = (jnp.arange(256) < 128)[None]
-    above = jnp.where(is_first | (above < 64), above, -1)
-    column = jnp.arange(192, dtype=jnp.int32)
-    picks = (jnp.concatenate([near, above])[:, :, None] == column).astype(jnp.bfloat16)
-
     arrived = []
     for chunk in range(CHUNKS):
         pieces = whiten(me, spectra, chunk)
@@ -213,6 +207,13 @@
         arrived.append(
             [pieces[0]] + [lax.ppermute(pieces[m], ("y", "c"), yc_pairs[m]) for m in (2, 3, 1)]
         )
+    near = lax.optimization_barrier((near, arrived[1][0]))[0]
+    above = lax.ppermute(lax.dynamic_slice_in_dim(near, me[0], 1, 0), "z", z_down)
+    is_first = (jnp.arange(256) < 128)[None]
+    above = jnp.where(is_first | (above < 64), above, -1)
+    column = jnp.arange(192, dtype=jnp.int32)
+    picks = (jnp.concatenate([near, above])[:, :, None] == column).astype(jnp.bfloat16)
+
     products, moved = [], []
     for chunk in range(CHUNKS):
         own, far, cross, side = arrived[chunk]

time: 96.3 us -> 95.4 us (level)
  Pallas kernels: 23.9 us -> 22.3 us
  other arithmetic: 5.21 us -> 3.64 us
  blocking collectives: 15.5 us -> 16.5 us
    ppermute x2, waiting for transfers between devices: 4.66 us -> 7.23 us  [on_device(): lax.ppermute(moved[-1], ('z', 'c'), one_way)]
    pallas_call x4, Pallas kernels: 9.65 us -> 8.06 us  [pair_products(): pl.pallas_call(functools.partial(pair_kernel, numbers), in_specs=[pl.Bloc...]
    ppermute x2, waiting for transfers between devices: 4.03 us -> 2.69 us  [on_device(): lax.ppermute(jnp.where(y == c, cross, side), ('z', 'c'), other_way)]
    all_to_all x1, waiting for transfers between devices: 4.03 us -> 2.7 us  [on_device(): lax.all_to_all(product, ('y', 'c', 'h'), 0, 0, tiled=True)]
    all_to_all x1, blocking collectives: 15.5 us -> 16.5 us  [on_device(): lax.all_to_all(product, ('y', 'c', 'h'), 0, 0, tiled=True)]
    ppermute x6, starting transfers between devices: 3.74 us -> 4.7 us  [on_device(): lax.ppermute(pieces[m], ('y', 'c'), yc_pairs[m])]
  transfers between devices with their start and end apart: 17 -> 17, of which waited for: 6 -> 6; matrix products, arithmetic and copies ran while one was open for 5% -> 3% of each run, Pallas kernels for 23% -> 22%
where the time goes in v7:
time: 95.4 us; the launch traced here: 95.1 us
  starting transfers between devices  29 us (30%)
  Pallas kernels  22.3 us (23%)
  waiting for transfers between devices  21.7 us (23%)
  blocking collectives  16.5 us (17%)
  other arithmetic  3.64 us (4%)
  local copies, waits for them, and re-layouts  1.06 us (1%)
    all_to_all x1, blocking collectives, on_device(): lax.all_to_all(product, ('y', 'c', 'h'), 0, 0, tiled=True)  16.5 us
    pallas_call x2, Pallas kernels, whiten(): pl.pallas_call(whiten_kernel, grid_spec=pltpu.PrefetchScalarGridSpec(num_...  12.6 us
    all_to_all x1, starting transfers between devices, on_device(): lax.all_to_all(product, ('y', 'c', 'h'), 0, 0, tiled=True)  8.21 us
    pallas_call x4, Pallas kernels, pair_products(): pl.pallas_call(functools.partial(pair_kernel, numbers), in_specs=[pl.Bloc...  8.06 us
    ppermute x2, starting transfers between devices, on_device(): lax.ppermute(jnp.where(y == c, cross, side), ('z', 'c'), other_way)  7.28 us
    ppermute x2, waiting for transfers between devices, on_device(): lax.ppermute(moved[-1], ('z', 'c'), one_way)  7.23 us
    ppermute x6, waiting for transfers between devices, on_device(): lax.ppermute(pieces[m], ('y', 'c'), yc_pairs[m])  5.5 us
    ppermute x6, starting transfers between devices, on_device(): lax.ppermute(pieces[m], ('y', 'c'), yc_pairs[m])  4.7 us
  transfers between devices with their start and end apart: 17, of which 6 were waited for; matrix products, arithmetic and copies ran while one was open for 3% of the time, Pallas kernels for 22%

profile of v7, /device:TPU:1, one launch (start us, length us, event | category | flops | bytes accessed | tf_op | source)
XLA Modules:
  0.0 95.1 jit_solution(2772353428006812527)
XLA Ops:
  1.5 2.8 %collective-permute-start.2 = (s32[1,256]{1,0:T(1,128)S(1)}, s32[1,256]{1,0:T(1,128)S(1)}, u32[]{:S(2)}, u32[]{:S(2)}) collective-permute-start(s32[1,256]{1,0:T(1,128)S(1)} %bitcast_select_fusion), channel_id=1, source_target_pairs={{0,24},{8,16},{16,8},{24,0},{1,25},{9,17},{17,9},{25,1},{2,26},{10... | collective-permute-start | bytes 3080 | tf_op jit(solution)/shard_map/ppermute | solution.py:200
  4.2 1.9 %collective-permute-start.1 = (s32[1,256]{1,0:T(1,128)S(1)}, s32[1,256]{1,0:T(1,128)S(1)}, u32[]{:S(2)}, u32[]{:S(2)}) collective-permute-start(s32[1,256]{1,0:T(1,128)S(1)} %bitcast_select_fusion), channel_id=1, source_target_pairs={{0,16},{8,24},{16,0},{24,8},{1,17},{9,25},{17,1},{25,9},{2,18},{10... | collective-permute-start | bytes 3080 | tf_op jit(solution)/shard_map/ppermute | solution.py:200
  6.1 6.3 %whiten.2 = (bf16[64,3072]{1,0:T(8,128)(2,1)}, bf16[64,3072]{1,0:T(8,128)(2,1)}, bf16[64,3072]{1,0:T(8,128)(2,1)}, bf16[64,3072]{1,0:T(8,128)(2,1)}) custom-call(s32[1]{0:T(128)} %bitcast.me_ref, bf16[64,6,2,2048]{3,2,1,0:T(2,128)(2,1)} %x_ref.1), custom_call_target="tpu_custom_call" | custom-call | tf_op jit(solution)/shard_map/whiten/pallas_call | solution.py:52
  13.4 1.4 %collective-permute-start.6 = (bf16[64,3072]{1,0:T(8,128)(2,1)}, bf16[64,3072]{1,0:T(8,128)(2,1)S(1)}, u32[]{:S(2)}, u32[]{:S(2)}) collective-permute-start(bf16[64,3072]{1,0:T(8,128)(2,1)} %get-tuple-element.41), channel_id=1, source_target_pairs={{0,24},{8,16},{16,8},{24,0},{1,25},{9,17},{17,9},{25,1},{2,26},{10... | collective-permute-start | bytes 1179656 | tf_op jit(solution)/shard_map/ppermute | solution.py:208
  14.7 6.3 %whiten.3 = (bf16[64,3072]{1,0:T(8,128)(2,1)}, bf16[64,3072]{1,0:T(8,128)(2,1)}, bf16[64,3072]{1,0:T(8,128)(2,1)}, bf16[64,3072]{1,0:T(8,128)(2,1)}) custom-call(s32[1]{0:T(128)} %bitcast.me_ref, bf16[64,6,2,2048]{3,2,1,0:T(2,128)(2,1)} %x_ref.1), custom_call_target="tpu_custom_call" | custom-call | tf_op jit(solution)/shard_map/whiten/pallas_call | solution.py:52
  21.0 4.0 %collective-permute-start.3 = (s32[1,256]{1,0:T(1,128)S(1)}, s32[1,256]{1,0:T(1,128)S(1)}, u32[]{:S(2)}, u32[]{:S(2)}) collective-permute-start(s32[1,256]{1,0:T(1,128)S(1)} %constant_dynamic-slice_fusion), channel_id=1, source_target_pairs={{32,0},{64,32},{96,64},{128,96},{160,128},{192,160},{224,192},{0,2... | collective-permute-start | bytes 3080 | tf_op jit(solution)/shard_map/ppermute | solution.py:211
  25.0 1.3 %collective-permute-start.10 = (bf16[64,3072]{1,0:T(8,128)(2,1)}, bf16[64,3072]{1,0:T(8,128)(2,1)S(1)}, u32[]{:S(2)}, u32[]{:S(2)}) collective-permute-start(bf16[64,3072]{1,0:T(8,128)(2,1)} %get-tuple-element.43), channel_id=1, source_target_pairs={{0,16},{8,24},{16,0},{24,8},{1,17},{9,25},{17,1},{25,9},{2,18},{10... | collective-permute-start | bytes 1179656 | tf_op jit(solution)/shard_map/ppermute | solution.py:208
  26.2 1.1 %collective-permute-start.11 = (bf16[64,3072]{1,0:T(8,128)(2,1)}, bf16[64,3072]{1,0:T(8,128)(2,1)S(1)}, u32[]{:S(2)}, u32[]{:S(2)}) collective-permute-start(bf16[64,3072]{1,0:T(8,128)(2,1)} %get-tuple-element.46), channel_id=1, source_target_pairs={{0,8},{8,0},{16,24},{24,16},{1,9},{9,1},{17,25},{25,17},{2,10},{10... | collective-permute-start | bytes 1179656 | tf_op jit(solution)/shard_map/ppermute | solution.py:208
  27.5 5.5 %collective-permute-done.6.refs_3_ = bf16[64,3072]{1,0:T(8,128)(2,1)S(1)} collective-permute-done((bf16[64,3072]{1,0:T(8,128)(2,1)}, bf16[64,3072]{1,0:T(8,128)(2,1)S(1)}, u32[]{:S(2)}, u32[]{:S(2)}) %collective-permute-start.6) | collective-permute-done | bytes 393248 | tf_op jit(solution)/shard_map/ppermute | solution.py:208
  33.1 3.9 %collective-permute-start.8 = (bf16[64,3072]{1,0:T(8,128)(2,1)S(1)}, bf16[64,3072]{1,0:T(8,128)(2,1)S(1)}, u32[]{:S(2)}, u32[]{:S(2)}) collective-permute-start(bf16[64,3072]{1,0:T(8,128)(2,1)S(1)} %broadcast_select_fusion.2), channel_id=1, source_target_pairs={{0,32},{8,232},{32,64},{40,8},{64,96},{72,40},{96,128},{104,72},{1... | collective-permute-start | bytes 1179656 | tf_op jit(solution)/shard_map/ppermute | solution.py:228
  37.2 5.7 %collective-permute-done.7.refs_4_ = bf16[64,3072]{1,0:T(8,128)(2,1)S(1)} collective-permute-done((bf16[64,3072]{1,0:T(8,128)(2,1)S(1)}, bf16[64,3072]{1,0:T(8,128)(2,1)S(1)}, u32[]{:S(2)}, u32[]{:S(2)}) %collective-permute-start.7) | collective-permute-done | bytes 393248 | tf_op jit(solution)/shard_map/ppermute | solution.py:227
  42.9 2.7 %collective-permute-done.8.refs_5_ = bf16[64,3072]{1,0:T(8,128)(2,1)S(1)} collective-permute-done((bf16[64,3072]{1,0:T(8,128)(2,1)S(1)}, bf16[64,3072]{1,0:T(8,128)(2,1)S(1)}, u32[]{:S(2)}, u32[]{:S(2)}) %collective-permute-start.8) | collective-permute-done | bytes 393248 | tf_op jit(solution)/shard_map/ppermute | solution.py:228
  45.6 1.0 %pair_products.4 = bf16[1,128,512]{2,1,0:T(8,128)(2,1)S(1)} custom-call(s32[1]{0:T(128)} %bitcast.me_ref, bf16[5,256,192]{2,1,0:T(8,128)(2,1)S(1)} %fusion.pick_ref, bf16[64,3072]{1,0:T(8,128)(2,1)S(1)} %copy-done.1, bf16[64,3072]{1,0:T(8,128)(2,1)S(1)} %collective-permute-done.4.refs_1_, bf16[64,3072]{1,0:T(8,128)(2,1)S(1)} %collective-permute-done.5.refs_2_, ...), custom_call_target="tpu_custom_call" | custom-call | tf_op jit(solution)/shard_map/pair_products/pallas_call | solution.py:110
  46.8 1.0 %copy-done.3 = bf16[64,3072]{1,0:T(8,128)(2,1)S(1)} copy-done((bf16[64,3072]{1,0:T(8,128)(2,1)S(1)}, bf16[64,3072]{1,0:T(8,128)(2,1)}, u32[]{:S(2)}) %copy-start.3) | copy-done | bytes 393240
  47.8 3.1 %pair_products.5 = bf16[4,128,512]{2,1,0:T(8,128)(2,1)S(1)} custom-call(s32[1]{0:T(128)} %bitcast.me_ref, bf16[5,256,192]{2,1,0:T(8,128)(2,1)S(1)} %fusion.pick_ref, bf16[64,3072]{1,0:T(8,128)(2,1)S(1)} %copy-done.1, bf16[64,3072]{1,0:T(8,128)(2,1)S(1)} %collective-permute-done.4.refs_1_, bf16[64,3072]{1,0:T(8,128)(2,1)S(1)} %collective-permute-done.5.refs_2_, ...), custom_call_target="tpu_custom_call" | custom-call | tf_op jit(solution)/shard_map/pair_products/pallas_call | solution.py:110
  52.5 3.4 %collective-permute-start.14 = (bf16[64,3072]{1,0:T(8,128)(2,1)}, bf16[64,3072]{1,0:T(8,128)(2,1)S(1)}, u32[]{:S(2)}, u32[]{:S(2)}) collective-permute-start(bf16[64,3072]{1,0:T(8,128)(2,1)} %broadcast_select_fusion), channel_id=1, source_target_pairs={{0,32},{8,232},{32,64},{40,8},{64,96},{72,40},{96,128},{104,72},{1... | collective-permute-start | bytes 1179656 | tf_op jit(solution)/shard_map/ppermute | solution.py:228
  56.8 8.2 %all-to-all-start = ((bf16[32,16,512]{2,1,0:T(8,128)(2,1)}), bf16[32,16,512]{2,1,0:T(8,128)(2,1)S(1)}, u32[]{:S(2)}, u32[]{:S(2)}) async-start(bf16[32,16,512]{2,1,0:T(8,128)(2,1)} %bitcast.12), calls=%async_computation | async-start | bytes 1048576 | tf_op jit(solution)/shard_map/all_to_all | solution.py:240
  65.0 1.5 %collective-permute-done.13.refs_4_ = bf16[64,3072]{1,0:T(8,128)(2,1)S(1)} collective-permute-done((bf16[64,3072]{1,0:T(8,128)(2,1)}, bf16[64,3072]{1,0:T(8,128)(2,1)S(1)}, u32[]{:S(2)}, u32[]{:S(2)}) %collective-permute-start.13) | collective-permute-done | bytes 393248 | tf_op jit(solution)/shard_map/ppermute | solution.py:227
  66.5 1.0 %pair_products.6 = bf16[1,128,512]{2,1,0:T(8,128)(2,1)S(1)} custom-call(s32[1]{0:T(128)} %bitcast.me_ref, bf16[5,256,192]{2,1,0:T(8,128)(2,1)S(1)} %fusion.pick_ref, bf16[64,3072]{1,0:T(8,128)(2,1)S(1)} %copy-done, bf16[64,3072]{1,0:T(8,128)(2,1)S(1)} %collective-permute-done.11.refs_1_, bf16[64,3072]{1,0:T(8,128)(2,1)S(1)} %collective-permute-done.10.refs_2_, ...), custom_call_target="tpu_custom_call" | custom-call | tf_op jit(solution)/shard_map/pair_products/pallas_call | solution.py:110
  67.6 3.0 %pair_products.7 = bf16[4,128,512]{2,1,0:T(8,128)(2,1)S(1)} custom-call(s32[1]{0:T(128)} %bitcast.me_ref, bf16[5,256,192]{2,1,0:T(8,128)(2,1)S(1)} %fusion.pick_ref, bf16[64,3072]{1,0:T(8,128)(2,1)S(1)} %copy-done, bf16[64,3072]{1,0:T(8,128)(2,1)S(1)} %collective-permute-done.11.refs_1_, bf16[64,3072]{1,0:T(8,128)(2,1)S(1)} %collective-permute-done.10.refs_2_, ...), custom_call_target="tpu_custom_call" | custom-call | tf_op jit(solution)/shard_map/pair_products/pallas_call | solution.py:110
  70.6 3.6 %collective-permute-done.15 = bf16[1,128,512]{2,1,0:T(8,128)(2,1)S(1)} collective-permute-done((bf16[1,128,512]{2,1,0:T(8,128)(2,1)S(1)}, bf16[1,128,512]{2,1,0:T(8,128)(2,1)S(1)}, u32[]{:S(2)}, u32[]{:S(2)}) %collective-permute-start.15) | collective-permute-done | bytes 131104 | tf_op jit(solution)/shard_map/ppermute | solution.py:231
  74.3 2.7 %all-to-all-done.refs_0_ = bf16[32,16,512]{2,1,0:T(8,128)(2,1)S(1)} async-done(((bf16[32,16,512]{2,1,0:T(8,128)(2,1)}), bf16[32,16,512]{2,1,0:T(8,128)(2,1)S(1)}, u32[]{:S(2)}, u32[]{:S(2)}) %all-to-all-start) | async-done | bytes 524320 | tf_op jit(solution)/shard_map/all_to_all | solution.py:240
  77.0 16.5 %all_to_all.18.refs_1_ = bf16[32,16,512]{2,1,0:T(8,128)(2,1)S(1)} all-to-all(bf16[32,16,512]{2,1,0:T(8,128)(2,1)S(1)} %bitcast.13), channel_id=1, replica_groups=mesh['z'=8,'y'=2,'c'=2,'h'=8] {'y','c','h'}, dimensions={0} | all-to-all | bytes 1048576 | tf_op jit(solution)/shard_map/all_to_all | solution.py:240
  93.5 1.6 %lag_sums.1 = f32[16,2432]{1,0:T(8,128)} custom-call(f32[19,2048]{1,0:T(8,128)S(1)} %copy-done.6, f32[19,2048]{1,0:T(8,128)S(1)} %copy-done.5, bf16[4096,128]{1,0:T(8,128)(2,1)S(1)} %copy-done.4, bf16[32,16,512]{2,1,0:T(8,128)(2,1)S(1)} %all-to-all-done.refs_0_, bf16[32,16,512]{2,1,0:T(8,128)(2,1)S(1)} %all_to_all.18.refs_1_), custom_call_target="tpu_custom_call" | custom-call | tf_op jit(solution)/shard_map/lag_sums/pallas_call | solution.py:157
  (48 shorter events, 4.9 us)
Async XLA Ops:
  1.5 11.0 %collective-permute-start.2 = (s32[1,256]{1,0:T(1,128)S(1)}, s32[1,256]{1,0:T(1,128)S(1)}, u32[]{:S(2)}, u32[]{:S(2)}) collective-permute-start(s32[1,256]{1,0:T(1,128)S(1)} %bitcast_select_fusion), channel_id=1, source_target_pairs={{0,24},{8,16},{16,8},{24,0},{1,25},{9,17},{17,9},{25,1},{2,26},{10... | collective-permute-start | bytes 3080 | tf_op jit(solution)/shard_map/ppermute | solution.py:200
  4.2 8.2 %collective-permute-start.1 = (s32[1,256]{1,0:T(1,128)S(1)}, s32[1,256]{1,0:T(1,128)S(1)}, u32[]{:S(2)}, u32[]{:S(2)}) collective-permute-start(s32[1,256]{1,0:T(1,128)S(1)} %bitcast_select_fusion), channel_id=1, source_target_pairs={{0,16},{8,24},{16,0},{24,8},{1,17},{9,25},{17,1},{25,9},{2,18},{10... | collective-permute-start | bytes 3080 | tf_op jit(solution)/shard_map/ppermute | solution.py:200
  6.1 6.3 %collective-permute-start = (s32[1,256]{1,0:T(1,128)S(1)}, s32[1,256]{1,0:T(1,128)S(1)}, u32[]{:S(2)}, u32[]{:S(2)}) collective-permute-start(s32[1,256]{1,0:T(1,128)S(1)} %bitcast_select_fusion), channel_id=1, source_target_pairs={{0,8},{8,0},{16,24},{24,16},{1,9},{9,1},{17,25},{25,17},{2,10},{10... | collective-permute-start | bytes 3080 | tf_op jit(solution)/shard_map/ppermute | solution.py:200
  12.5 13.8 %collective-permute-start.5 = (bf16[64,3072]{1,0:T(8,128)(2,1)}, bf16[64,3072]{1,0:T(8,128)(2,1)S(1)}, u32[]{:S(2)}, u32[]{:S(2)}) collective-permute-start(bf16[64,3072]{1,0:T(8,128)(2,1)} %get-tuple-element.40), channel_id=1, source_target_pairs={{0,16},{8,24},{16,0},{24,8},{1,17},{9,25},{17,1},{25,9},{2,18},{10... | collective-permute-start | bytes 1179656 | tf_op jit(solution)/shard_map/ppermute | solution.py:208
  13.1 14.2 %copy-start.1 = (bf16[64,3072]{1,0:T(8,128)(2,1)S(1)}, bf16[64,3072]{1,0:T(8,128)(2,1)}, u32[]{:S(2)}) copy-start(bf16[64,3072]{1,0:T(8,128)(2,1)} %get-tuple-element.38.refs_0_) | copy-start | bytes 1179652
  13.1 14.3 %collective-permute-start.4 = (bf16[64,3072]{1,0:T(8,128)(2,1)}, bf16[64,3072]{1,0:T(8,128)(2,1)S(1)}, u32[]{:S(2)}, u32[]{:S(2)}) collective-permute-start(bf16[64,3072]{1,0:T(8,128)(2,1)} %get-tuple-element.39), channel_id=1, source_target_pairs={{0,8},{8,0},{16,24},{24,16},{1,9},{9,1},{17,25},{25,17},{2,10},{10... | collective-permute-start | bytes 1179656 | tf_op jit(solution)/shard_map/ppermute | solution.py:208
  13.4 19.6 %collective-permute-start.6 = (bf16[64,3072]{1,0:T(8,128)(2,1)}, bf16[64,3072]{1,0:T(8,128)(2,1)S(1)}, u32[]{:S(2)}, u32[]{:S(2)}) collective-permute-start(bf16[64,3072]{1,0:T(8,128)(2,1)} %get-tuple-element.41), channel_id=1, source_target_pairs={{0,24},{8,16},{16,8},{24,0},{1,25},{9,17},{17,9},{25,1},{2,26},{10... | collective-permute-start | bytes 1179656 | tf_op jit(solution)/shard_map/ppermute | solution.py:208
  21.0 12.0 %collective-permute-start.3 = (s32[1,256]{1,0:T(1,128)S(1)}, s32[1,256]{1,0:T(1,128)S(1)}, u32[]{:S(2)}, u32[]{:S(2)}) collective-permute-start(s32[1,256]{1,0:T(1,128)S(1)} %constant_dynamic-slice_fusion), channel_id=1, source_target_pairs={{32,0},{64,32},{96,64},{128,96},{160,128},{192,160},{224,192},{0,2... | collective-permute-start | bytes 3080 | tf_op jit(solution)/shard_map/ppermute | solution.py:211
  25.0 25.9 %collective-permute-start.10 = (bf16[64,3072]{1,0:T(8,128)(2,1)}, bf16[64,3072]{1,0:T(8,128)(2,1)S(1)}, u32[]{:S(2)}, u32[]{:S(2)}) collective-permute-start(bf16[64,3072]{1,0:T(8,128)(2,1)} %get-tuple-element.43), channel_id=1, source_target_pairs={{0,16},{8,24},{16,0},{24,8},{1,17},{9,25},{17,1},{25,9},{2,18},{10... | collective-permute-start | bytes 1179656 | tf_op jit(solution)/shard_map/ppermute | solution.py:208
  26.2 24.7 %collective-permute-start.11 = (bf16[64,3072]{1,0:T(8,128)(2,1)}, bf16[64,3072]{1,0:T(8,128)(2,1)S(1)}, u32[]{:S(2)}, u32[]{:S(2)}) collective-permute-start(bf16[64,3072]{1,0:T(8,128)(2,1)} %get-tuple-element.46), channel_id=1, source_target_pairs={{0,8},{8,0},{16,24},{24,16},{1,9},{9,1},{17,25},{25,17},{2,10},{10... | collective-permute-start | bytes 1179656 | tf_op jit(solution)/shard_map/ppermute | solution.py:208
  27.4 23.5 %collective-permute-start.12 = (bf16[64,3072]{1,0:T(8,128)(2,1)}, bf16[64,3072]{1,0:T(8,128)(2,1)S(1)}, u32[]{:S(2)}, u32[]{:S(2)}) collective-permute-start(bf16[64,3072]{1,0:T(8,128)(2,1)} %get-tuple-element.48), channel_id=1, source_target_pairs={{0,24},{8,16},{16,8},{24,0},{1,25},{9,17},{17,9},{25,1},{2,26},{10... | collective-permute-start | bytes 1179656 | tf_op jit(solution)/shard_map/ppermute | solution.py:208
  33.0 12.6 %copy-start.2 = (bf16[64,3072]{1,0:T(8,128)(2,1)}, bf16[64,3072]{1,0:T(8,128)(2,1)S(1)}, u32[]{:S(2)}) copy-start(bf16[64,3072]{1,0:T(8,128)(2,1)S(1)} %collective-permute-done.6.refs_3_) | copy-start | bytes 1179652
  33.0 9.9 %collective-permute-start.7 = (bf16[64,3072]{1,0:T(8,128)(2,1)S(1)}, bf16[64,3072]{1,0:T(8,128)(2,1)S(1)}, u32[]{:S(2)}, u32[]{:S(2)}) collective-permute-start(bf16[64,3072]{1,0:T(8,128)(2,1)S(1)} %broadcast_select_fusion.3), channel_id=1, source_target_pairs={{0,224},{8,40},{32,0},{40,72},{64,32},{72,104},{96,64},{104,136},{... | collective-permute-start | bytes 1179656 | tf_op jit(solution)/shard_map/ppermute | solution.py:227
  33.1 12.6 %collective-permute-start.8 = (bf16[64,3072]{1,0:T(8,128)(2,1)S(1)}, bf16[64,3072]{1,0:T(8,128)(2,1)S(1)}, u32[]{:S(2)}, u32[]{:S(2)}) collective-permute-start(bf16[64,3072]{1,0:T(8,128)(2,1)S(1)} %broadcast_select_fusion.2), channel_id=1, source_target_pairs={{0,32},{8,232},{32,64},{40,8},{64,96},{72,40},{96,128},{104,72},{1... | collective-permute-start | bytes 1179656 | tf_op jit(solution)/shard_map/ppermute | solution.py:228
  46.6 4.3 %copy-start = (bf16[64,3072]{1,0:T(8,128)(2,1)S(1)}, bf16[64,3072]{1,0:T(8,128)(2,1)}, u32[]{:S(2)}) copy-start(bf16[64,3072]{1,0:T(8,128)(2,1)} %get-tuple-element.36.refs_0_) | copy-start | bytes 1179652
  46.7 9.3 %collective-permute-start.9 = (bf16[1,128,512]{2,1,0:T(8,128)(2,1)S(1)}, bf16[1,128,512]{2,1,0:T(8,128)(2,1)S(1)}, u32[]{:S(2)}, u32[]{:S(2)}) collective-permute-start(bf16[1,128,512]{2,1,0:T(8,128)(2,1)S(1)} %pair_products.4), channel_id=1, source_target_pairs={{0,32},{32,64},{64,96},{96,128},{128,160},{160,192},{192,224},{224... | collective-permute-start | bytes 393224 | tf_op jit(solution)/shard_map/ppermute | solution.py:231
  46.7 1.0 %copy-start.3 = (bf16[64,3072]{1,0:T(8,128)(2,1)S(1)}, bf16[64,3072]{1,0:T(8,128)(2,1)}, u32[]{:S(2)}) copy-start(bf16[64,3072]{1,0:T(8,128)(2,1)} %copy-done.2) | copy-start | bytes 1179652
  52.5 12.5 %collective-permute-start.14 = (bf16[64,3072]{1,0:T(8,128)(2,1)}, bf16[64,3072]{1,0:T(8,128)(2,1)S(1)}, u32[]{:S(2)}, u32[]{:S(2)}) collective-permute-start(bf16[64,3072]{1,0:T(8,128)(2,1)} %broadcast_select_fusion), channel_id=1, source_target_pairs={{0,32},{8,232},{32,64},{40,8},{64,96},{72,40},{96,128},{104,72},{1... | collective-permute-start | bytes 1179656 | tf_op jit(solution)/shard_map/ppermute | solution.py:228
  55.9 10.6 %collective-permute-start.13 = (bf16[64,3072]{1,0:T(8,128)(2,1)}, bf16[64,3072]{1,0:T(8,128)(2,1)S(1)}, u32[]{:S(2)}, u32[]{:S(2)}) collective-permute-start(bf16[64,3072]{1,0:T(8,128)(2,1)} %broadcast_select_fusion.1), channel_id=1, source_target_pairs={{0,224},{8,40},{32,0},{40,72},{64,32},{72,104},{96,64},{104,136},{... | collective-permute-start | bytes 1179656 | tf_op jit(solution)/shard_map/ppermute | solution.py:227
  56.8 20.2 %all-to-all-start = ((bf16[32,16,512]{2,1,0:T(8,128)(2,1)}), bf16[32,16,512]{2,1,0:T(8,128)(2,1)S(1)}, u32[]{:S(2)}, u32[]{:S(2)}) async-start(bf16[32,16,512]{2,1,0:T(8,128)(2,1)} %bitcast.12), calls=%async_computation | async-start | bytes 1048576 | tf_op jit(solution)/shard_map/all_to_all | solution.py:240
  67.5 6.7 %collective-permute-start.15 = (bf16[1,128,512]{2,1,0:T(8,128)(2,1)S(1)}, bf16[1,128,512]{2,1,0:T(8,128)(2,1)S(1)}, u32[]{:S(2)}, u32[]{:S(2)}) collective-permute-start(bf16[1,128,512]{2,1,0:T(8,128)(2,1)S(1)} %pair_products.6), channel_id=1, source_target_pairs={{0,32},{32,64},{64,96},{96,128},{128,160},{160,192},{192,224},{224... | collective-permute-start | bytes 393224 | tf_op jit(solution)/shard_map/ppermute | solution.py:231
  70.6 22.9 %copy-start.4 = (bf16[4096,128]{1,0:T(8,128)(2,1)S(1)}, bf16[4096,128]{1,0:T(8,128)(2,1)}, u32[]{:S(2)}) copy-start(bf16[4096,128]{1,0:T(8,128)(2,1)} %constant.36.clone.table_ref) | copy-start | bytes 3145732
  70.6 22.9 %copy-start.5 = (f32[19,2048]{1,0:T(8,128)S(1)}, f32[19,2048]{1,0:T(8,128)}, u32[]{:S(2)}) copy-start(f32[19,2048]{1,0:T(8,128)} %constant.35.clone.sin_ref) | copy-start | bytes 466948
  70.6 22.9 %copy-start.6 = (f32[19,2048]{1,0:T(8,128)S(1)}, f32[19,2048]{1,0:T(8,128)}, u32[]{:S(2)}) copy-start(f32[19,2048]{1,0:T(8,128)} %constant.34.clone.cos_ref) | copy-start | bytes 466948
